TPU v7x, 32 devices: a whole 2x2x4 slice. The times are simulated.
32 devices in a mesh: parts: 2 (over x), space: 8 (over z, y), member: 2 (over core).
Axes of the slice: x: 2, y: 2, z: 4, core: 2. Of those that a mesh axis runs over, the one named last changes fastest.
Arguments:
- densities: float32 [4096, 4, 4096], P('space', ('parts', 'member')), parts along dimension 1, may hold values from 0.05 to 40, as said below
- scaling: float32 [4096, 4, 4096], P('space', ('parts', 'member')), parts along dimension 1, may hold values from 0.25 to 4
- weights: float32 [4], P('parts'), parts along dimension 0, may hold values from 0.5 to 2
- band: float32 [32, 3, 128, 128], replicated, may hold values from 0 to 0.009375, as said below
Outputs:
- barycenter: float32 [8192, 4096], P(('parts', 'space')), parts along dimension 0
- new_scaling: float32 [4096, 4, 4096], P('space', ('parts', 'member')), parts along dimension 1
There are 2 independent parts, one for each index of `parts`. A program takes and returns all parts, laid end to end along the dimension named above; an argument that names none is the same for every part. Nothing has to cross between parts.
Inputs may be any that keep to these rules, and one draw needn't show every extreme that they name: Positive densities. `band`: positive entries.
All inputs are finite; a program needn't handle non-finite values.
Results may differ from a plain program's by a relative error of at most 0.0001.
Values sent between devices are 32-bit elements; how exact they have to be, the bound alone decides.
No kernel may reach another device: no remote copies, remote signals or barrier semaphores. Data moves between devices by JAX's collectives and lax.ppermute only.
A program may use at most 192 MiB of HBM per device.

v0:
```python
import jax
import jax.numpy as jnp
from jax import lax
from jax.sharding import PartitionSpec as P


def with_halo(block, sides, width):
    for axis, dim in sides:
        count = lax.axis_size(axis)
        forward = [(i, i + 1) for i in range(count - 1)]
        backward = [(target, source) for source, target in forward]
        low = lax.ppermute(
            lax.slice_in_dim(block, block.shape[dim] - width, None, axis=dim), axis, forward
        )
        high = lax.ppermute(lax.slice_in_dim(block, 0, width, axis=dim), axis, backward)
        block = jnp.concatenate([low, block, high], axis=dim)
    return block


def row_pass(field, band):
    nblocks, _, width, _ = band.shape
    lead = field.shape[:-1]
    blocks = field.reshape(lead + (nblocks, width))
    padding = [(0, 0)] * len(lead) + [(1, 1), (0, 0)]
    padded = jnp.pad(blocks, padding)
    total = jnp.zeros(blocks.shape, jnp.float32)
    for offset in range(3):
        window = lax.slice_in_dim(padded, offset, offset + nblocks, axis=len(lead))
        total = total + jnp.einsum(
            "...bq,bpq->...bp", window, band[:, offset], precision=lax.Precision.HIGHEST
        )
    return total.reshape(field.shape)


def rim_col_pass(field, band):
    rows_here = field.shape[0]
    width = band.shape[2]
    nlocal = rows_here // width
    first = lax.axis_index("space") * nlocal
    padded = with_halo(field, (("space", 0),), width)
    blocks = padded.reshape(nlocal + 2, width, -1)
    local_band = lax.dynamic_slice_in_dim(band, first, nlocal, 0)
    total = jnp.zeros((nlocal, width, blocks.shape[2]), jnp.float32)
    for offset in range(3):
        total = total + jnp.einsum(
            "bpq,bqc->bpc",
            local_band[:, offset],
            blocks[offset : offset + nlocal],
            precision=lax.Precision.HIGHEST,
        )
    return total.reshape(field.shape)


def local(densities, scaling, weights, band):
    rows_here, maps_here, cols_all = densities.shape
    shares = weights / jnp.sum(weights)
    local_shares = lax.dynamic_slice_in_dim(shares, lax.axis_index("member") * maps_here, maps_here)
    blurred = rim_col_pass(row_pass(scaling, band), band)
    ratio = densities / blurred
    smeared = rim_col_pass(row_pass(ratio, band), band)
    terms = jnp.sum(local_shares[None, :, None] * jnp.log(scaling * smeared), axis=1)
    logmean = lax.psum(terms, "member")
    raw = jnp.exp(logmean)
    mass = lax.psum(jnp.sum(raw), "space")
    barycenter = raw * (float(cols_all * cols_all) / mass)
    new_scaling = barycenter[:, None, :] / smeared
    return (barycenter, new_scaling)


def solution(mesh):
    return jax.shard_map(
        local,
        mesh=mesh,
        in_specs=(
            P("space", ("parts", "member"), None),
            P("space", ("parts", "member"), None),
            P("parts"),
            P(),
        ),
        out_specs=(P(("parts", "space"), None), P("space", ("parts", "member"), None)),
        check_vma=False,
    )
```

profile of v0, /device:TPU:0, one launch (start us, length us, event | category | flops | bytes accessed | tf_op | source)
XLA Modules:
  0.0 551.9 jit_solution(11775048219406270152)
XLA Ops:
  15.6 12.9 %fusion.1 = f32[32,512,128]{1,2,0:T(8,128)} fusion(f32[512,1,32,128]{3,0,2,1:T(8,128)S(1)} %copy.22, f32[32,3,128,128]{3,2,1,0:T(8,128)} %param.7), kind=kOutput, calls=%fused_computation.5 | convolution fusion | flops 3221225472 | bytes 18874368 | tf_op jit(solution)/shard_map/...bq,bpq->...bp/dot_general | solution.py:29
  28.6 17.9 %fusion.18 = f32[32,128,512]{2,1,0:T(8,128)} fusion(f32[512,32,128]{2,1,0:T(8,128)S(1)} %bitcast.120, f32[32,3,128,128]{3,2,1,0:T(8,128)} %param.7), kind=kOutput, calls=%fused_computation.26 | convolution fusion | flops 3221225472 | bytes 18874368 | tf_op jit(solution)/shard_map/...bq,bpq->...bp/dot_general | solution.py:29
  46.5 15.9 %bitcast_add_fusion = f32[32,128,512]{2,1,0:T(8,128)S(1)} fusion(f32[32,128,512]{2,1,0:T(8,128)} %fusion.18, f32[32,512,128]{1,2,0:T(8,128)} %fusion.1, f32[512,1,32,128]{3,0,2,1:T(8,128)} %copy-done.5, f32[32,3,128,128]{3,2,1,0:T(8,128)} %param.7), kind=kOutput, calls=%fused_computation.20 | convolution fusion | flops 3225419776 | bytes 35651584 | tf_op jit(solution)/shard_map/...bq,bpq->...bp/dot_general | solution.py:29
  74.6 9.9 %slice.109 = f32[4,128,4096]{1,0,2:T(4,128)} reshape(f32[512,1,32,128]{0,3,2,1:T(8,128)} %bitcast.110) | data formatting | bytes 16777216 | tf_op jit(solution)/shard_map/slice | solution.py:48
  84.5 19.0 %copy.30 = f32[512,1,4096]{0,2,1:T(8,128)} copy(f32[512,1,4096]{2,1,0:T(1,128)} %param.4) | data formatting | bytes 16777216 | tf_op args[0]
  103.5 12.8 %fusion.16 = f32[4,128,4096]{2,1,0:T(8,128)} fusion(f32[4,128,4096]{1,0,2:T(4,128)} %slice.109, f32[32,3,128,128]{3,2,1,0:T(8,128)} %param.7, s32[]{:T(128)S(6)} %select_n.8, s32[]{:T(128)S(6)} %add.74), kind=kOutput, calls=%fused_computation.24 | convolution fusion | flops 3221225472 | bytes 17039368 | tf_op jit(solution)/shard_map/bpq,bqc->bpc/dot_general | solution.py:45
  116.3 47.0 %collective-permute-done = f32[128,1,4096]{0,2,1:T(8,128)S(1)} collective-permute-done((f32[128,1,4096]{0,2,1:T(8,128)}, f32[128,1,4096]{0,2,1:T(8,128)S(1)}, u32[]{:S(2)}, u32[]{:S(2)}) %collective-permute-start) | collective-permute-done | bytes 2097184 | tf_op jit(solution)/shard_map/ppermute | solution.py:12
  163.3 9.9 %pad_maximum_fusion.2 = (f32[512,1,4096]{0,2,1:T(8,128)}, f32[512,1,4096]{0,2,1:T(8,128)}) fusion(f32[128,1,4096]{0,2,1:T(8,128)} %collective-permute-done.1, f32[512,1,4096]{0,2,1:T(8,128)} %bitcast.111, f32[128,1,4096]{0,2,1:T(8,128)S(1)} %collective-permute-done), kind=kLoop, calls=%fused_computation.14 | loop fusion | flops 4194304 | bytes 29360128 | tf_op jit(solution)/shard_map/concatenate | solution.py:16
  182.1 11.7 %fusion.38 = f32[4,128,4096]{2,1,0:T(8,128)} fusion(f32[4,128,4096]{2,1,0:T(8,128)} %bitcast.121, f32[32,3,128,128]{3,2,1,0:T(8,128)} %param.7, s32[]{:T(128)S(6)} %select_n.8), kind=kOutput, calls=%fused_computation.50 | convolution fusion | flops 3221225472 | bytes 17039364 | tf_op jit(solution)/shard_map/bpq,bqc->bpc/dot_general | solution.py:45
  202.8 15.0 %add_add_fusion.2 = f32[4,128,4096]{2,1,0:T(8,128)} fusion(f32[4,128,4096]{2,1,0:T(8,128)} %fusion.38, f32[4,128,4096]{2,1,0:T(8,128)} %fusion.16, f32[4,128,4096]{2,1,0:T(8,128)} %bitcast.124, f32[32,3,128,128]{3,2,1,0:T(8,128)} %param.7, s32[]{:T(128)S(6)} %select_n.8, s32[]{:T(128)S(6)} %add.75), kind=kOutput, calls=%fused_computation.30 | convolution fusion | flops 3225419776 | bytes 33816584 | tf_op jit(solution)/shard_map/bpq,bqc->bpc/dot_general | solution.py:45
  226.7 11.3 %div.20 = f32[512,1,4096]{0,2,1:T(8,128)} divide(f32[512,1,4096]{0,2,1:T(8,128)} %copy.30, f32[512,1,4096]{0,2,1:T(8,128)} %copy.31) | non-fusion elementwise | flops 2097152 | bytes 25165824 | tf_op jit(solution)/shard_map/div | solution.py:59
  246.9 12.8 %fusion.7 = f32[32,512,128]{1,2,0:T(8,128)} fusion(f32[512,1,32,128]{3,0,2,1:T(8,128)} %copy.32, f32[32,3,128,128]{3,2,1,0:T(8,128)} %param.7), kind=kOutput, calls=%fused_computation.9 | convolution fusion | flops 3221225472 | bytes 18874368 | tf_op jit(solution)/shard_map/...bq,bpq->...bp/dot_general | solution.py:29
  259.7 11.2 %fusion.26 = f32[32,512,128]{1,2,0:T(8,128)} fusion(f32[512,32,128]{0,2,1:T(8,128)S(1)} %bitcast.116, f32[32,3,128,128]{3,2,1,0:T(8,128)} %param.7), kind=kOutput, calls=%fused_computation.35 | convolution fusion | flops 3221225472 | bytes 18874368 | tf_op jit(solution)/shard_map/...bq,bpq->...bp/dot_general | solution.py:29
  270.9 15.4 %add_add_fusion.1 = f32[32,512,128]{1,2,0:T(8,128)S(1)} fusion(f32[32,512,128]{1,2,0:T(8,128)} %fusion.7, f32[32,512,128]{1,2,0:T(8,128)} %fusion.26, f32[512,1,32,128]{3,0,2,1:T(8,128)} %copy.32, f32[32,3,128,128]{3,2,1,0:T(8,128)} %param.7), kind=kOutput, calls=%fused_computation.29 | convolution fusion | flops 3225419776 | bytes 35651584 | tf_op jit(solution)/shard_map/...bq,bpq->...bp/dot_general | solution.py:29
  299.8 10.3 %slice.121 = f32[4,128,4096]{1,0,2:T(4,128)} reshape(f32[512,1,32,128]{0,3,2,1:T(8,128)} %bitcast.113) | data formatting | bytes 16777216 | tf_op jit(solution)/shard_map/slice | solution.py:48
  310.1 12.9 %fusion.14 = f32[4,128,4096]{2,1,0:T(8,128)} fusion(f32[4,128,4096]{1,0,2:T(4,128)} %slice.121, f32[32,3,128,128]{3,2,1,0:T(8,128)} %param.7, s32[]{:T(128)S(6)} %select_n.8, s32[]{:T(128)S(6)} %add.74), kind=kOutput, calls=%fused_computation.22 | convolution fusion | flops 3221225472 | bytes 17039368 | tf_op jit(solution)/shard_map/bpq,bqc->bpc/dot_general | solution.py:45
  323.0 62.7 %collective-permute-done.2 = f32[128,1,4096]{0,2,1:T(8,128)S(1)} collective-permute-done((f32[128,1,4096]{0,2,1:T(8,128)}, f32[128,1,4096]{0,2,1:T(8,128)S(1)}, u32[]{:S(2)}, u32[]{:S(2)}) %collective-permute-start.2) | collective-permute-done | bytes 2097184 | tf_op jit(solution)/shard_map/ppermute | solution.py:12
  402.7 11.8 %fusion.37 = f32[4,128,4096]{2,1,0:T(8,128)} fusion(f32[4,128,4096]{2,1,0:T(8,128)} %bitcast.122, f32[32,3,128,128]{3,2,1,0:T(8,128)} %param.7, s32[]{:T(128)S(6)} %select_n.8), kind=kOutput, calls=%fused_computation.49 | convolution fusion | flops 3221225472 | bytes 17039364 | tf_op jit(solution)/shard_map/bpq,bqc->bpc/dot_general | solution.py:45
  423.5 13.8 %add_add_fusion = f32[4,128,4096]{2,1,0:T(8,128)S(1)} fusion(f32[4,128,4096]{2,1,0:T(8,128)} %fusion.37, f32[4,128,4096]{2,1,0:T(8,128)} %fusion.14, f32[4,128,4096]{2,1,0:T(8,128)} %bitcast.123, f32[32,3,128,128]{3,2,1,0:T(8,128)} %param.7, s32[]{:T(128)S(6)} %select_n.8, s32[]{:T(128)S(6)} %add.75), kind=kOutput, calls=%fused_computation.28 | convolution fusion | flops 3225419776 | bytes 33816584 | tf_op jit(solution)/shard_map/bpq,bqc->bpc/dot_general | solution.py:45
  437.3 15.9 %fusion.13 = f32[512,1,4096]{2,0,1:T(8,128)} fusion(f32[4,128,4096]{2,1,0:T(8,128)S(1)} %add_add_fusion, f32[512,1,4096]{2,1,0:T(1,128)} %param.5, f32[]{:T(128)} %bitcast), kind=kLoop, calls=%fused_computation.19 | loop fusion | flops 4194304 | bytes 25165828 | tf_op jit(solution)/shard_map/mul | solution.py:61
  453.2 43.2 %all-reduce.4.cloned.1.call-done = f32[512,4096]{1,0:T(8,128)} async-done(((f32[512,4096]{1,0:T(8,128)}), f32[512,4096]{1,0:T(8,128)}) %all-reduce.4.cloned.1.call-update) | async-done | bytes 8388624 | tf_op jit(solution)/shard_map/psum | solution.py:62
  502.6 22.3 %psum.15 = f32[]{:T(128)} all-reduce(f32[]{:T(128)} %exponential_reduce_fusion), channel_id=1, replica_groups=mesh['parts'=2,'space'=8,'member'=2] {'space'}, use_global_device_ids=true, to_apply=%region_3.4 | all-reduce | flops 1 | bytes 8 | tf_op jit(solution)/shard_map/psum | solution.py:64
  525.5 9.3 %bitcast_divide_fusion = (f32[512,4096]{1,0:T(8,128)S(1)}, f32[512,4096]{1,0:T(8,128)}) fusion(f32[4,128,4096]{2,1,0:T(8,128)} %copy-done.3, f32[]{:T(128)S(6)} %div.21, f32[512,4096]{1,0:T(8,128)} %all-reduce.4.cloned.1.call-done), kind=kLoop, calls=%fused_computation.16 | loop fusion | flops 4194304 | bytes 33554436 | tf_op jit(solution)/shard_map/div | solution.py:66
  534.8 10.0 %div.23 = f32[512,1,4096]{2,1,0:T(1,128)} reshape(f32[512,4096]{1,0:T(8,128)S(1)} %get-tuple-element.2) | data formatting | bytes 16777216 | tf_op jit(solution)/shard_map/div | solution.py:66
  (41 shorter events, 101.9 us)
Async XLA Ops:
  7.2 489.3 %all-reduce.4.cloned.1.call-start = ((), (), s32[]{:S(2)}) async-start(), calls=%async_computation | async-start | bytes 16777216 | tf_op jit(solution)/shard_map/psum | solution.py:62
  7.2 21.4 %slice-start = ((s8[8388608]{0:T(1024)(128)(4,1)}), s8[4194304]{0:T(1024)(128)(4,1)S(1)}, s32[]{:S(2)}) async-start(s8[8388608]{0:T(1024)(128)(4,1)} %bitcast.118), calls=%async_computation.1 | async-start | bytes 8388608
  15.6 12.9 %copy-start.5 = (f32[512,1,32,128]{3,0,2,1:T(8,128)}, f32[512,1,32,128]{3,0,2,1:T(8,128)S(1)}, u32[]{:S(2)}) copy-start(f32[512,1,32,128]{3,0,2,1:T(8,128)S(1)} %copy.22) | copy-start | bytes 25165828
  15.6 12.9 %slice-start.1 = ((s8[8388608]{0:T(1024)(128)(4,1)}), s8[4194304]{0:T(1024)(128)(4,1)S(1)}, s32[]{:S(2)}) async-start(s8[8388608]{0:T(1024)(128)(4,1)} %bitcast.118), calls=%async_computation.2 | async-start | bytes 8388608
  62.4 3.4 copy-start
  68.3 95.0 %collective-permute-start = (f32[128,1,4096]{0,2,1:T(8,128)}, f32[128,1,4096]{0,2,1:T(8,128)S(1)}, u32[]{:S(2)}, u32[]{:S(2)}) collective-permute-start(f32[128,1,4096]{0,2,1:T(8,128)} %bitcast.13), channel_id=1, source_target_pairs={{0,2},{2,4},{4,6},{6,8},{8,10},{10,12},{12,14},{1,3},{3,5},{5,7},{... | collective-permute-start | bytes 6291464 | tf_op jit(solution)/shard_map/ppermute | solution.py:12
  73.3 90.0 %collective-permute-start.1 = (f32[128,1,4096]{0,2,1:T(8,128)}, f32[128,1,4096]{0,2,1:T(8,128)}, u32[]{:S(2)}, u32[]{:S(2)}) collective-permute-start(f32[128,1,4096]{0,2,1:T(8,128)} %bitcast.20), channel_id=1, source_target_pairs={{2,0},{4,2},{6,4},{8,6},{10,8},{12,10},{14,12},{3,1},{5,3},{7,5},{... | collective-permute-start | bytes 6291464 | tf_op jit(solution)/shard_map/ppermute | solution.py:15
  246.9 12.8 %copy-start.4 = (f32[512,1,4096]{0,2,1:T(8,128)S(1)}, f32[512,1,4096]{0,2,1:T(8,128)}, u32[]{:S(2)}) copy-start(f32[512,1,4096]{0,2,1:T(8,128)} %div.20) | copy-start | bytes 25165828
  286.3 3.4 copy-start.1
  286.3 11.6 %copy-start.6 = (f32[2]{0:T(128)S(1)}, f32[2]{0:T(128)}, u32[]{:S(2)}) copy-start(f32[2]{0:T(128)} %param.6) | copy-start | bytes 28
  292.2 93.5 %collective-permute-start.2 = (f32[128,1,4096]{0,2,1:T(8,128)}, f32[128,1,4096]{0,2,1:T(8,128)S(1)}, u32[]{:S(2)}, u32[]{:S(2)}) collective-permute-start(f32[128,1,4096]{0,2,1:T(8,128)} %bitcast.30), channel_id=1, source_target_pairs={{0,2},{2,4},{4,6},{6,8},{8,10},{10,12},{12,14},{1,3},{3,5},{5,7},{... | collective-permute-start | bytes 6291464 | tf_op jit(solution)/shard_map/ppermute | solution.py:12
  296.6 89.1 %collective-permute-start.3 = (f32[128,1,4096]{0,2,1:T(8,128)}, f32[128,1,4096]{0,2,1:T(8,128)}, u32[]{:S(2)}, u32[]{:S(2)}) collective-permute-start(f32[128,1,4096]{0,2,1:T(8,128)} %bitcast.36), channel_id=1, source_target_pairs={{2,0},{4,2},{6,4},{8,6},{10,8},{12,10},{14,12},{3,1},{5,3},{7,5},{... | collective-permute-start | bytes 6291464 | tf_op jit(solution)/shard_map/ppermute | solution.py:15
  310.1 75.7 %copy-start.2 = (f32[32,512,128]{1,2,0:T(8,128)S(1)}, f32[32,512,128]{1,2,0:T(8,128)}, u32[]{:S(2)}) copy-start(f32[32,512,128]{1,2,0:T(8,128)} %copy-done.1) | copy-start | bytes 25165828
  437.3 15.9 %copy-start.3 = (f32[4,128,4096]{2,1,0:T(8,128)}, f32[4,128,4096]{2,1,0:T(8,128)S(1)}, u32[]{:S(2)}) copy-start(f32[4,128,4096]{2,1,0:T(8,128)S(1)} %add_add_fusion) | copy-start | bytes 25165828
Sparse Core Ops, SparseCore 0:
  453.3 43.0 all-reduce.3
where the time goes:
time: 559 us; the launch traced here: 552 us
  matrix products  164 us (29%)
  waiting for transfers between devices  153 us (27%)
  local copies, waits for them, and re-layouts  124 us (22%)
  other arithmetic  61.9 us (11%)
  blocking collectives  22.3 us (4%)
  between operations  15.1 us (3%)
  starting transfers between devices  12 us (2%)
    ppermute x2, waiting for transfers between devices, with_halo(): lax.ppermute(lax.slice_in_dim(block, block.shape[dim] - width, None, axis...  110 us
    dot_general x6, matrix products, row_pass(): jnp.einsum('...bq,bpq->...bp', window, band[:, offset], precision=lax.Pre...  86.1 us
    dot_general x6, matrix products, rim_col_pass(): jnp.einsum('bpq,bqc->bpc', local_band[:, offset], blocks[offset:offset +...  78 us
    slice x6, local copies, waits for them, and re-layouts, rim_col_pass(): blocks[offset:offset + nlocal]  55.8 us
    psum x1, waiting for transfers between devices, local(): logmean = lax.psum(terms, 'member')  43.2 us
    unnamed x19, local copies, waits for them, and re-layouts  25.8 us
    psum x1, blocking collectives, local(): mass = lax.psum(jnp.sum(raw), 'space')  22.3 us
    concatenate x2, other arithmetic, with_halo(): block = jnp.concatenate([low, block, high], axis=dim)  18 us
  transfers between devices with their start and end apart: 5, of which 3 were waited for; matrix products, arithmetic and copies ran while one was open for 12% of the time, Pallas kernels for 0%

commit v1 on v0

v1 whole, which is shorter than its diff:
```python
import functools

import jax
import jax.numpy as jnp
from jax import lax
from jax.experimental import pallas as pl
from jax.experimental.pallas import tpu as pltpu
from jax.sharding import PartitionSpec as P

F32 = jnp.float32
BF16 = jnp.bfloat16
VMEM_LIMIT = 56 * 1024 * 1024
ANY = pl.BlockSpec(memory_space=pl.ANY)
INVMEM = pl.BlockSpec(memory_space=pltpu.VMEM)
INSMEM = pl.BlockSpec(memory_space=pltpu.SMEM)


def split(x):
    high = x.astype(BF16)
    return high, (x - high.astype(F32)).astype(BF16)


def dot3(a, b, dims):
    one = functools.partial(lax.dot_general, dimension_numbers=(dims, ((), ())), preferred_element_type=F32)
    return one(a[0], b[0]) + (one(a[0], b[1]) + one(a[1], b[0]))


def params():
    return pltpu.CompilerParams(vmem_limit_bytes=VMEM_LIMIT)


def weight_kernel(nblocks, band_ref, high_ref, low_ref):
    pair = pl.program_id(0)
    width = band_ref.shape[2]
    zero = jnp.zeros((width, width), F32)
    for o in range(2):
        for i in range(4):
            j = i - o
            value = band_ref[o, j] if 0 <= j <= 2 else zero
            if (o, j) == (0, 0):
                value = jnp.where(pair > 0, value, 0.0)
            if (o, j) == (1, 2):
                value = jnp.where(pair < nblocks // 2 - 1, value, 0.0)
            high, low = split(value)
            rows, columns = slice(o * width, (o + 1) * width), slice(i * width, (i + 1) * width)
            high_ref[0, rows, columns] = high
            low_ref[0, rows, columns] = low


def row_weights(band):
    nblocks, _, width, _ = band.shape
    shape = jax.ShapeDtypeStruct((nblocks // 2, 2 * width, 4 * width), BF16)
    out_spec = pl.BlockSpec((1, 2 * width, 4 * width), lambda t: (t, 0, 0))
    return pl.pallas_call(
        functools.partial(weight_kernel, nblocks),
        grid=(nblocks // 2,),
        in_specs=[pl.BlockSpec((2, 3, width, width), lambda t: (t, 0, 0, 0))],
        out_specs=(out_spec, out_spec),
        out_shape=(shape, shape),
        name="row_weights",
    )(band)


def blur_kernel(plan, *refs):
    pieces, narrays, groups, extra, first, last, nblocks, width, final = plan
    arrays = refs[:narrays]
    a_ref, high_ref, low_ref, extra_ref = refs[narrays : narrays + 4]
    rest = refs[narrays + 4 :]
    if final:
        share_ref, rest = rest[0], rest[1:]
    nouts = 2 if final else len(groups)
    outs = rest[:nouts]
    field, yhigh, ylow, whigh, wlow, other, sems = rest[nouts:]

    copies = []
    for k, (which, row, block, rows, blocks, to_row, to_block) in enumerate(pieces):
        copies.append(
            pltpu.make_async_copy(
                arrays[which].at[pl.ds(row, rows), pl.ds(block * width, blocks * width)],
                field.at[pl.ds(to_row, rows), pl.ds(to_block * width, blocks * width)],
                sems.at[k],
            )
        )
    count = len(pieces)
    late = []
    pairs = (last - first) // 2
    for src, dst in ((high_ref, whigh), (low_ref, wlow)):
        late.append(pltpu.make_async_copy(src.at[pl.ds(first // 2, pairs)], dst, sems.at[count]))
        count += 1
    at = 0
    for row, rows in extra:
        late.append(
            pltpu.make_async_copy(
                extra_ref.at[pl.ds(row, rows), pl.ds(first * width, (last - first) * width)],
                other.at[pl.ds(at, rows)],
                sems.at[count],
            )
        )
        count += 1
        at += rows
    for copy in copies + late:
        copy.start()
    if first == 0:
        field[:, :width] = jnp.zeros((field.shape[0], width), F32)
    if last == nblocks:
        field[:, field.shape[1] - width :] = jnp.zeros((field.shape[0], width), F32)
    bands = [split(a_ref[to : to + m, :k]) for _, k, to, m in groups]
    for copy in copies:
        copy.wait()

    def columns_pass(i, carry):
        at = pl.ds(pl.multiple_of(i * 2 * width, 2 * width), 2 * width)
        for (row, k, to, m), a in zip(groups, bands):
            y = dot3(a, split(field[row : row + k, at]), ((1,), (0,)))
            high, low = split(y)
            yhigh[to : to + m, at] = high
            ylow[to : to + m, at] = low
        return carry

    lax.fori_loop(0, pairs + 1, columns_pass, 0)
    for copy in late:
        copy.wait()

    def rows_pass(t, carry):
        source = pl.ds(pl.multiple_of(t * 2 * width, 2 * width), 4 * width)
        at = pl.ds(pl.multiple_of(t * 2 * width, 2 * width), 2 * width)
        value = dot3((yhigh[:, source], ylow[:, source]), (whigh[t], wlow[t]), ((1,), (1,)))
        if final:
            outs[0][:, at] = share_ref[0] * jnp.log(other[:, at] * value)
            outs[1][:, at] = value
        else:
            ratio = other[:, at] / value
            for out, (_, _, to, m) in zip(outs, groups):
                out[:, at] = ratio[to : to + m]
        return carry

    lax.fori_loop(0, pairs, rows_pass, 0)


def blur(name, arrays, pieces, groups, extra, first, last, a, weights, other, share=None):
    width = weights[0].shape[1] // 2
    nblocks = weights[0].shape[0] * 2
    total = sum(m for _, _, _, m in groups)
    depth = max(row + k for row, k, _, _ in groups)
    columns = (last - first) * width
    final = share is not None
    plan = (pieces, len(arrays), groups, extra, first, last, nblocks, width, final)
    if final:
        shapes = [jax.ShapeDtypeStruct((total, columns), F32)] * 2
    else:
        shapes = [jax.ShapeDtypeStruct((m, columns), F32) for _, _, _, m in groups]
    pairs = (last - first) // 2
    work = 3 * 2 * total * columns * (depth + 4 * width)
    moved = 4 * (depth + 3 * total) * columns + pairs * 2 * 2 * 8 * width * width
    return pl.pallas_call(
        functools.partial(blur_kernel, plan),
        in_specs=[ANY] * len(arrays) + [INVMEM, ANY, ANY, ANY] + [INSMEM] * final,
        out_specs=[INVMEM] * len(shapes),
        out_shape=shapes,
        scratch_shapes=[
            pltpu.VMEM((depth, columns + 2 * width), F32),
            pltpu.VMEM((total, columns + 2 * width), BF16),
            pltpu.VMEM((total, columns + 2 * width), BF16),
            pltpu.VMEM((pairs, 2 * width, 4 * width), BF16),
            pltpu.VMEM((pairs, 2 * width, 4 * width), BF16),
            pltpu.VMEM((total, columns), F32),
            pltpu.SemaphoreType.DMA((len(pieces) + 2 + len(extra),)),
        ],
        compiler_params=params(),
        cost_estimate=pl.CostEstimate(flops=work, bytes_accessed=moved, transcendentals=0),
        name=name,
    )(*arrays, a, *weights, other, *([share] if final else []))


def raw_kernel(plan, t_ref, peer_ref, m_ref, *refs):
    extra, column, fresh = plan
    if fresh:
        raw_all, quotient_all, mass_ref, raw, quotient, sems = refs
    else:
        _, _, before_ref, raw_all, quotient_all, mass_ref, raw, quotient, sems = refs
    raw[...] = jnp.exp(t_ref[...] + peer_ref[...])
    quotient[...] = raw[...] / m_ref[...]
    copies = []
    at = 0
    for row, rows in extra:
        for src, dst in ((raw, raw_all), (quotient, quotient_all)):
            copies.append(
                pltpu.make_async_copy(
                    src.at[pl.ds(at, rows)],
                    dst.at[pl.ds(row, rows), pl.ds(column, raw.shape[1])],
                    sems.at[len(copies)],
                )
            )
        at += rows
    for copy in copies:
        copy.start()
    mass = jnp.sum(raw[...])
    mass_ref[0] = mass if fresh else mass + before_ref[0]
    for copy in copies:
        copy.wait()


def raw_piece(name, t, peer, m, extra, column, whole, so_far):
    fresh = so_far is None
    shape = jax.ShapeDtypeStruct(whole, F32)
    return pl.pallas_call(
        functools.partial(raw_kernel, (extra, column, fresh)),
        in_specs=[INVMEM] * 3 + ([] if fresh else [ANY, ANY, INSMEM]),
        out_specs=(ANY, ANY, INSMEM),
        out_shape=(shape, shape, jax.ShapeDtypeStruct((1,), F32)),
        scratch_shapes=[
            pltpu.VMEM(t.shape, F32),
            pltpu.VMEM(t.shape, F32),
            pltpu.SemaphoreType.DMA((2 * len(extra),)),
        ],
        input_output_aliases={} if fresh else {3: 0, 4: 1},
        compiler_params=params(),
        cost_estimate=pl.CostEstimate(flops=4 * t.size, bytes_accessed=20 * t.size, transcendentals=2 * t.size),
        name=name,
    )(t, peer, m, *([] if fresh else so_far))


def output_kernel(raw_ref, quotient_ref, scale_ref, barycenter_ref, scaling_ref):
    scale = scale_ref[0]
    barycenter_ref[...] = raw_ref[...] * scale
    width = scaling_ref.shape[2]
    for b in range(scaling_ref.shape[1]):
        scaling_ref[:, b, :] = quotient_ref[:, b * width : (b + 1) * width] * scale


def outputs(raw, quotient, scale, width):
    rows, columns = raw.shape
    tile = 64
    flat = pl.BlockSpec((tile, columns), lambda i: (i, 0))
    return pl.pallas_call(
        output_kernel,
        grid=(rows // tile,),
        in_specs=[flat, flat, INSMEM],
        out_specs=(flat, pl.BlockSpec((tile, columns // width, width), lambda i: (i, 0, 0))),
        out_shape=(
            jax.ShapeDtypeStruct((rows, columns), F32),
            jax.ShapeDtypeStruct((rows, columns // width, width), F32),
        ),
        compiler_params=params(),
        name="outputs",
    )(raw, quotient, scale)


def local(densities, scaling, weights, band):
    rows_here, maps_here, cols_all = densities.shape
    nblocks, _, width, _ = band.shape
    nlocal = rows_here // width
    count = lax.axis_size("space")
    members = lax.axis_size("member")
    forward = [(i, i + 1) for i in range(count - 1)]
    backward = [(i + 1, i) for i in range(count - 1)]
    swap = [(0, 1), (1, 0)]
    assert maps_here == 1 and members == 2

    cuts1 = [0, nblocks // 2 + 2, nblocks]
    cuts2 = [0, nblocks // 2, nblocks]
    cuts3 = [0, nblocks // 2 - 2, nblocks]
    chunks = len(cuts1) - 1

    halo1 = []
    for c in range(chunks):
        start, stop = cuts1[c] * width, cuts1[c + 1] * width
        bottom = scaling[rows_here - width :, 0, start:stop]
        top = scaling[:width, 0, start:stop]
        halo1.append((lax.ppermute(bottom, "space", forward), lax.ppermute(top, "space", backward)))

    shares = weights / jnp.sum(weights)
    share = lax.dynamic_slice_in_dim(shares, lax.axis_index("member"), 1)
    own = scaling.reshape(rows_here, cols_all)
    dens = densities.reshape(rows_here, cols_all)
    wts = row_weights(band)
    mine = lax.dynamic_slice_in_dim(band, lax.axis_index("space") * nlocal, nlocal, 0)
    mine = mine.transpose(0, 2, 1, 3).reshape(nlocal, width, 3 * width)

    edges = sorted({0, nlocal - 1})
    inner = nlocal - 2
    a_edge = jnp.concatenate([mine[e] for e in edges], axis=0)
    edge_rows = tuple((e * width, width) for e in edges)
    edge_groups = tuple((g * 3 * width, 3 * width, g * width, width) for g in range(len(edges)))
    if inner > 0:
        a_inner = jnp.concatenate(
            [jnp.pad(mine[1 + i], ((0, 0), (i * width, (inner - 1 - i) * width))) for i in range(inner)], axis=0
        )
        inner_rows = ((width, inner * width),)
        inner_groups = ((0, nlocal * width, 0, inner * width),)

    def needs(blocks):
        return [(g * 3 * width + j * width, e - 1 + j) for g, e in enumerate(edges) for j in range(3)]

    def chunk_pieces(ids, to_row, cuts, first, last, row=0):
        found = []
        low, high = max(first - 1, 0), min(last + 1, nblocks)
        for c, which in enumerate(ids):
            a, b = max(low, cuts[c]), min(high, cuts[c + 1])
            if a < b:
                found.append((which, row, a - cuts[c], width, b - a, to_row, a - (first - 1)))
        return found

    if inner > 0:
        (ratio_inner,) = blur(
            "ratio_inner", [own], ((0, 0, 0, nlocal * width, nblocks, 0, 1),), inner_groups, inner_rows,
            0, nblocks, a_inner, wts, dens,
        )
    ratio_edges = []
    halo2 = []
    for c in range(chunks):
        first, last = cuts2[c], cuts2[c + 1]
        tops = [h[0] for h in halo1[: c + 1]]
        bottoms = [h[1] for h in halo1[: c + 1]]
        arrays = [own] + tops + bottoms
        pieces = []
        for to_row, b in needs(edges):
            if b < 0:
                pieces += chunk_pieces(range(1, c + 2), to_row, cuts1, first, last)
            elif b >= nlocal:
                pieces += chunk_pieces(range(c + 2, 2 * c + 3), to_row, cuts1, first, last)
            else:
                pieces += chunk_pieces([0], to_row, [0, nblocks], first, last, row=b * width)
        got = blur(
            f"ratio_edges_{c}", arrays, tuple(pieces), edge_groups, edge_rows, first, last, a_edge, wts, dens
        )
        ratio_edges.append(got)
        halo2.append((lax.ppermute(got[-1], "space", forward), lax.ppermute(got[0], "space", backward)))

    state = None
    whole = (rows_here, cols_all)
    if inner > 0:
        arrays = [ratio_inner] + [r[0] for r in ratio_edges] + [r[-1] for r in ratio_edges]
        pieces = [(0, 0, 0, inner * width, nblocks, width, 1)]
        pieces += chunk_pieces(range(1, chunks + 1), 0, cuts2, 0, nblocks)
        pieces += chunk_pieces(range(chunks + 1, 2 * chunks + 1), (nlocal - 1) * width, cuts2, 0, nblocks)
        t, m = blur(
            "logs_inner", arrays, tuple(pieces), inner_groups, inner_rows, 0, nblocks, a_inner, wts, own, share
        )
        state = raw_piece("raw_inner", t, lax.ppermute(t, "member", swap), m, inner_rows, 0, whole, state)
    for c in range(chunks):
        first, last = cuts3[c], cuts3[c + 1]
        arrays = [ratio_inner] if inner > 0 else []
        base = len(arrays)
        arrays += [h[0] for h in halo2[: c + 1]] + [h[1] for h in halo2[: c + 1]]
        arrays += [r[0] for r in ratio_edges[: c + 1]] + [r[-1] for r in ratio_edges[: c + 1]]
        ids = lambda part: range(base + part * (c + 1), base + (part + 1) * (c + 1))
        pieces = []
        for to_row, b in needs(edges):
            if b < 0:
                pieces += chunk_pieces(ids(0), to_row, cuts2, first, last)
            elif b >= nlocal:
                pieces += chunk_pieces(ids(1), to_row, cuts2, first, last)
            elif b == 0:
                pieces += chunk_pieces(ids(2), to_row, cuts2, first, last)
            elif b == nlocal - 1:
                pieces += chunk_pieces(ids(3), to_row, cuts2, first, last)
            else:
                pieces += chunk_pieces([0], to_row, [0, nblocks], first, last, row=(b - 1) * width)
        t, m = blur(
            f"logs_edges_{c}", arrays, tuple(pieces), edge_groups, edge_rows, first, last, a_edge, wts, own, share
        )
        state = raw_piece(
            f"raw_edges_{c}", t, lax.ppermute(t, "member", swap), m, edge_rows, first * width, whole, state
        )

    raw, quotient, mass = state
    mass = lax.psum(mass, "space")
    barycenter, new_scaling = outputs(raw, quotient, float(cols_all * cols_all) / mass, width)
    return barycenter, new_scaling.reshape(rows_here, 1, cols_all)


def solution(mesh):
    return jax.shard_map(
        local,
        mesh=mesh,
        in_specs=(
            P("space", ("parts", "member"), None),
            P("space", ("parts", "member"), None),
            P("parts"),
            P(),
        ),
        out_specs=(P(("parts", "space"), None), P("space", ("parts", "member"), None)),
        check_vma=False,
    )
```

time: 559 us -> 338 us (0.60); the launches traced: 552 us -> 337 us
  matrix products: 164 us -> 0 us
  Pallas kernels: 0 us -> 145 us
  local copies, waits for them, and re-layouts: 124 us -> 46.5 us
  other arithmetic: 61.9 us -> 2.88 us
  waiting for transfers between devices: 153 us -> 94.7 us
  between operations: 15.1 us -> 1.62 us
  starting transfers between devices: 12 us -> 25.2 us
    dot_general x12 -> x0, matrix products: 164 us -> none  [the longest x6 86.1 us: row_pass(): jnp.einsum('...bq,bpq->...bp', window, band[:, offset], precision=lax.Pre...]
    pallas_call x0 -> x11, Pallas kernels: none -> 145 us  [the longest x6 94.4 us: blur(): pl.pallas_call(functools.partial(blur_kernel, plan), in_specs=[ANY] * len...]
    slice x8 -> x3, local copies, waits for them, and re-layouts: 60.9 us -> 6.77 us  [the longest x2 5.97 us: local(): top = scaling[:width, 0, start:stop]]
    psum x1 -> x0, waiting for transfers between devices: 43.2 us -> none  [local(): logmean = lax.psum(terms, 'member')]
    reshape x3 -> x0, local copies, waits for them, and re-layouts: 26.3 us -> none  [the longest x2 17.3 us: row_pass(): blocks = field.reshape(lead + (nblocks, width))]
    div x2 -> x0, other arithmetic: 20.6 us -> none  [the longest x1 11.3 us: local(): ratio = densities / blurred]
    concatenate x2, other arithmetic: 18 us -> 1.65 us  [the longest x1 0.87 us: local(): jnp.concatenate([jnp.pad(mine[1 + i], ((0, 0), (i * width, (inner - 1 - i...]
    mul x1 -> x0, other arithmetic: 15.9 us -> none  [local(): local_shares[None, :, None] * jnp.log(scaling * smeared)]
  transfers between devices with their start and end apart: 5 -> 11, of which waited for: 3 -> 3; matrix products, arithmetic and copies ran while one was open for 12% -> 12% of each run, Pallas kernels for 0% -> 26%
where the time goes in v1:
time: 338 us; the launch traced here: 337 us
  Pallas kernels  145 us (43%)
  waiting for transfers between devices  94.7 us (28%)
  local copies, waits for them, and re-layouts  46.5 us (14%)
  starting transfers between devices  25.2 us (7%)
  blocking collectives  20.9 us (6%)
    pallas_call x6, Pallas kernels, blur(): pl.pallas_call(functools.partial(blur_kernel, plan), in_specs=[ANY] * len...  94.4 us
    ppermute x2, waiting for transfers between devices, local(): lax.ppermute(got[-1], 'space', forward)  83.3 us
    unnamed x32, local copies, waits for them, and re-layouts  36.6 us
    pallas_call x3, Pallas kernels, raw_piece(): pl.pallas_call(functools.partial(raw_kernel, (extra, column, fresh)), in_...  22.5 us
    psum x1, blocking collectives, local(): mass = lax.psum(mass, 'space')  20.9 us
    pallas_call x1, Pallas kernels, outputs(): pl.pallas_call(output_kernel, grid=(rows // tile,), in_specs=[flat, flat,...  16.7 us
    pallas_call x1, Pallas kernels, row_weights(): pl.pallas_call(functools.partial(weight_kernel, nblocks), grid=(nblocks /...  11.7 us
    ppermute x2, waiting for transfers between devices, local(): lax.ppermute(bottom, 'space', forward)  11.3 us
  transfers between devices with their start and end apart: 11, of which 3 were waited for; matrix products, arithmetic and copies ran while one was open for 12% of the time, Pallas kernels for 26%

profile of v1, /device:TPU:0, one launch (start us, length us, event | category | flops | bytes accessed | tf_op | source)
XLA Modules:
  0.0 337.1 jit_solution(3972412519854825398)
XLA Ops:
  0.6 2.7 fusion
  4.4 5.8 %collective-permute-start.3 = (f32[128,1792]{1,0:T(8,128)}, f32[128,1792]{1,0:T(8,128)}, u32[]{:S(2)}, u32[]{:S(2)}) collective-permute-start(f32[128,1792]{1,0:T(8,128)} %bitcast.21), channel_id=1, source_target_pairs={{0,2},{2,4},{4,6},{6,8},{8,10},{10,12},{12,14},{1,3},{3,5},{5,7},{... | collective-permute-start | bytes 2752520 | tf_op jit(solution)/shard_map/ppermute | solution.py:270
  12.4 3.2 fusion.1
  16.8 4.6 %collective-permute-start = (f32[128,2304]{1,0:T(8,128)}, f32[128,2304]{1,0:T(8,128)S(1)}, u32[]{:S(2)}, u32[]{:S(2)}) collective-permute-start(f32[128,2304]{1,0:T(8,128)} %bitcast.19), channel_id=1, source_target_pairs={{0,2},{2,4},{4,6},{6,8},{8,10},{10,12},{12,14},{1,3},{3,5},{5,7},{... | collective-permute-start | bytes 3538952 | tf_op jit(solution)/shard_map/ppermute | solution.py:270
  23.8 2.1 constant_dynamic-slice_fusion
  27.3 24.5 %copy_bitcast_fusion = (f32[512,4096]{1,0:T(8,128)}, f32[512,4096]{1,0:T(8,128)}) fusion(f32[512,1,4096]{2,1,0:T(1,128)} %param.4, f32[512,1,4096]{2,1,0:T(1,128)} %param.5), kind=kLoop, calls=%fused_computation | loop fusion | bytes 33554432
  52.6 11.7 %row_weights.1 = (bf16[16,256,512]{2,1,0:T(8,128)(2,1)}, bf16[16,256,512]{2,1,0:T(8,128)(2,1)}) custom-call(f32[32,3,128,128]{3,2,1,0:T(8,128)} %band_ref.1), custom_call_target="tpu_custom_call" | custom-call | tf_op jit(solution)/shard_map/row_weights/pallas_call | solution.py:54
  68.3 19.7 %ratio_inner.1.refs_0_ = f32[256,4096]{1,0:T(8,128)} custom-call(f32[512,4096]{1,0:T(8,128)} %get-tuple-element.61.refs_0_.refs_12_.refs_8_, f32[256,512]{1,0:T(8,128)} %select_maximum_fusion.refs_1_.refs_5_, bf16[16,256,512]{2,1,0:T(8,128)(2,1)} %get-tuple-element.25.refs_2_.refs_4_.refs_6_.refs_10_, ...), custom_call_target="tpu_custom_call" | custom-call | flops 6442450944 | bytes 29360128 | tf_op jit(solution)/shard_map/ratio_inner/pallas_call | solution.py:155
  88.1 11.3 %collective-permute-done.refs_1_ = f32[128,2304]{1,0:T(8,128)S(1)} collective-permute-done((f32[128,2304]{1,0:T(8,128)}, f32[128,2304]{1,0:T(8,128)S(1)}, u32[]{:S(2)}, u32[]{:S(2)}) %collective-permute-start) | collective-permute-done | bytes 1179680 | tf_op jit(solution)/shard_map/ppermute | solution.py:270
  101.4 12.3 %ratio_edges_0.1 = (f32[128,2048]{1,0:T(8,128)}, f32[128,2048]{1,0:T(8,128)}) custom-call(f32[512,4096]{1,0:T(8,128)} %get-tuple-element.61.refs_0_.refs_12_.refs_8_, f32[128,2304]{1,0:T(8,128)} %copy-done.2, f32[128,2304]{1,0:T(8,128)} %copy-done.3, f32[256,384]{1,0:T(8,128)} %pad_maximum_fusion.refs_3_.refs_5_.refs_9_, ...), custom_call_target="tpu_custom_call" | custom-call | flops 4026531840 | bytes 16777216 | tf_op jit(solution)/shard_map/ratio_edges_0/pallas_call | solution.py:155
  113.8 12.4 %ratio_edges_1.1 = (f32[128,2048]{1,0:T(8,128)}, f32[128,2048]{1,0:T(8,128)}) custom-call(f32[512,4096]{1,0:T(8,128)} %get-tuple-element.61.refs_0_.refs_12_.refs_8_, f32[128,2304]{1,0:T(8,128)} %copy-done.2, f32[128,1792]{1,0:T(8,128)} %collective-permute-done.3.refs_2_, f32[128,2304]{1,0:T(8,128)} %copy-done.3, ...), custom_call_target="tpu_custom_call" | custom-call | flops 4026531840 | bytes 16777216 | tf_op jit(solution)/shard_map/ratio_edges_1/pallas_call | solution.py:155
  126.2 22.3 %logs_inner.1 = (f32[256,4096]{1,0:T(8,128)}, f32[256,4096]{1,0:T(8,128)}) custom-call(f32[256,4096]{1,0:T(8,128)} %ratio_inner.1.refs_0_, f32[128,2048]{1,0:T(8,128)} %get-tuple-element.29.refs_5_.refs_3_.refs_1_, f32[128,2048]{1,0:T(8,128)} %get-tuple-element.30.refs_6_.refs_2_, f32[128,2048]{1,0:T(8,128)} %get-tuple-element.27.refs_7_.refs_4_.refs_3_, ...), custom_call_target="tpu_custom_call" | custom-call | flops 6442450944 | bytes 29360128 | tf_op jit(solution)/shard_map/logs_inner/pallas_call | solution.py:155
  148.5 4.3 %collective-permute-start.5 = (f32[128,2048]{1,0:T(8,128)}, f32[128,2048]{1,0:T(8,128)S(1)}, u32[]{:S(2)}, u32[]{:S(2)}) collective-permute-start(f32[128,2048]{1,0:T(8,128)} %get-tuple-element.28.refs_8_.refs_4_), channel_id=1, source_target_pairs={{0,2},{2,4},{4,6},{6,8},{8,10},{10,12},{12,14},{1,3},{3,5},{5,7},{... | collective-permute-start | bytes 3145736 | tf_op jit(solution)/shard_map/ppermute | solution.py:328
  154.2 4.6 %collective-permute-start.2 = (f32[128,2048]{1,0:T(8,128)S(1)}, f32[128,2048]{1,0:T(8,128)S(1)}, u32[]{:S(2)}, u32[]{:S(2)}) collective-permute-start(f32[128,2048]{1,0:T(8,128)S(1)} %copy-done.1), channel_id=1, source_target_pairs={{0,2},{2,4},{4,6},{6,8},{8,10},{10,12},{12,14},{1,3},{3,5},{5,7},{... | collective-permute-start | bytes 3145736 | tf_op jit(solution)/shard_map/ppermute | solution.py:328
  160.1 61.4 %collective-permute-done.5.refs_2_ = f32[128,2048]{1,0:T(8,128)S(1)} collective-permute-done((f32[128,2048]{1,0:T(8,128)}, f32[128,2048]{1,0:T(8,128)S(1)}, u32[]{:S(2)}, u32[]{:S(2)}) %collective-permute-start.5) | collective-permute-done | bytes 1048608 | tf_op jit(solution)/shard_map/ppermute | solution.py:328
  221.5 22.0 %collective-permute-done.2.refs_1_ = f32[128,2048]{1,0:T(8,128)S(1)} collective-permute-done((f32[128,2048]{1,0:T(8,128)S(1)}, f32[128,2048]{1,0:T(8,128)S(1)}, u32[]{:S(2)}, u32[]{:S(2)}) %collective-permute-start.2) | collective-permute-done | bytes 1048608 | tf_op jit(solution)/shard_map/ppermute | solution.py:328
  244.5 15.1 %logs_edges_1.1 = (f32[256,2304]{1,0:T(8,128)}, f32[256,2304]{1,0:T(8,128)}) custom-call(f32[256,4096]{1,0:T(8,128)} %ratio_inner.1.refs_0_, f32[128,2048]{1,0:T(8,128)} %copy-done.6, f32[128,2048]{1,0:T(8,128)} %copy-done.8, f32[128,2048]{1,0:T(8,128)} %collective-permute-done.6.refs_3_.refs_2_, f32[128,2048]{1,0:T(8,128)} %copy-done.9, ...), custom_call_target="tpu_custom_call" | custom-call | flops 4529848320 | bytes 18874368 | tf_op jit(solution)/shard_map/logs_edges_1/pallas_call | solution.py:155
  259.7 12.6 %logs_edges_0.1 = (f32[256,1792]{1,0:T(8,128)}, f32[256,1792]{1,0:T(8,128)}) custom-call(f32[256,4096]{1,0:T(8,128)} %ratio_inner.1.refs_0_, f32[128,2048]{1,0:T(8,128)} %copy-done.6, f32[128,2048]{1,0:T(8,128)} %collective-permute-done.6.refs_3_.refs_2_, f32[128,2048]{1,0:T(8,128)} %get-tuple-element.29.refs_5_.refs_3_.refs_1_, ...), custom_call_target="tpu_custom_call" | custom-call | flops 3523215360 | bytes 14680064 | tf_op jit(solution)/shard_map/logs_edges_0/pallas_call | solution.py:155
  272.9 2.0 copy-done.4
  274.9 9.1 %raw_inner.1 = (f32[512,4096]{1,0:T(8,128)}, f32[512,4096]{1,0:T(8,128)}, f32[1]{0:T(128)}) custom-call(f32[256,4096]{1,0:T(8,128)} %get-tuple-element.35.t_ref, f32[256,4096]{1,0:T(8,128)} %copy-done.4, f32[256,4096]{1,0:T(8,128)} %get-tuple-element.36.m_ref), custom_call_target="tpu_custom_call" | custom-call | flops 4194304 | bytes 20971520 | tf_op jit(solution)/shard_map/raw_inner/pallas_call | solution.py:206
  283.9 6.3 %raw_edges_0.1 = (f32[512,4096]{1,0:T(8,128)}, f32[512,4096]{1,0:T(8,128)}, f32[1]{0:T(128)}) custom-call(f32[256,1792]{1,0:T(8,128)} %get-tuple-element.33.t_ref, f32[256,1792]{1,0:T(8,128)} %collective-permute-done.9.peer_ref, f32[256,1792]{1,0:T(8,128)} %get-tuple-element.34.m_ref, ...), custom_call_target="tpu_custom_call", output_to_operand_aliasing={{0}: (3, {}), {1}: (4, {})} | custom-call | flops 1835008 | bytes 9175040 | tf_op jit(solution)/shard_map/raw_edges_0/pallas_call | solution.py:206
  291.7 7.1 %raw_edges_1.1 = (f32[512,4096]{1,0:T(8,128)}, f32[512,4096]{1,0:T(8,128)}, f32[1]{0:T(128)}) custom-call(f32[256,2304]{1,0:T(8,128)} %get-tuple-element.31.t_ref, f32[256,2304]{1,0:T(8,128)} %copy-done.7, f32[256,2304]{1,0:T(8,128)} %get-tuple-element.32.m_ref, ...), custom_call_target="tpu_custom_call", output_to_operand_aliasing={{0}: (3, {}), {1}: (4, {})} | custom-call | flops 2359296 | bytes 11796480 | tf_op jit(solution)/shard_map/raw_edges_1/pallas_call | solution.py:206
  298.8 20.9 %psum.7 = f32[1]{0:T(128)} all-reduce(f32[1]{0:T(128)} %get-tuple-element.45), channel_id=1, replica_groups=mesh['parts'=2,'space'=8,'member'=2] {'space'}, use_global_device_ids=true, to_apply=%region_1.2 | all-reduce | flops 1 | bytes 8 | tf_op jit(solution)/shard_map/psum | solution.py:368
  320.5 16.7 %outputs.1 = (f32[512,4096]{1,0:T(8,128)}, f32[512,32,128]{2,1,0:T(8,128)}) custom-call(f32[512,4096]{1,0:T(8,128)} %get-tuple-element.43.raw_ref, f32[512,4096]{1,0:T(8,128)} %get-tuple-element.44.quotient_ref, f32[1]{0:T(128)S(6)} %div.11.scale_ref), custom_call_target="tpu_custom_call" | custom-call | tf_op jit(solution)/shard_map/outputs/pallas_call | solution.py:235
  (55 shorter events, 20.7 us)
Async XLA Ops:
  4.4 109.4 %collective-permute-start.3 = (f32[128,1792]{1,0:T(8,128)}, f32[128,1792]{1,0:T(8,128)}, u32[]{:S(2)}, u32[]{:S(2)}) collective-permute-start(f32[128,1792]{1,0:T(8,128)} %bitcast.21), channel_id=1, source_target_pairs={{0,2},{2,4},{4,6},{6,8},{8,10},{10,12},{12,14},{1,3},{3,5},{5,7},{... | collective-permute-start | bytes 2752520 | tf_op jit(solution)/shard_map/ppermute | solution.py:270
  11.1 102.6 %collective-permute-start.4 = (f32[128,1792]{1,0:T(8,128)}, f32[128,1792]{1,0:T(8,128)}, u32[]{:S(2)}, u32[]{:S(2)}) collective-permute-start(f32[128,1792]{1,0:T(8,128)} %bitcast.20), channel_id=1, source_target_pairs={{2,0},{4,2},{6,4},{8,6},{10,8},{12,10},{14,12},{3,1},{5,3},{7,5},{... | collective-permute-start | bytes 2752520 | tf_op jit(solution)/shard_map/ppermute | solution.py:270
  16.8 82.6 %collective-permute-start = (f32[128,2304]{1,0:T(8,128)}, f32[128,2304]{1,0:T(8,128)S(1)}, u32[]{:S(2)}, u32[]{:S(2)}) collective-permute-start(f32[128,2304]{1,0:T(8,128)} %bitcast.19), channel_id=1, source_target_pairs={{0,2},{2,4},{4,6},{6,8},{8,10},{10,12},{12,14},{1,3},{3,5},{5,7},{... | collective-permute-start | bytes 3538952 | tf_op jit(solution)/shard_map/ppermute | solution.py:270
  22.5 76.8 %collective-permute-start.1 = (f32[128,2304]{1,0:T(8,128)}, f32[128,2304]{1,0:T(8,128)S(1)}, u32[]{:S(2)}, u32[]{:S(2)}) collective-permute-start(f32[128,2304]{1,0:T(8,128)} %bitcast.18), channel_id=1, source_target_pairs={{2,0},{4,2},{6,4},{8,6},{10,8},{12,10},{14,12},{3,1},{5,3},{7,5},{... | collective-permute-start | bytes 3538952 | tf_op jit(solution)/shard_map/ppermute | solution.py:270
  51.8 13.1 %copy-start.12 = (f32[2]{0:T(128)S(1)}, f32[2]{0:T(128)}, u32[]{:S(2)}) copy-start(f32[2]{0:T(128)} %param.6) | copy-start | bytes 28
  52.6 11.7 %copy-start.11 = (f32[1,128,3,128]{1,3,2,0:T(8,128)S(1)}, f32[1,128,3,128]{1,3,2,0:T(8,128)}, u32[]{:S(2)}) copy-start(f32[1,128,3,128]{1,3,2,0:T(8,128)} %get-tuple-element.56) | copy-start | bytes 589828
  52.6 11.8 %copy-start.10 = (f32[1,128,3,128]{1,3,2,0:T(8,128)S(1)}, f32[1,128,3,128]{1,3,2,0:T(8,128)}, u32[]{:S(2)}) copy-start(f32[1,128,3,128]{1,3,2,0:T(8,128)} %get-tuple-element.57) | copy-start | bytes 589828
  99.4 1.0 copy-start.2
  100.4 1.0 copy-start.3
  126.1 26.7 %copy-start.5 = (f32[128,2048]{1,0:T(8,128)S(1)}, f32[128,2048]{1,0:T(8,128)}, u32[]{:S(2)}) copy-start(f32[128,2048]{1,0:T(8,128)} %get-tuple-element.30.refs_6_.refs_2_) | copy-start | bytes 3145732
  126.1 28.0 %copy-start.1 = (f32[128,2048]{1,0:T(8,128)S(1)}, f32[128,2048]{1,0:T(8,128)}, u32[]{:S(2)}) copy-start(f32[128,2048]{1,0:T(8,128)} %get-tuple-element.27.refs_7_.refs_4_.refs_3_) | copy-start | bytes 3145732
  126.2 32.7 %copy-start = (f32[128,2048]{1,0:T(8,128)S(1)}, f32[128,2048]{1,0:T(8,128)}, u32[]{:S(2)}) copy-start(f32[128,2048]{1,0:T(8,128)} %get-tuple-element.29.refs_5_.refs_3_.refs_1_) | copy-start | bytes 3145732
  148.5 124.4 %collective-permute-start.10 = (f32[256,4096]{1,0:T(8,128)}, f32[256,4096]{1,0:T(8,128)S(1)}, u32[]{:S(2)}, u32[]{:S(2)}) collective-permute-start(f32[256,4096]{1,0:T(8,128)} %get-tuple-element.35.t_ref), channel_id=1, source_target_pairs={{0,1},{1,0},{2,3},{3,2},{4,5},{5,4},{6,7},{7,6},{8,9},{9,8},{10,11... | collective-permute-start | bytes 12582920 | tf_op jit(solution)/shard_map/ppermute | solution.py:340
  148.5 73.0 %collective-permute-start.5 = (f32[128,2048]{1,0:T(8,128)}, f32[128,2048]{1,0:T(8,128)S(1)}, u32[]{:S(2)}, u32[]{:S(2)}) collective-permute-start(f32[128,2048]{1,0:T(8,128)} %get-tuple-element.28.refs_8_.refs_4_), channel_id=1, source_target_pairs={{0,2},{2,4},{4,6},{6,8},{8,10},{10,12},{12,14},{1,3},{3,5},{5,7},{... | collective-permute-start | bytes 3145736 | tf_op jit(solution)/shard_map/ppermute | solution.py:328
  152.9 68.6 %collective-permute-start.7 = (f32[128,2048]{1,0:T(8,128)S(1)}, f32[128,2048]{1,0:T(8,128)S(1)}, u32[]{:S(2)}, u32[]{:S(2)}) collective-permute-start(f32[128,2048]{1,0:T(8,128)S(1)} %copy-done.5), channel_id=1, source_target_pairs={{2,0},{4,2},{6,4},{8,6},{10,8},{12,10},{14,12},{3,1},{5,3},{7,5},{... | collective-permute-start | bytes 3145736 | tf_op jit(solution)/shard_map/ppermute | solution.py:328
  154.2 89.3 %collective-permute-start.2 = (f32[128,2048]{1,0:T(8,128)S(1)}, f32[128,2048]{1,0:T(8,128)S(1)}, u32[]{:S(2)}, u32[]{:S(2)}) collective-permute-start(f32[128,2048]{1,0:T(8,128)S(1)} %copy-done.1), channel_id=1, source_target_pairs={{0,2},{2,4},{4,6},{6,8},{8,10},{10,12},{12,14},{1,3},{3,5},{5,7},{... | collective-permute-start | bytes 3145736 | tf_op jit(solution)/shard_map/ppermute | solution.py:328
  158.8 85.7 %collective-permute-start.6 = (f32[128,2048]{1,0:T(8,128)S(1)}, f32[128,2048]{1,0:T(8,128)}, u32[]{:S(2)}, u32[]{:S(2)}) collective-permute-start(f32[128,2048]{1,0:T(8,128)S(1)} %copy-done), channel_id=1, source_target_pairs={{2,0},{4,2},{6,4},{8,6},{10,8},{12,10},{14,12},{3,1},{5,3},{7,5},{... | collective-permute-start | bytes 3145736 | tf_op jit(solution)/shard_map/ppermute | solution.py:328
  221.5 22.0 %copy-start.8 = (f32[128,2048]{1,0:T(8,128)}, f32[128,2048]{1,0:T(8,128)S(1)}, u32[]{:S(2)}) copy-start(f32[128,2048]{1,0:T(8,128)S(1)} %collective-permute-done.5.refs_2_) | copy-start | bytes 3145732
  221.5 22.0 %copy-start.9 = (f32[128,2048]{1,0:T(8,128)}, f32[128,2048]{1,0:T(8,128)S(1)}, u32[]{:S(2)}) copy-start(f32[128,2048]{1,0:T(8,128)S(1)} %collective-permute-done.7.refs_4_) | copy-start | bytes 3145732
  243.5 1.0 copy-start.6
  259.6 30.6 %collective-permute-start.8 = (f32[256,2304]{1,0:T(8,128)}, f32[256,2304]{1,0:T(8,128)S(1)}, u32[]{:S(2)}, u32[]{:S(2)}) collective-permute-start(f32[256,2304]{1,0:T(8,128)} %get-tuple-element.31.t_ref), channel_id=1, source_target_pairs={{0,1},{1,0},{2,3},{3,2},{4,5},{5,4},{6,7},{7,6},{8,9},{9,8},{10,11... | collective-permute-start | bytes 7077896 | tf_op jit(solution)/shard_map/ppermute | solution.py:364
  272.3 11.6 %collective-permute-start.9 = (f32[256,1792]{1,0:T(8,128)}, f32[256,1792]{1,0:T(8,128)}, u32[]{:S(2)}, u32[]{:S(2)}) collective-permute-start(f32[256,1792]{1,0:T(8,128)} %get-tuple-element.33.t_ref), channel_id=1, source_target_pairs={{0,1},{1,0},{2,3},{3,2},{4,5},{5,4},{6,7},{7,6},{8,9},{9,8},{10,11... | collective-permute-start | bytes 5505032 | tf_op jit(solution)/shard_map/ppermute | solution.py:364
  272.9 2.0 copy-start.4
  290.3 1.4 copy-start.7

commit v2 on v0

v2 whole, which is shorter than its diff:
```python
import functools

import jax
import jax.numpy as jnp
from jax import lax
from jax.experimental import pallas as pl
from jax.experimental.pallas import tpu as pltpu
from jax.sharding import PartitionSpec as P

F32 = jnp.float32
BF16 = jnp.bfloat16
VMEM_LIMIT = 48 * 1024 * 1024
GROUPS = 4
ANY = pl.BlockSpec(memory_space=pl.ANY)
INVMEM = pl.BlockSpec(memory_space=pltpu.VMEM)
INSMEM = pl.BlockSpec(memory_space=pltpu.SMEM)


def split(x):
    high = x.astype(BF16)
    return high, (x - high.astype(F32)).astype(BF16)


def dot3(a, b, dims):
    one = functools.partial(lax.dot_general, dimension_numbers=(dims, ((), ())), preferred_element_type=F32)
    return one(a[0], b[0]) + (one(a[0], b[1]) + one(a[1], b[0]))


def params():
    return pltpu.CompilerParams(vmem_limit_bytes=VMEM_LIMIT)


def pick(choice, side):
    if isinstance(choice, tuple):
        return pl.multiple_of(jnp.where(side == 0, choice[0], choice[1]), 128)
    return choice


def flatten_kernel(*refs):
    half = len(refs) // 2
    for src, dst in zip(refs[:half], refs[half:]):
        width = src.shape[2]
        for b in range(src.shape[1]):
            dst[:, b * width : (b + 1) * width] = src[:, b, :]


def flatten(arrays, width):
    rows, _, columns = arrays[0].shape
    tile = 64
    deep = pl.BlockSpec((tile, columns // width, width), lambda i: (i, 0, 0))
    flat = pl.BlockSpec((tile, columns), lambda i: (i, 0))
    return pl.pallas_call(
        flatten_kernel,
        grid=(rows // tile,),
        in_specs=[deep] * len(arrays),
        out_specs=[flat] * len(arrays),
        out_shape=[jax.ShapeDtypeStruct((rows, columns), F32)] * len(arrays),
        compiler_params=params(),
        name="flatten",
    )(*[a.reshape(rows, columns // width, width) for a in arrays])


def weight_kernel(nblocks, band_ref, high_ref, low_ref):
    pair = pl.program_id(0)
    width = band_ref.shape[2]
    zero = jnp.zeros((width, width), F32)
    for o in range(2):
        for i in range(4):
            j = i - o
            value = band_ref[o, j] if 0 <= j <= 2 else zero
            if (o, j) == (0, 0):
                value = jnp.where(pair > 0, value, 0.0)
            if (o, j) == (1, 2):
                value = jnp.where(pair < nblocks // 2 - 1, value, 0.0)
            high, low = split(value)
            rows, columns = slice(o * width, (o + 1) * width), slice(i * width, (i + 1) * width)
            high_ref[0, rows, columns] = high
            low_ref[0, rows, columns] = low


def row_weights(band):
    nblocks, _, width, _ = band.shape
    shape = jax.ShapeDtypeStruct((nblocks // 2, 2 * width, 4 * width), BF16)
    out_spec = pl.BlockSpec((1, 2 * width, 4 * width), lambda t: (t, 0, 0))
    return pl.pallas_call(
        functools.partial(weight_kernel, nblocks),
        grid=(nblocks // 2,),
        in_specs=[pl.BlockSpec((2, 3, width, width), lambda t: (t, 0, 0, 0))],
        out_specs=(out_spec, out_spec),
        out_shape=(shape, shape),
        name="row_weights",
    )(band)


def blur_kernel(plan, *refs):
    pieces, narrays, extra, final = plan
    side_ref, refs = refs[0], refs[1:]
    arrays = refs[:narrays]
    band_ref, high_ref, low_ref, extra_ref = refs[narrays : narrays + 4]
    rest = refs[narrays + 4 :]
    if final:
        share_ref, rest = rest[0], rest[1:]
    nouts = GROUPS + 1 if final else 1
    outs = rest[:nouts]
    field, ahigh, alow, yhigh, ylow, whigh, wlow, other = rest[nouts : nouts + 8]
    *results, in_sems, late_sems, out_sems = rest[nouts + 8 :]

    side = side_ref[0]
    nout, _, width, _ = band_ref.shape
    columns = field.shape[1]
    step = columns // GROUPS
    pairs = step // (2 * width)
    inside, late = [], []
    for g in range(GROUPS):
        at = pl.ds(g * step, step)
        inside.append(
            [
                pltpu.make_async_copy(
                    arrays[which].at[pl.ds(pick(row, side), rows), at],
                    field.at[pl.ds(pick(to, side), rows), at],
                    in_sems.at[g, k],
                )
                for k, (which, row, rows, to) in enumerate(pieces)
            ]
        )
        some = pl.ds(g * pairs, pairs)
        late.append(
            [
                pltpu.make_async_copy(high_ref.at[some], whigh.at[some], late_sems.at[g, 0]),
                pltpu.make_async_copy(low_ref.at[some], wlow.at[some], late_sems.at[g, 1]),
                pltpu.make_async_copy(
                    extra_ref.at[pl.ds(pick(extra, side), other.shape[0]), at], other.at[:, at], late_sems.at[g, 2]
                ),
            ]
        )
    for g in range(GROUPS):
        for copy in inside[g]:
            copy.start()
        if g > 0:
            for copy in late[g - 1]:
                copy.start()
    for copy in late[GROUPS - 1]:
        copy.start()

    ahigh[...] = jnp.zeros_like(ahigh)
    alow[...] = jnp.zeros_like(alow)
    for i in range(nout):
        for j in range(3):
            k = i % 2 + j
            place = (slice(i * width, (i + 1) * width), slice(k * width, (k + 1) * width))
            ahigh[place], alow[place] = split(band_ref[i, j])
    blocks = [(i, min(2, nout - i)) for i in range(0, nout, 2)]
    for y in (yhigh, ylow):
        y[:, :width] = jnp.zeros((y.shape[0], width), BF16)
        y[:, columns + width :] = jnp.zeros((y.shape[0], width), BF16)

    def columns_pass(g):
        for copy in inside[g]:
            copy.wait()
        for i in range(g * pairs, (g + 1) * pairs):
            at = slice(i * 2 * width, (i + 1) * 2 * width)
            to = slice((2 * i + 1) * width, (2 * i + 3) * width)
            for first, n in blocks:
                rows = slice(first * width, (first + n) * width)
                a = (ahigh[rows, : (n + 2) * width], alow[rows, : (n + 2) * width])
                y = dot3(a, split(field[first * width : (first + n + 2) * width, at]), ((1,), (0,)))
                yhigh[rows, to], ylow[rows, to] = split(y)

    def rows_pass(g):
        for copy in late[g]:
            copy.wait()
        for t in range(g * pairs, (g + 1) * pairs):
            source = slice(t * 2 * width, (t + 2) * 2 * width)
            at = slice(t * 2 * width, (t + 1) * 2 * width)
            value = dot3((yhigh[:, source], ylow[:, source]), (whigh[t], wlow[t]), ((1,), (1,)))
            if final:
                results[0][:, at] = value
                results[1][:, at] = share_ref[0] * jnp.log(other[:, at] * value)
            else:
                results[0][:, at] = other[:, at] / value
        at = pl.ds(g * step, step)
        targets = [outs[-1].at[:, at]] + ([outs[g]] if final else [])
        copies = [
            pltpu.make_async_copy(src.at[:, at], dst, out_sems.at[g, k])
            for k, (src, dst) in enumerate(zip(results, targets))
        ]
        for copy in copies:
            copy.start()
        return copies

    going = []
    for g in range(GROUPS):
        columns_pass(g)
        if g > 0:
            going += rows_pass(g - 1)
    going += rows_pass(GROUPS - 1)
    for copy in going:
        copy.wait()


def blur(name, side, arrays, pieces, bands, weights, other, extra, share=None):
    nout, _, width, _ = bands.shape
    npairs = weights[0].shape[0]
    columns = npairs * 2 * width
    rows, depth = nout * width, (nout + 2) * width
    final = share is not None
    nouts = 2 if final else 1
    shapes = [jax.ShapeDtypeStruct((rows, columns // GROUPS), F32)] * (GROUPS if final else 0)
    shapes.append(jax.ShapeDtypeStruct((rows, columns), F32))
    plan = (tuple(pieces), len(arrays), extra, final)
    work = 3 * 2 * rows * columns * (depth + 4 * width)
    moved = 4 * (depth + 3 * rows) * columns + npairs * 2 * 2 * 8 * width * width
    result = pl.pallas_call(
        functools.partial(blur_kernel, plan),
        in_specs=[INSMEM] + [ANY] * len(arrays) + [INVMEM, ANY, ANY, ANY] + [INSMEM] * final,
        out_specs=[ANY] * len(shapes),
        out_shape=shapes,
        scratch_shapes=[
            pltpu.VMEM((depth, columns), F32),
            pltpu.VMEM((rows, min(depth, 4 * width)), BF16),
            pltpu.VMEM((rows, min(depth, 4 * width)), BF16),
            pltpu.VMEM((rows, columns + 2 * width), BF16),
            pltpu.VMEM((rows, columns + 2 * width), BF16),
            pltpu.VMEM((npairs, 2 * width, 4 * width), BF16),
            pltpu.VMEM((npairs, 2 * width, 4 * width), BF16),
            pltpu.VMEM((rows, columns), F32),
        ]
        + [pltpu.VMEM((rows, columns), F32)] * nouts
        + [
            pltpu.SemaphoreType.DMA((GROUPS, len(pieces))),
            pltpu.SemaphoreType.DMA((GROUPS, 3)),
            pltpu.SemaphoreType.DMA((GROUPS, nouts)),
        ],
        compiler_params=params(),
        cost_estimate=pl.CostEstimate(flops=work // 64, bytes_accessed=moved // 64, transcendentals=0),
        name=name,
    )(side, *arrays, bands, *weights, other, *([share] if final else []))
    return (result[:-1], result[-1]) if final else result[0]


def raw_kernel(fresh, start_ref, *refs):
    own, peer, m_ref = refs[:GROUPS], refs[GROUPS : 2 * GROUPS], refs[2 * GROUPS]
    raw_ref, quotient_ref, mass_ref = refs[-3:]
    width = quotient_ref.shape[2]
    mass = 0.0
    for g in range(GROUPS):
        raw = jnp.exp(own[g][...] + peer[g][...])
        step = raw.shape[1]
        raw_ref[:, g * step : (g + 1) * step] = raw
        mass += jnp.sum(raw)
        quotient = raw / m_ref[:, g * step : (g + 1) * step]
        for b in range(step // width):
            quotient_ref[:, g * (step // width) + b, :] = quotient[:, b * width : (b + 1) * width]
    before = 0.0 if fresh else refs[2 * GROUPS + 3][0]
    mass_ref[0] = mass + jnp.where(pl.program_id(0) == 0, before, mass_ref[0])


def raw_rows(name, row, t, swap, m, choose, rows_here, width, so_far):
    fresh = so_far is None
    rows, columns = m.shape
    tile = 32
    part = pl.BlockSpec((tile, columns), lambda i, at: (i, 0))
    group = pl.BlockSpec((tile, columns // GROUPS), lambda i, at: (i, 0))
    deep = columns // width
    return pl.pallas_call(
        functools.partial(raw_kernel, fresh),
        grid_spec=pltpu.PrefetchScalarGridSpec(
            num_scalar_prefetch=1,
            grid=(rows // tile,),
            in_specs=[group] * (2 * GROUPS) + [part] + ([] if fresh else [ANY, ANY, INSMEM]),
            out_specs=(
                pl.BlockSpec((tile, columns), lambda i, at: (at[0] + i, 0)),
                pl.BlockSpec((tile, deep, width), lambda i, at: (at[0] + i, 0, 0)),
                INSMEM,
            ),
        ),
        out_shape=(
            jax.ShapeDtypeStruct((rows_here, columns), F32),
            jax.ShapeDtypeStruct((rows_here, deep, width), F32),
            jax.ShapeDtypeStruct((1,), F32),
        ),
        input_output_aliases={} if fresh else {2 * GROUPS + 2: 0, 2 * GROUPS + 3: 1},
        compiler_params=params(),
        cost_estimate=pl.CostEstimate(flops=m.size // 16, bytes_accessed=m.size // 4, transcendentals=0),
        name=name,
    )(choose([r // tile for r in row]).reshape(1), *t, *[swap(part) for part in t], m, *([] if fresh else so_far))


def output_kernel(raw_ref, quotient_ref, scale_ref, barycenter_ref, scaling_ref):
    scale = scale_ref[0]
    barycenter_ref[...] = raw_ref[...] * scale
    scaling_ref[...] = quotient_ref[...] * scale


def outputs(raw, quotient, scale):
    rows, columns = raw.shape
    tile = 64
    flat = pl.BlockSpec((tile, columns), lambda i: (i, 0))
    deep = pl.BlockSpec((tile,) + quotient.shape[1:], lambda i: (i, 0, 0))
    return pl.pallas_call(
        output_kernel,
        grid=(rows // tile,),
        in_specs=[flat, deep, INSMEM],
        out_specs=(flat, deep),
        out_shape=(jax.ShapeDtypeStruct(raw.shape, F32), jax.ShapeDtypeStruct(quotient.shape, F32)),
        compiler_params=params(),
        name="outputs",
    )(raw, quotient, scale)


def local(densities, scaling, weights, band):
    rows_here, maps_here, cols_all = densities.shape
    _, _, width, _ = band.shape
    nlocal = rows_here // width
    inner = max(nlocal - 2, 0)
    place = lax.axis_index("space")
    count = lax.axis_size("space")
    assert maps_here == 1 and lax.axis_size("member") == 2 and count % 2 == 0

    odd = place & 1
    side = odd.reshape(1)
    last = rows_here - width
    cross_row, near_row = (0, last), (last, 0)
    both = lambda pairs: pairs + [(b, a) for a, b in pairs]
    cross = functools.partial(
        lax.ppermute, axis_name="space", perm=both([(i, i + 1) for i in range(1, count - 1, 2)])
    )
    near = functools.partial(lax.ppermute, axis_name="space", perm=both([(i, i + 1) for i in range(0, count, 2)]))
    swap = functools.partial(lax.ppermute, axis_name="member", perm=[(0, 1), (1, 0)])

    def choose(choice):
        return jnp.where(odd == 0, choice[0], choice[1]).astype(jnp.int32)

    def rows_of(choice):
        return lax.dynamic_slice_in_dim(scaling, choose(choice), width, 0).reshape(width, cols_all)

    cross1 = cross(rows_of(cross_row))
    near1 = near(rows_of(near_row))

    shares = weights / jnp.sum(weights)
    share = lax.dynamic_slice_in_dim(shares, lax.axis_index("member"), 1)
    own, dens = flatten([scaling, densities], width)
    wts = row_weights(band)
    mine = place * nlocal
    band_at = lambda row, blocks: lax.dynamic_slice_in_dim(band, mine + row // width, blocks, 0)

    if nlocal > 1:
        two = rows_here - 2 * width
        cross_pieces = [(0, (0, two), 2 * width, (width, 0)), (1, 0, width, (0, 2 * width))]
        near_pieces = [(0, (two, 0), 2 * width, (0, width)), (1, 0, width, (2 * width, 0))]
        edges = [("cross", cross_row, cross_pieces, cross), ("near", near_row, near_pieces, near)]
        halos1 = [[cross1], [near1]]
    else:
        pieces = [(0, 0, width, width), (1, 0, width, (0, 2 * width)), (2, 0, width, (2 * width, 0))]
        edges = [("only", (0, 0), pieces, None)]
        halos1 = [[cross1, near1]]
    edge_bands = [band_at(choose(row), 1) for _, row, _, _ in edges]

    if inner > 0:
        inner_bands = band_at(width, inner)
        ratio_inner = blur(
            "ratio_inner", side, [own], [(0, 0, rows_here, 0)], inner_bands, wts, dens, width
        )
    ratios, halos2 = [], []
    for (name, row, pieces, send), halo, bands in zip(edges, halos1, edge_bands):
        if ratios:
            bands, ratios[-1] = lax.optimization_barrier((bands, ratios[-1]))
        ratio = blur("ratio_" + name, side, [own] + halo, pieces, bands, wts, dens, row)
        ratios.append(ratio)
        halos2.append([cross(ratio), near(ratio)] if send is None else [send(ratio)])

    def finish(name, arrays, pieces, bands, row, share, state):
        t, m = blur("logs_" + name, side, arrays, pieces, bands, wts, own, row, share)
        return raw_rows("raw_" + name, row, t, swap, m, choose, rows_here, width, state)

    if nlocal == 1:
        state = finish("only", ratios + halos2[0], pieces, edge_bands[0], (0, 0), share, None)
    else:
        most, end = rows_here - width, rows_here
        pieces = [(0, 0, width, (width, most)), (1, 0, width, (end, 0)), (2, 0, width, (0, end))]
        if inner > 0:
            pieces.append((3, 0, inner * width, (2 * width, width)))
        arrays = ratios + halos2[0] + ([ratio_inner] if inner > 0 else [])
        row = (0, width)
        state = finish("most", arrays, pieces, band_at(choose(row), nlocal - 1), row, share, None)
        share, state = lax.optimization_barrier((share, state))
        if inner > 0:
            beside = (ratio_inner, ((inner - 1) * width, 0))
        else:
            beside = (ratios[0], 0)
        pieces = [(0, 0, width, width), (1, beside[1], width, (0, 2 * width)), (2, 0, width, (2 * width, 0))]
        state = finish("near", [ratios[1], beside[0]] + halos2[1], pieces, edge_bands[1], near_row, share, state)

    raw, quotient, mass = state
    mass = lax.psum(mass, "space")
    barycenter, new_scaling = outputs(raw, quotient, float(cols_all * cols_all) / mass)
    return barycenter, new_scaling.reshape(rows_here, 1, cols_all)


def solution(mesh):
    return jax.shard_map(
        local,
        mesh=mesh,
        in_specs=(
            P("space", ("parts", "member"), None),
            P("space", ("parts", "member"), None),
            P("parts"),
            P(),
        ),
        out_specs=(P(("parts", "space"), None), P("space", ("parts", "member"), None)),
        check_vma=False,
    )
```

time: 559 us -> 291 us (0.52)
  matrix products: 164 us -> 0 us
  Pallas kernels: 0 us -> 125 us
  local copies, waits for them, and re-layouts: 124 us -> 21.9 us
  other arithmetic: 61.9 us -> 1.14 us
  waiting for transfers between devices: 153 us -> 101 us
  between operations: 15.1 us -> 1.76 us
    dot_general x12 -> x0, matrix products: 164 us -> none  [the longest x6 86.1 us: row_pass(): jnp.einsum('...bq,bpq->...bp', window, band[:, offset], precision=lax.Pre...]
    pallas_call x0 -> x10, Pallas kernels: none -> 125 us  [the longest x5 60 us: blur(): pl.pallas_call(functools.partial(blur_kernel, plan), in_specs=[INSMEM] +...]
    slice x8 -> x0, local copies, waits for them, and re-layouts: 60.9 us -> none  [the longest x6 55.8 us: rim_col_pass(): blocks[offset:offset + nlocal]]
    psum x1 -> x0, waiting for transfers between devices: 43.2 us -> none  [local(): logmean = lax.psum(terms, 'member')]
    reshape x3 -> x0, local copies, waits for them, and re-layouts: 26.3 us -> none  [the longest x2 17.3 us: row_pass(): blocks = field.reshape(lead + (nblocks, width))]
    div x2 -> x0, other arithmetic: 20.6 us -> none  [the longest x1 11.3 us: local(): ratio = densities / blurred]
    concatenate x2 -> x0, other arithmetic: 18 us -> none  [with_halo(): block = jnp.concatenate([low, block, high], axis=dim)]
    mul x1 -> x0, other arithmetic: 15.9 us -> none  [local(): local_shares[None, :, None] * jnp.log(scaling * smeared)]
  transfers between devices with their start and end apart: 5 -> 12, of which waited for: 3 -> 9; matrix products, arithmetic and copies ran while one was open for 12% -> 3% of each run, Pallas kernels for 0% -> 33%
where the time goes in v2:
time: 291 us; the launch traced here: 286 us
  Pallas kernels  125 us (43%)
  waiting for transfers between devices  101 us (35%)
  local copies, waits for them, and re-layouts  21.9 us (8%)
  blocking collectives  21.3 us (7%)
  starting transfers between devices  13.6 us (5%)
    ppermute x1, waiting for transfers between devices, local(): near1 = near(rows_of(near_row))  88.1 us
    pallas_call x5, Pallas kernels, blur(): pl.pallas_call(functools.partial(blur_kernel, plan), in_specs=[INSMEM] +...  60 us
    pallas_call x2, Pallas kernels, raw_rows(): pl.pallas_call(functools.partial(raw_kernel, fresh), grid_spec=pltpu.Pref...  23.1 us
    psum x1, blocking collectives, local(): mass = lax.psum(mass, 'space')  21.3 us
    pallas_call x1, Pallas kernels, flatten(): pl.pallas_call(flatten_kernel, grid=(rows // tile,), in_specs=[deep] * le...  16.9 us
    pallas_call x1, Pallas kernels, outputs(): pl.pallas_call(output_kernel, grid=(rows // tile,), in_specs=[flat, deep,...  13.7 us
    ppermute x8, waiting for transfers between devices, raw_rows(): swap(part)  12.7 us
    unnamed x14, local copies, waits for them, and re-layouts  12.2 us
  transfers between devices with their start and end apart: 12, of which 9 were waited for; matrix products, arithmetic and copies ran while one was open for 3% of the time, Pallas kernels for 33%

profile of v2, /device:TPU:0, one launch (start us, length us, event | category | flops | bytes accessed | tf_op | source)
XLA Modules:
  0.0 285.8 jit_solution(6862913018361484826)
XLA Ops:
  0.6 6.0 %constant_dynamic-slice_fusion.3 = (f32[128,1,4096]{2,1,0:T(1,128)S(1)}, f32[128,1,4096]{2,1,0:T(1,128)S(1)}) fusion(f32[512,1,4096]{2,1,0:T(1,128)} %param.5, s32[]{:T(128)S(6)} %select_n.50, s32[]{:T(128)S(6)} %select_n.47), kind=kLoop, calls=%fused_computation.5 | loop fusion | bytes 8388616 | tf_op jit(solution)/shard_map/dynamic_slice | solution.py:335
  6.7 3.0 %copy.13 = f32[128,1,4096]{2,0,1:T(8,128)} copy(f32[128,1,4096]{2,1,0:T(1,128)S(1)} %get-tuple-element.60) | data formatting | bytes 4194304
  9.6 2.5 collective-permute-start.1
  12.1 3.0 %copy.14 = f32[128,1,4096]{2,0,1:T(8,128)} copy(f32[128,1,4096]{2,1,0:T(1,128)S(1)} %get-tuple-element.61) | data formatting | bytes 4194304
  15.1 4.4 %collective-permute-start = (f32[128,4096]{1,0:T(8,128)}, f32[128,4096]{1,0:T(8,128)S(1)}, u32[]{:S(2)}, u32[]{:S(2)}) collective-permute-start(f32[128,4096]{1,0:T(8,128)} %bitcast.11), channel_id=1, source_target_pairs={{0,2},{4,6},{8,10},{12,14},{2,0},{6,4},{10,8},{14,12},{1,3},{5,7},... | collective-permute-start | bytes 6291464 | tf_op jit(solution)/shard_map/ppermute | solution.py:338
  19.5 11.7 %row_weights.1 = (bf16[16,256,512]{2,1,0:T(8,128)(2,1)}, bf16[16,256,512]{2,1,0:T(8,128)(2,1)}) custom-call(f32[32,3,128,128]{3,2,1,0:T(8,128)} %band_ref.1), custom_call_target="tpu_custom_call" | custom-call | tf_op jit(solution)/shard_map/row_weights/pallas_call | solution.py:85
  31.2 16.9 %flatten.1 = (f32[512,4096]{1,0:T(8,128)}, f32[512,4096]{1,0:T(8,128)}) custom-call(f32[512,32,128]{2,1,0:T(8,128)} %bitcast.12, f32[512,32,128]{2,1,0:T(8,128)} %bitcast.13), custom_call_target="tpu_custom_call" | custom-call | tf_op jit(solution)/shard_map/flatten/pallas_call | solution.py:52
  49.1 11.1 %ratio_cross.1.refs_1_ = f32[128,4096]{1,0:T(8,128)} custom-call(s32[1]{0:T(128)} %bitcast.1.refs_0_, f32[512,4096]{1,0:T(8,128)} %get-tuple-element.30.refs_1_.refs_8_.refs_7_, f32[128,4096]{1,0:T(8,128)} %collective-permute-done.1.refs_2_, f32[1,3,128,128]{3,2,1,0:T(8,128)S(1)} %get-tuple-element.62.refs_3_, ...), custom_call_target="tpu_custom_call" | custom-call | flops 44040192 | bytes 327680 | tf_op jit(solution)/shard_map/ratio_cross/pallas_call | solution.py:213
  60.2 2.1 collective-permute-start.3
  62.4 88.1 %collective-permute-done.refs_2_ = f32[128,4096]{1,0:T(8,128)S(1)} collective-permute-done((f32[128,4096]{1,0:T(8,128)}, f32[128,4096]{1,0:T(8,128)S(1)}, u32[]{:S(2)}, u32[]{:S(2)}) %collective-permute-start) | collective-permute-done | bytes 2097184 | tf_op jit(solution)/shard_map/ppermute | solution.py:338
  153.4 8.6 %ratio_near.1.refs_2_.refs_1_ = f32[128,4096]{1,0:T(8,128)S(1)} custom-call(s32[1]{0:T(128)} %bitcast.1.refs_0_, f32[512,4096]{1,0:T(8,128)} %get-tuple-element.30.refs_1_.refs_8_.refs_7_, f32[128,4096]{1,0:T(8,128)S(1)} %copy-done.4, f32[1,3,128,128]{3,2,1,0:T(8,128)S(1)} %get-tuple-element.34.refs_3_.refs_4_, ...), custom_call_target="tpu_custom_call" | custom-call | flops 44040192 | bytes 327680 | tf_op jit(solution)/shard_map/ratio_near/pallas_call | solution.py:213
  162.1 2.4 collective-permute-start.2
  167.3 13.0 %ratio_inner.1.refs_4_.refs_2_ = f32[256,4096]{1,0:T(8,128)S(1)} custom-call(s32[1]{0:T(128)} %bitcast.1.refs_0_, f32[512,4096]{1,0:T(8,128)} %get-tuple-element.30.refs_1_.refs_8_.refs_7_, f32[2,3,128,128]{3,2,1,0:T(8,128)S(1)} %constant_dynamic-slice_fusion.1.refs_2_, bf16[16,256,512]{2,1,0:T(8,128)(2,1)} %get-tuple-element.31.refs_4_.refs_3_.refs_6_.refs_5_, ...), custom_call_target="tpu_custom_call" | custom-call | flops 100663296 | bytes 458752 | tf_op jit(solution)/shard_map/ratio_inner/pallas_call | solution.py:213
  180.3 2.0 copy-done
  183.4 16.2 %logs_most.1 = (f32[384,1024]{1,0:T(8,128)}, f32[384,1024]{1,0:T(8,128)}, f32[384,1024]{1,0:T(8,128)}, f32[384,1024]{1,0:T(8,128)}, f32[384,4096]{1,0:T(8,128)}) custom-call(s32[1]{0:T(128)} %bitcast.1.refs_0_, f32[128,4096]{1,0:T(8,128)} %ratio_cross.1.refs_1_, f32[128,4096]{1,0:T(8,128)} %copy-done.1, f32[128,4096]{1,0:T(8,128)} %collective-permute-done.3.refs_3_, ...), custom_call_target="tpu_custom_call" | custom-call | flops 169869312 | bytes 589824 | tf_op jit(solution)/shard_map/logs_most/pallas_call | solution.py:213
  200.7 2.7 collective-permute-done.4.refs_4_
  203.4 2.2 collective-permute-done.5.refs_5_
  205.7 2.2 collective-permute-done.6.refs_6_
  207.9 2.2 collective-permute-done.7.refs_7_
  210.2 17.0 %raw_most.1 = (f32[512,4096]{1,0:T(8,128)}, f32[512,32,128]{2,1,0:T(8,128)}, f32[1]{0:T(128)}) custom-call(s32[1]{0:T(128)} %bitcast.4.start_ref, f32[384,1024]{1,0:T(8,128)} %get-tuple-element.36.refs_0_, f32[384,1024]{1,0:T(8,128)} %get-tuple-element.37.refs_1_, f32[384,1024]{1,0:T(8,128)} %get-tuple-element.38.refs_2_, ...), custom_call_target="tpu_custom_call" | custom-call | flops 98304 | bytes 393216 | tf_op jit(solution)/shard_map/raw_most/pallas_call | solution.py:265
  227.2 11.0 %logs_near.1 = (f32[128,1024]{1,0:T(8,128)S(1)}, f32[128,1024]{1,0:T(8,128)S(1)}, f32[128,1024]{1,0:T(8,128)S(1)}, f32[128,1024]{1,0:T(8,128)S(1)}, f32[128,4096]{1,0:T(8,128)S(1)}) custom-call(s32[1]{0:T(128)} %bitcast.1.refs_0_, f32[128,4096]{1,0:T(8,128)} %copy-done.1, f32[256,4096]{1,0:T(8,128)} %copy-done, f32[128,4096]{1,0:T(8,128)} %collective-permute-done.2.refs_3_, ...), custom_call_target="tpu_custom_call" | custom-call | flops 44040192 | bytes 327680 | tf_op jit(solution)/shard_map/logs_near/pallas_call | solution.py:213
  243.8 6.1 %raw_near.1 = (f32[512,4096]{1,0:T(8,128)}, f32[512,32,128]{2,1,0:T(8,128)}, f32[1]{0:T(128)}) custom-call(s32[1]{0:T(128)} %bitcast.start_ref, f32[128,1024]{1,0:T(8,128)S(1)} %get-tuple-element.45.refs_0_, f32[128,1024]{1,0:T(8,128)S(1)} %get-tuple-element.46.refs_1_, ...), custom_call_target="tpu_custom_call", output_to_operand_aliasing={{0}: (10, {}), {1}: (11, {})} | custom-call | flops 32768 | bytes 131072 | tf_op jit(solution)/shard_map/raw_near/pallas_call | solution.py:265
  249.9 21.3 %psum.7 = f32[1]{0:T(128)} all-reduce(f32[1]{0:T(128)} %get-tuple-element.55), channel_id=1, replica_groups=mesh['parts'=2,'space'=8,'member'=2] {'space'}, use_global_device_ids=true, to_apply=%region_1.2 | all-reduce | flops 1 | bytes 8 | tf_op jit(solution)/shard_map/psum | solution.py:395
  271.9 13.7 %outputs.1 = (f32[512,4096]{1,0:T(8,128)}, f32[512,32,128]{2,1,0:T(8,128)}) custom-call(f32[512,4096]{1,0:T(8,128)} %get-tuple-element.53.raw_ref, f32[512,32,128]{2,1,0:T(8,128)} %get-tuple-element.54.quotient_ref, f32[1]{0:T(128)S(6)} %div.24.scale_ref), custom_call_target="tpu_custom_call" | custom-call | tf_op jit(solution)/shard_map/outputs/pallas_call | solution.py:300
  (32 shorter events, 14.5 us)
Async XLA Ops:
  9.6 39.5 %collective-permute-start.1 = (f32[128,4096]{1,0:T(8,128)}, f32[128,4096]{1,0:T(8,128)}, u32[]{:S(2)}, u32[]{:S(2)}) collective-permute-start(f32[128,4096]{1,0:T(8,128)} %bitcast.10), channel_id=1, source_target_pairs={{2,4},{6,8},{10,12},{4,2},{8,6},{12,10},{3,5},{7,9},{11,13},{5,3},... | collective-permute-start | bytes 6291464 | tf_op jit(solution)/shard_map/ppermute | solution.py:337
  15.1 135.4 %collective-permute-start = (f32[128,4096]{1,0:T(8,128)}, f32[128,4096]{1,0:T(8,128)S(1)}, u32[]{:S(2)}, u32[]{:S(2)}) collective-permute-start(f32[128,4096]{1,0:T(8,128)} %bitcast.11), channel_id=1, source_target_pairs={{0,2},{4,6},{8,10},{12,14},{2,0},{6,4},{10,8},{14,12},{1,3},{5,7},... | collective-permute-start | bytes 6291464 | tf_op jit(solution)/shard_map/ppermute | solution.py:338
  60.2 123.2 %collective-permute-start.3 = (f32[128,4096]{1,0:T(8,128)}, f32[128,4096]{1,0:T(8,128)}, u32[]{:S(2)}, u32[]{:S(2)}) collective-permute-start(f32[128,4096]{1,0:T(8,128)} %ratio_cross.1.refs_1_), channel_id=1, source_target_pairs={{2,4},{6,8},{10,12},{4,2},{8,6},{12,10},{3,5},{7,9},{11,13},{5,3},... | collective-permute-start | bytes 6291464 | tf_op jit(solution)/shard_map/ppermute | solution.py:370
  150.5 1.3 copy-start.3
  151.8 1.6 copy-start.4
  153.4 11.1 %copy-start.5 = (f32[2]{0:T(128)S(1)}, f32[2]{0:T(128)}, u32[]{:S(2)}) copy-start(f32[2]{0:T(128)} %param.6) | copy-start | bytes 28
  162.0 18.3 %copy-start.1 = (f32[128,4096]{1,0:T(8,128)}, f32[128,4096]{1,0:T(8,128)S(1)}, u32[]{:S(2)}) copy-start(f32[128,4096]{1,0:T(8,128)S(1)} %ratio_near.1.refs_2_.refs_1_) | copy-start | bytes 6291460
  162.1 65.1 %collective-permute-start.2 = (f32[128,4096]{1,0:T(8,128)S(1)}, f32[128,4096]{1,0:T(8,128)}, u32[]{:S(2)}, u32[]{:S(2)}) collective-permute-start(f32[128,4096]{1,0:T(8,128)S(1)} %ratio_near.1.refs_2_.refs_1_), channel_id=1, source_target_pairs={{0,2},{4,6},{8,10},{12,14},{2,0},{6,4},{10,8},{14,12},{1,3},{5,7},... | collective-permute-start | bytes 6291464 | tf_op jit(solution)/shard_map/ppermute | solution.py:370
  180.3 2.0 copy-start
  199.6 3.8 %collective-permute-start.4 = (f32[384,1024]{1,0:T(8,128)}, f32[384,1024]{1,0:T(8,128)}, u32[]{:S(2)}, u32[]{:S(2)}) collective-permute-start(f32[384,1024]{1,0:T(8,128)} %get-tuple-element.36.refs_0_), channel_id=1, source_target_pairs={{0,1},{1,0},{2,3},{3,2},{4,5},{5,4},{6,7},{7,6},{8,9},{9,8},{10,11... | collective-permute-start | bytes 4718600 | tf_op jit(solution)/shard_map/ppermute | solution.py:286
  199.7 6.0 %collective-permute-start.5 = (f32[384,1024]{1,0:T(8,128)}, f32[384,1024]{1,0:T(8,128)}, u32[]{:S(2)}, u32[]{:S(2)}) collective-permute-start(f32[384,1024]{1,0:T(8,128)} %get-tuple-element.37.refs_1_), channel_id=1, source_target_pairs={{0,1},{1,0},{2,3},{3,2},{4,5},{5,4},{6,7},{7,6},{8,9},{9,8},{10,11... | collective-permute-start | bytes 4718600 | tf_op jit(solution)/shard_map/ppermute | solution.py:286
  200.2 7.7 %collective-permute-start.6 = (f32[384,1024]{1,0:T(8,128)}, f32[384,1024]{1,0:T(8,128)}, u32[]{:S(2)}, u32[]{:S(2)}) collective-permute-start(f32[384,1024]{1,0:T(8,128)} %get-tuple-element.38.refs_2_), channel_id=1, source_target_pairs={{0,1},{1,0},{2,3},{3,2},{4,5},{5,4},{6,7},{7,6},{8,9},{9,8},{10,11... | collective-permute-start | bytes 4718600 | tf_op jit(solution)/shard_map/ppermute | solution.py:286
  200.3 9.9 %collective-permute-start.7 = (f32[384,1024]{1,0:T(8,128)}, f32[384,1024]{1,0:T(8,128)}, u32[]{:S(2)}, u32[]{:S(2)}) collective-permute-start(f32[384,1024]{1,0:T(8,128)} %get-tuple-element.39.refs_3_), channel_id=1, source_target_pairs={{0,1},{1,0},{2,3},{3,2},{4,5},{5,4},{6,7},{7,6},{8,9},{9,8},{10,11... | collective-permute-start | bytes 4718600 | tf_op jit(solution)/shard_map/ppermute | solution.py:286
  238.2 1.3 copy-start.2
  239.6 1.9 collective-permute-start.10
  239.7 3.3 %collective-permute-start.11 = (f32[128,1024]{1,0:T(8,128)S(1)}, f32[128,1024]{1,0:T(8,128)S(1)}, u32[]{:S(2)}, u32[]{:S(2)}) collective-permute-start(f32[128,1024]{1,0:T(8,128)S(1)} %get-tuple-element.48.refs_3_), channel_id=1, source_target_pairs={{0,1},{1,0},{2,3},{3,2},{4,5},{5,4},{6,7},{7,6},{8,9},{9,8},{10,11... | collective-permute-start | bytes 1572872 | tf_op jit(solution)/shard_map/ppermute | solution.py:286
  240.1 3.0 %collective-permute-start.8 = (f32[128,1024]{1,0:T(8,128)S(1)}, f32[128,1024]{1,0:T(8,128)}, u32[]{:S(2)}, u32[]{:S(2)}) collective-permute-start(f32[128,1024]{1,0:T(8,128)S(1)} %get-tuple-element.45.refs_0_), channel_id=1, source_target_pairs={{0,1},{1,0},{2,3},{3,2},{4,5},{5,4},{6,7},{7,6},{8,9},{9,8},{10,11... | collective-permute-start | bytes 1572872 | tf_op jit(solution)/shard_map/ppermute | solution.py:286
  240.2 3.7 %collective-permute-start.9 = (f32[128,1024]{1,0:T(8,128)S(1)}, f32[128,1024]{1,0:T(8,128)}, u32[]{:S(2)}, u32[]{:S(2)}) collective-permute-start(f32[128,1024]{1,0:T(8,128)S(1)} %get-tuple-element.46.refs_1_), channel_id=1, source_target_pairs={{0,1},{1,0},{2,3},{3,2},{4,5},{5,4},{6,7},{7,6},{8,9},{9,8},{10,11... | collective-permute-start | bytes 1572872 | tf_op jit(solution)/shard_map/ppermute | solution.py:286

commit v3 on v2

--- a/solution.py
+++ b/solution.py
@@ -9,7 +9,6 @@
 
 F32 = jnp.float32
 BF16 = jnp.bfloat16
-VMEM_LIMIT = 48 * 1024 * 1024
 GROUPS = 4
 ANY = pl.BlockSpec(memory_space=pl.ANY)
 INVMEM = pl.BlockSpec(memory_space=pltpu.VMEM)
@@ -26,8 +25,12 @@
     return one(a[0], b[0]) + (one(a[0], b[1]) + one(a[1], b[0]))
 
 
-def params():
-    return pltpu.CompilerParams(vmem_limit_bytes=VMEM_LIMIT)
+def params(mebibytes):
+    return pltpu.CompilerParams(vmem_limit_bytes=mebibytes * 1024 * 1024)
+
+
+def hbm(*arrays):
+    return [pltpu.with_memory_space_constraint(a, pltpu.HBM) for a in arrays]
 
 
 def pick(choice, side):
@@ -36,28 +39,25 @@
     return choice
 
 
-def flatten_kernel(*refs):
-    half = len(refs) // 2
-    for src, dst in zip(refs[:half], refs[half:]):
-        width = src.shape[2]
-        for b in range(src.shape[1]):
-            dst[:, b * width : (b + 1) * width] = src[:, b, :]
-
-
-def flatten(arrays, width):
-    rows, _, columns = arrays[0].shape
-    tile = 64
-    deep = pl.BlockSpec((tile, columns // width, width), lambda i: (i, 0, 0))
-    flat = pl.BlockSpec((tile, columns), lambda i: (i, 0))
+def cut_kernel(first, side_ref, src, dst, sem):
+    copy = pltpu.make_async_copy(src.at[pl.ds(pick(first, side_ref[0]), dst.shape[0])], dst, sem)
+    copy.start()
+    copy.wait()
+
+
+def cut(name, side, array, first, rows):
     return pl.pallas_call(
-        flatten_kernel,
-        grid=(rows // tile,),
-        in_specs=[deep] * len(arrays),
-        out_specs=[flat] * len(arrays),
-        out_shape=[jax.ShapeDtypeStruct((rows, columns), F32)] * len(arrays),
-        compiler_params=params(),
-        name="flatten",
-    )(*[a.reshape(rows, columns // width, width) for a in arrays])
+        functools.partial(cut_kernel, first),
+        in_specs=[INSMEM, ANY],
+        out_specs=ANY,
+        out_shape=pltpu.HBM((rows,) + array.shape[1:], F32),
+        scratch_shapes=[pltpu.SemaphoreType.DMA],
+        name=name,
+    )(side, *hbm(array))
+
+
+def area(ref, row, rows, columns):
+    return ref.at[pl.ds(row, rows), 0, columns] if len(ref.shape) == 3 else ref.at[pl.ds(row, rows), columns]
 
 
 def weight_kernel(nblocks, band_ref, high_ref, low_ref):
@@ -80,7 +80,7 @@
 
 def row_weights(band):
     nblocks, _, width, _ = band.shape
-    shape = jax.ShapeDtypeStruct((nblocks // 2, 2 * width, 4 * width), BF16)
+    shape = pltpu.HBM((nblocks // 2, 2 * width, 4 * width), BF16)
     out_spec = pl.BlockSpec((1, 2 * width, 4 * width), lambda t: (t, 0, 0))
     return pl.pallas_call(
         functools.partial(weight_kernel, nblocks),
@@ -89,7 +89,7 @@
         out_specs=(out_spec, out_spec),
         out_shape=(shape, shape),
         name="row_weights",
-    )(band)
+    )(*hbm(band))
 
 
 def blur_kernel(plan, *refs):
@@ -116,7 +116,7 @@
         inside.append(
             [
                 pltpu.make_async_copy(
-                    arrays[which].at[pl.ds(pick(row, side), rows), at],
+                    area(arrays[which], pick(row, side), rows, at),
                     field.at[pl.ds(pick(to, side), rows), at],
                     in_sems.at[g, k],
                 )
@@ -129,7 +129,7 @@
                 pltpu.make_async_copy(high_ref.at[some], whigh.at[some], late_sems.at[g, 0]),
                 pltpu.make_async_copy(low_ref.at[some], wlow.at[some], late_sems.at[g, 1]),
                 pltpu.make_async_copy(
-                    extra_ref.at[pl.ds(pick(extra, side), other.shape[0]), at], other.at[:, at], late_sems.at[g, 2]
+                    area(extra_ref, pick(extra, side), other.shape[0], at), other.at[:, at], late_sems.at[g, 2]
                 ),
             ]
         )
@@ -198,18 +198,20 @@
         copy.wait()
 
 
-def blur(name, side, arrays, pieces, bands, weights, other, extra, share=None):
+def blur(name, side, arrays, pieces, bands, weights, other, extra, share=None, pin=True):
     nout, _, width, _ = bands.shape
     npairs = weights[0].shape[0]
     columns = npairs * 2 * width
     rows, depth = nout * width, (nout + 2) * width
     final = share is not None
     nouts = 2 if final else 1
-    shapes = [jax.ShapeDtypeStruct((rows, columns // GROUPS), F32)] * (GROUPS if final else 0)
-    shapes.append(jax.ShapeDtypeStruct((rows, columns), F32))
+    kind = pltpu.HBM if pin else jax.ShapeDtypeStruct
+    shapes = [kind((rows, columns // GROUPS), F32)] * (GROUPS if final else 0)
+    shapes.append(kind((rows, columns), F32))
     plan = (tuple(pieces), len(arrays), extra, final)
     work = 3 * 2 * rows * columns * (depth + 4 * width)
     moved = 4 * (depth + 3 * rows) * columns + npairs * 2 * 2 * 8 * width * width
+    size = 4 * columns * (depth + (1 + nouts) * rows) + 4 * rows * columns + npairs * 2 * 2 * 8 * width * width
     result = pl.pallas_call(
         functools.partial(blur_kernel, plan),
         in_specs=[INSMEM] + [ANY] * len(arrays) + [INVMEM, ANY, ANY, ANY] + [INSMEM] * final,
@@ -231,37 +233,51 @@
             pltpu.SemaphoreType.DMA((GROUPS, 3)),
             pltpu.SemaphoreType.DMA((GROUPS, nouts)),
         ],
-        compiler_params=params(),
+        compiler_params=params(size // 2**20 + 6),
         cost_estimate=pl.CostEstimate(flops=work // 64, bytes_accessed=moved // 64, transcendentals=0),
         name=name,
-    )(side, *arrays, bands, *weights, other, *([share] if final else []))
+    )(side, *arrays, bands, *hbm(*weights, other), *([share] if final else []))
     return (result[:-1], result[-1]) if final else result[0]
 
 
 def raw_kernel(fresh, start_ref, *refs):
     own, peer, m_ref = refs[:GROUPS], refs[GROUPS : 2 * GROUPS], refs[2 * GROUPS]
-    raw_ref, quotient_ref, mass_ref = refs[-3:]
-    width = quotient_ref.shape[2]
+    raw_ref, quotient_ref, mass_ref, quotient, sems = refs[-5:]
+    tile = raw_ref.shape[0]
+    at = pl.program_id(0)
+    slot = lax.rem(at, 2)
+
+    def copy(step, slot):
+        row = pl.multiple_of((start_ref[0] + step) * tile, tile)
+        return pltpu.make_async_copy(quotient.at[slot], area(quotient_ref, row, tile, slice(None)), sems.at[slot])
+
+    @pl.when(at >= 2)
+    def _():
+        copy(at - 2, slot).wait()
+
     mass = 0.0
     for g in range(GROUPS):
         raw = jnp.exp(own[g][...] + peer[g][...])
         step = raw.shape[1]
         raw_ref[:, g * step : (g + 1) * step] = raw
         mass += jnp.sum(raw)
-        quotient = raw / m_ref[:, g * step : (g + 1) * step]
-        for b in range(step // width):
-            quotient_ref[:, g * (step // width) + b, :] = quotient[:, b * width : (b + 1) * width]
+        quotient[slot, :, g * step : (g + 1) * step] = raw / m_ref[:, g * step : (g + 1) * step]
     before = 0.0 if fresh else refs[2 * GROUPS + 3][0]
-    mass_ref[0] = mass + jnp.where(pl.program_id(0) == 0, before, mass_ref[0])
-
-
-def raw_rows(name, row, t, swap, m, choose, rows_here, width, so_far):
+    mass_ref[0] = mass + jnp.where(at == 0, before, mass_ref[0])
+    copy(at, slot).start()
+
+    @pl.when(at == pl.num_programs(0) - 1)
+    def _():
+        copy(at - 1, 1 - slot).wait()
+        copy(at, slot).wait()
+
+
+def raw_rows(name, row, t, peers, m, choose, rows_here, so_far):
     fresh = so_far is None
     rows, columns = m.shape
     tile = 32
     part = pl.BlockSpec((tile, columns), lambda i, at: (i, 0))
     group = pl.BlockSpec((tile, columns // GROUPS), lambda i, at: (i, 0))
-    deep = columns // width
     return pl.pallas_call(
         functools.partial(raw_kernel, fresh),
         grid_spec=pltpu.PrefetchScalarGridSpec(
@@ -270,20 +286,21 @@
             in_specs=[group] * (2 * GROUPS) + [part] + ([] if fresh else [ANY, ANY, INSMEM]),
             out_specs=(
                 pl.BlockSpec((tile, columns), lambda i, at: (at[0] + i, 0)),
-                pl.BlockSpec((tile, deep, width), lambda i, at: (at[0] + i, 0, 0)),
+                ANY,
                 INSMEM,
             ),
+            scratch_shapes=[pltpu.VMEM((2, tile, columns), F32), pltpu.SemaphoreType.DMA((2,))],
         ),
         out_shape=(
-            jax.ShapeDtypeStruct((rows_here, columns), F32),
-            jax.ShapeDtypeStruct((rows_here, deep, width), F32),
+            pltpu.HBM((rows_here, columns), F32),
+            pltpu.HBM((rows_here, 1, columns), F32),
             jax.ShapeDtypeStruct((1,), F32),
         ),
         input_output_aliases={} if fresh else {2 * GROUPS + 2: 0, 2 * GROUPS + 3: 1},
-        compiler_params=params(),
+        compiler_params=params(16),
         cost_estimate=pl.CostEstimate(flops=m.size // 16, bytes_accessed=m.size // 4, transcendentals=0),
         name=name,
-    )(choose([r // tile for r in row]).reshape(1), *t, *[swap(part) for part in t], m, *([] if fresh else so_far))
+    )(choose([r // tile for r in row]).reshape(1), *t, *peers, m, *([] if fresh else hbm(*so_far[:2]) + [so_far[2]]))
 
 
 def output_kernel(raw_ref, quotient_ref, scale_ref, barycenter_ref, scaling_ref):
@@ -303,9 +320,9 @@
         in_specs=[flat, deep, INSMEM],
         out_specs=(flat, deep),
         out_shape=(jax.ShapeDtypeStruct(raw.shape, F32), jax.ShapeDtypeStruct(quotient.shape, F32)),
-        compiler_params=params(),
+        compiler_params=params(16),
         name="outputs",
-    )(raw, quotient, scale)
+    )(*hbm(raw, quotient), scale)
 
 
 def local(densities, scaling, weights, band):
@@ -331,69 +348,66 @@
     def choose(choice):
         return jnp.where(odd == 0, choice[0], choice[1]).astype(jnp.int32)
 
-    def rows_of(choice):
-        return lax.dynamic_slice_in_dim(scaling, choose(choice), width, 0).reshape(width, cols_all)
-
-    cross1 = cross(rows_of(cross_row))
-    near1 = near(rows_of(near_row))
+    cross1 = cross(cut("cut_cross", side, scaling, cross_row, width))
+    near1 = near(cut("cut_near", side, scaling, near_row, width))
 
     shares = weights / jnp.sum(weights)
     share = lax.dynamic_slice_in_dim(shares, lax.axis_index("member"), 1)
-    own, dens = flatten([scaling, densities], width)
     wts = row_weights(band)
     mine = place * nlocal
     band_at = lambda row, blocks: lax.dynamic_slice_in_dim(band, mine + row // width, blocks, 0)
 
-    if nlocal > 1:
-        two = rows_here - 2 * width
-        cross_pieces = [(0, (0, two), 2 * width, (width, 0)), (1, 0, width, (0, 2 * width))]
-        near_pieces = [(0, (two, 0), 2 * width, (0, width)), (1, 0, width, (2 * width, 0))]
-        edges = [("cross", cross_row, cross_pieces, cross), ("near", near_row, near_pieces, near)]
-        halos1 = [[cross1], [near1]]
-    else:
-        pieces = [(0, 0, width, width), (1, 0, width, (0, 2 * width)), (2, 0, width, (2 * width, 0))]
-        edges = [("only", (0, 0), pieces, None)]
-        halos1 = [[cross1, near1]]
-    edge_bands = [band_at(choose(row), 1) for _, row, _, _ in edges]
-
     if inner > 0:
         inner_bands = band_at(width, inner)
         ratio_inner = blur(
-            "ratio_inner", side, [own], [(0, 0, rows_here, 0)], inner_bands, wts, dens, width
+            "ratio_inner", side, hbm(scaling), [(0, 0, rows_here, 0)], inner_bands, wts, densities, width
         )
-    ratios, halos2 = [], []
-    for (name, row, pieces, send), halo, bands in zip(edges, halos1, edge_bands):
-        if ratios:
-            bands, ratios[-1] = lax.optimization_barrier((bands, ratios[-1]))
-        ratio = blur("ratio_" + name, side, [own] + halo, pieces, bands, wts, dens, row)
-        ratios.append(ratio)
-        halos2.append([cross(ratio), near(ratio)] if send is None else [send(ratio)])
-
-    def finish(name, arrays, pieces, bands, row, share, state):
-        t, m = blur("logs_" + name, side, arrays, pieces, bands, wts, own, row, share)
-        return raw_rows("raw_" + name, row, t, swap, m, choose, rows_here, width, state)
-
+        cross1, ratio_inner = lax.optimization_barrier((cross1, ratio_inner))
     if nlocal == 1:
-        state = finish("only", ratios + halos2[0], pieces, edge_bands[0], (0, 0), share, None)
+        pieces = [(0, 0, width, width), (1, 0, width, (0, 2 * width)), (2, 0, width, (2 * width, 0))]
+        bands = band_at(0, 1)
+        ratio = blur("ratio_only", side, [scaling, cross1, near1], pieces, bands, wts, densities, 0)
+        cross2, near2 = cross(ratio), near(ratio)
+    else:
+        two = rows_here - 2 * width
+        pieces = [(0, (0, two), 2 * width, (width, 0)), (1, 0, width, (0, 2 * width))]
+        bands = band_at(choose(cross_row), 1)
+        ratio_cross = blur("ratio_cross", side, hbm(scaling) + [cross1], pieces, bands, wts, densities, cross_row)
+        ratio_cross, near1 = lax.optimization_barrier((ratio_cross, near1))
+        cross2 = cross(ratio_cross)
+        pieces = [(0, (two, 0), 2 * width, (0, width)), (1, 0, width, (2 * width, 0))]
+        bands = band_at(choose(near_row), 1)
+        ratio_near = blur("ratio_near", side, hbm(scaling) + [near1], pieces, bands, wts, densities, near_row)
+        near2 = near(ratio_near)
+
+    def finish(name, arrays, pieces, bands, row, share, state, pin=True):
+        t, m = blur("logs_" + name, side, arrays, pieces, bands, wts, scaling, row, share, pin)
+        keep = hbm if pin else lambda *a: list(a)
+        return raw_rows(
+            "raw_" + name, row, keep(*t), [swap(part) for part in t], *keep(m), choose, rows_here, state
+        )
+
+    if nlocal == 1:
+        pieces = [(0, 0, width, width), (1, 0, width, (0, 2 * width)), (2, 0, width, (2 * width, 0))]
+        state = finish("only", [ratio, cross2, near2], pieces, bands, (0, 0), share, None)
     else:
         most, end = rows_here - width, rows_here
         pieces = [(0, 0, width, (width, most)), (1, 0, width, (end, 0)), (2, 0, width, (0, end))]
+        arrays = [ratio_cross, ratio_near, cross2]
+        beside, beside_row = ratio_cross, 0
         if inner > 0:
             pieces.append((3, 0, inner * width, (2 * width, width)))
-        arrays = ratios + halos2[0] + ([ratio_inner] if inner > 0 else [])
+            arrays.append(ratio_inner)
+            beside, beside_row = ratio_inner, ((inner - 1) * width, 0)
         row = (0, width)
-        state = finish("most", arrays, pieces, band_at(choose(row), nlocal - 1), row, share, None)
+        state = finish("most", hbm(*arrays[:2]) + arrays[2:3] + hbm(*arrays[3:]), pieces, band_at(choose(row), nlocal - 1), row, share, None)
         share, state = lax.optimization_barrier((share, state))
-        if inner > 0:
-            beside = (ratio_inner, ((inner - 1) * width, 0))
-        else:
-            beside = (ratios[0], 0)
-        pieces = [(0, 0, width, width), (1, beside[1], width, (0, 2 * width)), (2, 0, width, (2 * width, 0))]
-        state = finish("near", [ratios[1], beside[0]] + halos2[1], pieces, edge_bands[1], near_row, share, state)
+        pieces = [(0, 0, width, width), (1, beside_row, width, (0, 2 * width)), (2, 0, width, (2 * width, 0))]
+        state = finish("near", hbm(ratio_near, beside) + [near2], pieces, bands, near_row, share, state, False)
 
     raw, quotient, mass = state
     mass = lax.psum(mass, "space")
-    barycenter, new_scaling = outputs(raw, quotient, float(cols_all * cols_all) / mass)
+    barycenter, new_scaling = outputs(raw, quotient.reshape(rows_here, cols_all // width, width), float(cols_all * cols_all) / mass)
     return barycenter, new_scaling.reshape(rows_here, 1, cols_all)
 
 

time: 291 us -> 335 us (1.15); the launches traced: 286 us -> 334 us
  Pallas kernels: 125 us -> 232 us
  waiting for transfers between devices: 101 us -> 56.9 us
  local copies, waits for them, and re-layouts: 21.9 us -> 6.69 us
    pallas_call x1 -> x2, Pallas kernels: 16.9 us -> 129 us  [cut(): pl.pallas_call(functools.partial(cut_kernel, first), in_specs=[INSMEM, AN...]
    ppermute x12, waiting for transfers between devices: 101 us -> 56.9 us  [the longest x1 33 us: local(): near2 = near(ratio_near)]
    unnamed x14 -> x6, local copies, waits for them, and re-layouts: 12.2 us -> 2.91 us
    dynamic_slice x1 -> x0, local copies, waits for them, and re-layouts: 6.01 us -> none  [rows_of(): lax.dynamic_slice_in_dim(scaling, choose(choice), width, 0)]
    pallas_call x5, Pallas kernels: 60 us -> 56.5 us  [blur(): pl.pallas_call(functools.partial(blur_kernel, plan), in_specs=[INSMEM] +...]
  transfers between devices with their start and end apart: 12 -> 12, of which waited for: 9 -> 9; matrix products, arithmetic and copies ran while one was open for 3% -> 2% of each run, Pallas kernels for 33% -> 41%
where the time goes in v3:
time: 335 us; the launch traced here: 334 us
  Pallas kernels  232 us (69%)
  waiting for transfers between devices  56.9 us (17%)
  blocking collectives  21.2 us (6%)
  starting transfers between devices  13.9 us (4%)
  local copies, waits for them, and re-layouts  6.69 us (2%)
    pallas_call x2, Pallas kernels, cut(): pl.pallas_call(functools.partial(cut_kernel, first), in_specs=[INSMEM, AN...  129 us
    pallas_call x5, Pallas kernels, blur(): pl.pallas_call(functools.partial(blur_kernel, plan), in_specs=[INSMEM] +...  56.5 us
    ppermute x1, waiting for transfers between devices, local(): near2 = near(ratio_near)  33 us
    pallas_call x2, Pallas kernels, raw_rows(): pl.pallas_call(functools.partial(raw_kernel, fresh), grid_spec=pltpu.Pref...  21.4 us
    psum x1, blocking collectives, local(): mass = lax.psum(mass, 'space')  21.2 us
    pallas_call x1, Pallas kernels, outputs(): pl.pallas_call(output_kernel, grid=(rows // tile,), in_specs=[flat, deep,...  13.7 us
    ppermute x8, waiting for transfers between devices, finish(): swap(part)  12.6 us
    pallas_call x1, Pallas kernels, row_weights(): pl.pallas_call(functools.partial(weight_kernel, nblocks), grid=(nblocks /...  11.6 us
  transfers between devices with their start and end apart: 12, of which 9 were waited for; matrix products, arithmetic and copies ran while one was open for 2% of the time, Pallas kernels for 41%

profile of v3, /device:TPU:0, one launch (start us, length us, event | category | flops | bytes accessed | tf_op | source)
XLA Modules:
  0.0 333.9 jit_solution(8919708012544610658)
XLA Ops:
  0.6 64.6 %cut_cross.1 = f32[128,1,4096]{2,1,0:T(1,128)} custom-call(s32[1]{0:T(128)} %bitcast.1.side_ref.refs_0_, f32[512,1,4096]{2,1,0:T(1,128)} %refs_7_.1), custom_call_target="tpu_custom_call" | custom-call | tf_op jit(solution)/shard_map/cut_cross/pallas_call | solution.py:49
  65.3 2.0 collective-permute-start
  67.3 64.6 %cut_near.1 = f32[128,1,4096]{2,1,0:T(1,128)} custom-call(s32[1]{0:T(128)} %bitcast.1.side_ref.refs_0_, f32[512,1,4096]{2,1,0:T(1,128)} %refs_7_.1), custom_call_target="tpu_custom_call" | custom-call | tf_op jit(solution)/shard_map/cut_near/pallas_call | solution.py:49
  131.9 4.5 %collective-permute-start.1 = (f32[128,1,4096]{2,1,0:T(1,128)}, f32[128,1,4096]{2,1,0:T(1,128)S(1)}, u32[]{:S(2)}, u32[]{:S(2)}) collective-permute-start(f32[128,1,4096]{2,1,0:T(1,128)} %cut_near.1), channel_id=1, source_target_pairs={{0,2},{4,6},{8,10},{12,14},{2,0},{6,4},{10,8},{14,12},{1,3},{5,7},... | collective-permute-start | bytes 6291464 | tf_op jit(solution)/shard_map/ppermute | solution.py:352
  136.4 11.6 %row_weights.1 = (bf16[16,256,512]{2,1,0:T(8,128)(2,1)}, bf16[16,256,512]{2,1,0:T(8,128)(2,1)}) custom-call(f32[32,3,128,128]{3,2,1,0:T(8,128)} %band_ref.1), custom_call_target="tpu_custom_call" | custom-call | tf_op jit(solution)/shard_map/row_weights/pallas_call | solution.py:85
  149.0 11.0 %ratio_inner.1.refs_4_.refs_2_ = f32[256,4096]{1,0:T(8,128)} custom-call(s32[1]{0:T(128)} %bitcast.1.side_ref.refs_0_, f32[512,1,4096]{2,1,0:T(1,128)} %refs_7_.1, f32[2,3,128,128]{3,2,1,0:T(8,128)S(1)} %constant_dynamic-slice_fusion.3.refs_2_, bf16[16,256,512]{2,1,0:T(8,128)(2,1)} %get-tuple-element.30.refs_3_.refs_4_.refs_6_.refs_5_, ...), custom_call_target="tpu_custom_call" | custom-call | flops 100663296 | bytes 458752 | tf_op jit(solution)/shard_map/ratio_inner/pallas_call | solution.py:215
  161.1 9.6 %ratio_cross.1.refs_1_ = f32[128,4096]{1,0:T(8,128)} custom-call(s32[1]{0:T(128)} %bitcast.1.side_ref.refs_0_, f32[512,1,4096]{2,1,0:T(1,128)} %refs_7_.1, f32[128,1,4096]{2,1,0:T(1,128)} %collective-permute-done.refs_2_, f32[1,3,128,128]{3,2,1,0:T(8,128)S(1)} %get-tuple-element.61.refs_3_, ...), custom_call_target="tpu_custom_call" | custom-call | flops 44040192 | bytes 327680 | tf_op jit(solution)/shard_map/ratio_cross/pallas_call | solution.py:215
  170.7 11.2 %collective-permute-done.1.refs_2_ = f32[128,1,4096]{2,1,0:T(1,128)S(1)} collective-permute-done((f32[128,1,4096]{2,1,0:T(1,128)}, f32[128,1,4096]{2,1,0:T(1,128)S(1)}, u32[]{:S(2)}, u32[]{:S(2)}) %collective-permute-start.1) | collective-permute-done | bytes 2097184 | tf_op jit(solution)/shard_map/ppermute | solution.py:352
  182.0 2.0 collective-permute-start.3
  184.0 9.6 %ratio_near.1.refs_2_.refs_1_ = f32[128,4096]{1,0:T(8,128)} custom-call(s32[1]{0:T(128)} %bitcast.1.side_ref.refs_0_, f32[512,1,4096]{2,1,0:T(1,128)} %refs_7_.1, f32[128,1,4096]{2,1,0:T(1,128)S(1)} %collective-permute-done.1.refs_2_, f32[1,3,128,128]{3,2,1,0:T(8,128)S(1)} %get-tuple-element.60.refs_3_.refs_4_, ...), custom_call_target="tpu_custom_call" | custom-call | flops 44040192 | bytes 327680 | tf_op jit(solution)/shard_map/ratio_near/pallas_call | solution.py:215
  193.6 3.3 collective-permute-start.2
  199.9 16.1 %logs_most.1 = (f32[384,1024]{1,0:T(8,128)}, f32[384,1024]{1,0:T(8,128)}, f32[384,1024]{1,0:T(8,128)}, f32[384,1024]{1,0:T(8,128)}, f32[384,4096]{1,0:T(8,128)}) custom-call(s32[1]{0:T(128)} %bitcast.1.side_ref.refs_0_, f32[128,4096]{1,0:T(8,128)} %ratio_cross.1.refs_1_, f32[128,4096]{1,0:T(8,128)} %ratio_near.1.refs_2_.refs_1_, ...), custom_call_target="tpu_custom_call" | custom-call | flops 169869312 | bytes 589824 | tf_op jit(solution)/shard_map/logs_most/pallas_call | solution.py:215
  217.1 2.7 collective-permute-done.4.refs_4_
  219.9 2.2 collective-permute-done.5.refs_5_
  222.1 2.2 collective-permute-done.6.refs_6_
  224.4 2.2 collective-permute-done.7.refs_7_
  226.6 15.8 %raw_most.1 = (f32[512,4096]{1,0:T(8,128)}, f32[512,1,4096]{2,1,0:T(1,128)}, f32[1]{0:T(128)}) custom-call(s32[1]{0:T(128)} %bitcast.2.start_ref, f32[384,1024]{1,0:T(8,128)} %get-tuple-element.36.refs_0_, f32[384,1024]{1,0:T(8,128)} %get-tuple-element.37.refs_1_, f32[384,1024]{1,0:T(8,128)} %get-tuple-element.38.refs_2_, ...), custom_call_target="tpu_custom_call" | custom-call | flops 98304 | bytes 393216 | tf_op jit(solution)/shard_map/raw_most/pallas_call | solution.py:281
  242.4 33.0 %collective-permute-done.2.refs_3_ = f32[128,4096]{1,0:T(8,128)S(1)} collective-permute-done((f32[128,4096]{1,0:T(8,128)}, f32[128,4096]{1,0:T(8,128)S(1)}, u32[]{:S(2)}, u32[]{:S(2)}) %collective-permute-start.2) | collective-permute-done | bytes 2097184 | tf_op jit(solution)/shard_map/ppermute | solution.py:381
  275.4 10.1 %logs_near.1 = (f32[128,1024]{1,0:T(8,128)S(1)}, f32[128,1024]{1,0:T(8,128)S(1)}, f32[128,1024]{1,0:T(8,128)}, f32[128,1024]{1,0:T(8,128)}, f32[128,4096]{1,0:T(8,128)S(1)}) custom-call(s32[1]{0:T(128)} %bitcast.1.side_ref.refs_0_, f32[128,4096]{1,0:T(8,128)} %ratio_near.1.refs_2_.refs_1_, f32[256,4096]{1,0:T(8,128)} %ratio_inner.1.refs_4_.refs_2_, ...), custom_call_target="tpu_custom_call" | custom-call | flops 44040192 | bytes 327680 | tf_op jit(solution)/shard_map/logs_near/pallas_call | solution.py:215
  289.0 1.5 collective-permute-done.11.refs_7_
  291.1 1.6 copy-done.1
  292.7 5.7 %raw_near.1 = (f32[512,4096]{1,0:T(8,128)}, f32[512,1,4096]{2,1,0:T(1,128)}, f32[1]{0:T(128)}) custom-call(s32[1]{0:T(128)} %bitcast.start_ref, f32[128,1024]{1,0:T(8,128)S(1)} %get-tuple-element.45.refs_0_, f32[128,1024]{1,0:T(8,128)S(1)} %get-tuple-element.46.refs_1_, ...), custom_call_target="tpu_custom_call", output_to_operand_aliasing={{0}: (10, {}), {1}: (11, {})} | custom-call | flops 32768 | bytes 131072 | tf_op jit(solution)/shard_map/raw_near/pallas_call | solution.py:281
  298.3 21.2 %psum.7 = f32[1]{0:T(128)} all-reduce(f32[1]{0:T(128)} %get-tuple-element.55), channel_id=1, replica_groups=mesh['parts'=2,'space'=8,'member'=2] {'space'}, use_global_device_ids=true, to_apply=%region_1.2 | all-reduce | flops 1 | bytes 8 | tf_op jit(solution)/shard_map/psum | solution.py:409
  320.2 13.7 %outputs.1 = (f32[512,4096]{1,0:T(8,128)}, f32[512,32,128]{2,1,0:T(8,128)}) custom-call(f32[512,4096]{1,0:T(8,128)} %get-tuple-element.53.raw_ref, f32[512,32,128]{2,1,0:T(8,128)} %bitcast.5, f32[1]{0:T(128)S(6)} %div.24.scale_ref), custom_call_target="tpu_custom_call" | custom-call | tf_op jit(solution)/shard_map/outputs/pallas_call | solution.py:317
  (24 shorter events, 10.1 us)
Async XLA Ops:
  65.3 95.8 %collective-permute-start = (f32[128,1,4096]{2,1,0:T(1,128)}, f32[128,1,4096]{2,1,0:T(1,128)}, u32[]{:S(2)}, u32[]{:S(2)}) collective-permute-start(f32[128,1,4096]{2,1,0:T(1,128)} %cut_cross.1), channel_id=1, source_target_pairs={{2,4},{6,8},{10,12},{4,2},{8,6},{12,10},{3,5},{7,9},{11,13},{5,3},... | collective-permute-start | bytes 6291464 | tf_op jit(solution)/shard_map/ppermute | solution.py:351
  131.9 50.0 %collective-permute-start.1 = (f32[128,1,4096]{2,1,0:T(1,128)}, f32[128,1,4096]{2,1,0:T(1,128)S(1)}, u32[]{:S(2)}, u32[]{:S(2)}) collective-permute-start(f32[128,1,4096]{2,1,0:T(1,128)} %cut_near.1), channel_id=1, source_target_pairs={{0,2},{4,6},{8,10},{12,14},{2,0},{6,4},{10,8},{14,12},{1,3},{5,7},... | collective-permute-start | bytes 6291464 | tf_op jit(solution)/shard_map/ppermute | solution.py:352
  182.0 18.0 %collective-permute-start.3 = (f32[128,4096]{1,0:T(8,128)}, f32[128,4096]{1,0:T(8,128)}, u32[]{:S(2)}, u32[]{:S(2)}) collective-permute-start(f32[128,4096]{1,0:T(8,128)} %ratio_cross.1.refs_1_), channel_id=1, source_target_pairs={{2,4},{6,8},{10,12},{4,2},{8,6},{12,10},{3,5},{7,9},{11,13},{5,3},... | collective-permute-start | bytes 6291464 | tf_op jit(solution)/shard_map/ppermute | solution.py:377
  184.0 13.0 %copy-start.2 = (f32[2]{0:T(128)S(1)}, f32[2]{0:T(128)}, u32[]{:S(2)}) copy-start(f32[2]{0:T(128)} %param.6) | copy-start | bytes 28
  193.6 81.8 %collective-permute-start.2 = (f32[128,4096]{1,0:T(8,128)}, f32[128,4096]{1,0:T(8,128)S(1)}, u32[]{:S(2)}, u32[]{:S(2)}) collective-permute-start(f32[128,4096]{1,0:T(8,128)} %ratio_near.1.refs_2_.refs_1_), channel_id=1, source_target_pairs={{0,2},{4,6},{8,10},{12,14},{2,0},{6,4},{10,8},{14,12},{1,3},{5,7},... | collective-permute-start | bytes 6291464 | tf_op jit(solution)/shard_map/ppermute | solution.py:381
  216.0 3.8 %collective-permute-start.4 = (f32[384,1024]{1,0:T(8,128)}, f32[384,1024]{1,0:T(8,128)}, u32[]{:S(2)}, u32[]{:S(2)}) collective-permute-start(f32[384,1024]{1,0:T(8,128)} %get-tuple-element.36.refs_0_), channel_id=1, source_target_pairs={{0,1},{1,0},{2,3},{3,2},{4,5},{5,4},{6,7},{7,6},{8,9},{9,8},{10,11... | collective-permute-start | bytes 4718600 | tf_op jit(solution)/shard_map/ppermute | solution.py:387
  216.1 6.0 %collective-permute-start.5 = (f32[384,1024]{1,0:T(8,128)}, f32[384,1024]{1,0:T(8,128)}, u32[]{:S(2)}, u32[]{:S(2)}) collective-permute-start(f32[384,1024]{1,0:T(8,128)} %get-tuple-element.37.refs_1_), channel_id=1, source_target_pairs={{0,1},{1,0},{2,3},{3,2},{4,5},{5,4},{6,7},{7,6},{8,9},{9,8},{10,11... | collective-permute-start | bytes 4718600 | tf_op jit(solution)/shard_map/ppermute | solution.py:387
  216.6 7.7 %collective-permute-start.6 = (f32[384,1024]{1,0:T(8,128)}, f32[384,1024]{1,0:T(8,128)}, u32[]{:S(2)}, u32[]{:S(2)}) collective-permute-start(f32[384,1024]{1,0:T(8,128)} %get-tuple-element.38.refs_2_), channel_id=1, source_target_pairs={{0,1},{1,0},{2,3},{3,2},{4,5},{5,4},{6,7},{7,6},{8,9},{9,8},{10,11... | collective-permute-start | bytes 4718600 | tf_op jit(solution)/shard_map/ppermute | solution.py:387
  216.7 9.9 %collective-permute-start.7 = (f32[384,1024]{1,0:T(8,128)}, f32[384,1024]{1,0:T(8,128)}, u32[]{:S(2)}, u32[]{:S(2)}) collective-permute-start(f32[384,1024]{1,0:T(8,128)} %get-tuple-element.39.refs_3_), channel_id=1, source_target_pairs={{0,1},{1,0},{2,3},{3,2},{4,5},{5,4},{6,7},{7,6},{8,9},{9,8},{10,11... | collective-permute-start | bytes 4718600 | tf_op jit(solution)/shard_map/ppermute | solution.py:387
  285.6 1.3 copy-start
  286.9 2.1 collective-permute-start.10
  286.9 3.6 %collective-permute-start.11 = (f32[128,1024]{1,0:T(8,128)}, f32[128,1024]{1,0:T(8,128)S(1)}, u32[]{:S(2)}, u32[]{:S(2)}) collective-permute-start(f32[128,1024]{1,0:T(8,128)} %get-tuple-element.48.refs_3_), channel_id=1, source_target_pairs={{0,1},{1,0},{2,3},{3,2},{4,5},{5,4},{6,7},{7,6},{8,9},{9,8},{10,11... | collective-permute-start | bytes 1572872 | tf_op jit(solution)/shard_map/ppermute | solution.py:387
  287.4 3.1 collective-permute-start.8
  287.5 3.6 %collective-permute-start.9 = (f32[128,1024]{1,0:T(8,128)S(1)}, f32[128,1024]{1,0:T(8,128)S(1)}, u32[]{:S(2)}, u32[]{:S(2)}) collective-permute-start(f32[128,1024]{1,0:T(8,128)S(1)} %get-tuple-element.46.refs_1_), channel_id=1, source_target_pairs={{0,1},{1,0},{2,3},{3,2},{4,5},{5,4},{6,7},{7,6},{8,9},{9,8},{10,11... | collective-permute-start | bytes 1572872 | tf_op jit(solution)/shard_map/ppermute | solution.py:387
  291.1 1.6 copy-start.1

commit v4 on v3

--- a/solution.py
+++ b/solution.py
@@ -39,19 +39,33 @@
     return choice
 
 
-def cut_kernel(first, side_ref, src, dst, sem):
-    copy = pltpu.make_async_copy(src.at[pl.ds(pick(first, side_ref[0]), dst.shape[0])], dst, sem)
-    copy.start()
-    copy.wait()
+def cut_kernel(first, side_ref, src, dst, stage, sems):
+    rows = stage.shape[0] // GROUPS
+    start = pick(first, side_ref[0])
+    parts = [pl.ds(g * rows, rows) for g in range(GROUPS)]
+    inward = [
+        pltpu.make_async_copy(src.at[pl.ds(start + g * rows, rows)], stage.at[part], sems.at[0, g])
+        for g, part in enumerate(parts)
+    ]
+    outward = [pltpu.make_async_copy(stage.at[part], dst.at[part], sems.at[1, g]) for g, part in enumerate(parts)]
+    for copy in inward:
+        copy.start()
+    for g in range(GROUPS):
+        inward[g].wait()
+        outward[g].start()
+    for copy in outward:
+        copy.wait()
 
 
 def cut(name, side, array, first, rows):
+    shape = (rows,) + array.shape[1:]
     return pl.pallas_call(
         functools.partial(cut_kernel, first),
         in_specs=[INSMEM, ANY],
         out_specs=ANY,
-        out_shape=pltpu.HBM((rows,) + array.shape[1:], F32),
-        scratch_shapes=[pltpu.SemaphoreType.DMA],
+        out_shape=pltpu.HBM(shape, F32),
+        scratch_shapes=[pltpu.VMEM(shape, F32), pltpu.SemaphoreType.DMA((2, GROUPS))],
+        compiler_params=params(8),
         name=name,
     )(side, *hbm(array))
 

time: 335 us -> 254 us (0.76)
  Pallas kernels: 232 us -> 108 us
  waiting for transfers between devices: 56.9 us -> 99.6 us
    pallas_call x2, Pallas kernels: 129 us -> 4.86 us  [cut(): pl.pallas_call(functools.partial(cut_kernel, first), in_specs=[INSMEM, AN...]
    ppermute x1, waiting for transfers between devices: 11.2 us -> 52.7 us  [local(): near1 = near(cut('cut_near', side, scaling, near_row, width))]
  transfers between devices with their start and end apart: 12 -> 12, of which waited for: 9 -> 9; matrix products, arithmetic and copies ran while one was open for 2% -> 2% of each run, Pallas kernels for 41% -> 30%
where the time goes in v4:
time: 254 us; the launch traced here: 253 us
  Pallas kernels  108 us (43%)
  waiting for transfers between devices  99.6 us (39%)
  blocking collectives  21.3 us (8%)
  starting transfers between devices  14.6 us (6%)
  local copies, waits for them, and re-layouts  6.69 us (3%)
    pallas_call x5, Pallas kernels, blur(): pl.pallas_call(functools.partial(blur_kernel, plan), in_specs=[INSMEM] +...  56.5 us
    ppermute x1, waiting for transfers between devices, local(): near1 = near(cut('cut_near', side, scaling, near_row, width))  52.7 us
    ppermute x1, waiting for transfers between devices, local(): near2 = near(ratio_near)  34.3 us
    pallas_call x2, Pallas kernels, raw_rows(): pl.pallas_call(functools.partial(raw_kernel, fresh), grid_spec=pltpu.Pref...  21.4 us
    psum x1, blocking collectives, local(): mass = lax.psum(mass, 'space')  21.3 us
    pallas_call x1, Pallas kernels, outputs(): pl.pallas_call(output_kernel, grid=(rows // tile,), in_specs=[flat, deep,...  13.7 us
    ppermute x8, waiting for transfers between devices, finish(): swap(part)  12.6 us
    pallas_call x1, Pallas kernels, row_weights(): pl.pallas_call(functools.partial(weight_kernel, nblocks), grid=(nblocks /...  11.6 us
  transfers between devices with their start and end apart: 12, of which 9 were waited for; matrix products, arithmetic and copies ran while one was open for 2% of the time, Pallas kernels for 30%

profile of v4, /device:TPU:0, one launch (start us, length us, event | category | flops | bytes accessed | tf_op | source)
XLA Modules:
  0.0 253.0 jit_solution(15982817276296124364)
XLA Ops:
  0.6 2.4 cut_cross.1
  3.1 2.0 collective-permute-start
  5.1 2.4 cut_near.1
  7.5 4.5 %collective-permute-start.1 = (f32[128,1,4096]{2,1,0:T(1,128)}, f32[128,1,4096]{2,1,0:T(1,128)S(1)}, u32[]{:S(2)}, u32[]{:S(2)}) collective-permute-start(f32[128,1,4096]{2,1,0:T(1,128)} %cut_near.1), channel_id=1, source_target_pairs={{0,2},{4,6},{8,10},{12,14},{2,0},{6,4},{10,8},{14,12},{1,3},{5,7},... | collective-permute-start | bytes 6291464 | tf_op jit(solution)/shard_map/ppermute | solution.py:366
  12.0 11.6 %row_weights.1 = (bf16[16,256,512]{2,1,0:T(8,128)(2,1)}, bf16[16,256,512]{2,1,0:T(8,128)(2,1)}) custom-call(f32[32,3,128,128]{3,2,1,0:T(8,128)} %band_ref.1), custom_call_target="tpu_custom_call" | custom-call | tf_op jit(solution)/shard_map/row_weights/pallas_call | solution.py:99
  24.6 11.0 %ratio_inner.1.refs_4_.refs_2_ = f32[256,4096]{1,0:T(8,128)} custom-call(s32[1]{0:T(128)} %bitcast.1.side_ref.refs_0_, f32[512,1,4096]{2,1,0:T(1,128)} %refs_7_.1, f32[2,3,128,128]{3,2,1,0:T(8,128)S(1)} %constant_dynamic-slice_fusion.3.refs_2_, bf16[16,256,512]{2,1,0:T(8,128)(2,1)} %get-tuple-element.30.refs_3_.refs_4_.refs_6_.refs_5_, ...), custom_call_target="tpu_custom_call" | custom-call | flops 100663296 | bytes 458752 | tf_op jit(solution)/shard_map/ratio_inner/pallas_call | solution.py:229
  36.7 9.6 %ratio_cross.1.refs_1_ = f32[128,4096]{1,0:T(8,128)} custom-call(s32[1]{0:T(128)} %bitcast.1.side_ref.refs_0_, f32[512,1,4096]{2,1,0:T(1,128)} %refs_7_.1, f32[128,1,4096]{2,1,0:T(1,128)} %collective-permute-done.refs_2_, f32[1,3,128,128]{3,2,1,0:T(8,128)S(1)} %get-tuple-element.61.refs_3_, ...), custom_call_target="tpu_custom_call" | custom-call | flops 44040192 | bytes 327680 | tf_op jit(solution)/shard_map/ratio_cross/pallas_call | solution.py:229
  46.3 52.7 %collective-permute-done.1.refs_2_ = f32[128,1,4096]{2,1,0:T(1,128)S(1)} collective-permute-done((f32[128,1,4096]{2,1,0:T(1,128)}, f32[128,1,4096]{2,1,0:T(1,128)S(1)}, u32[]{:S(2)}, u32[]{:S(2)}) %collective-permute-start.1) | collective-permute-done | bytes 2097184 | tf_op jit(solution)/shard_map/ppermute | solution.py:366
  99.0 2.0 collective-permute-start.3
  101.0 9.7 %ratio_near.1.refs_2_.refs_1_ = f32[128,4096]{1,0:T(8,128)} custom-call(s32[1]{0:T(128)} %bitcast.1.side_ref.refs_0_, f32[512,1,4096]{2,1,0:T(1,128)} %refs_7_.1, f32[128,1,4096]{2,1,0:T(1,128)S(1)} %collective-permute-done.1.refs_2_, f32[1,3,128,128]{3,2,1,0:T(8,128)S(1)} %get-tuple-element.60.refs_3_.refs_4_, ...), custom_call_target="tpu_custom_call" | custom-call | flops 44040192 | bytes 327680 | tf_op jit(solution)/shard_map/ratio_near/pallas_call | solution.py:229
  110.6 4.1 %collective-permute-start.2 = (f32[128,4096]{1,0:T(8,128)}, f32[128,4096]{1,0:T(8,128)S(1)}, u32[]{:S(2)}, u32[]{:S(2)}) collective-permute-start(f32[128,4096]{1,0:T(8,128)} %ratio_near.1.refs_2_.refs_1_), channel_id=1, source_target_pairs={{0,2},{4,6},{8,10},{12,14},{2,0},{6,4},{10,8},{14,12},{1,3},{5,7},... | collective-permute-start | bytes 6291464 | tf_op jit(solution)/shard_map/ppermute | solution.py:395
  117.7 16.1 %logs_most.1 = (f32[384,1024]{1,0:T(8,128)}, f32[384,1024]{1,0:T(8,128)}, f32[384,1024]{1,0:T(8,128)}, f32[384,1024]{1,0:T(8,128)}, f32[384,4096]{1,0:T(8,128)}) custom-call(s32[1]{0:T(128)} %bitcast.1.side_ref.refs_0_, f32[128,4096]{1,0:T(8,128)} %ratio_cross.1.refs_1_, f32[128,4096]{1,0:T(8,128)} %ratio_near.1.refs_2_.refs_1_, ...), custom_call_target="tpu_custom_call" | custom-call | flops 169869312 | bytes 589824 | tf_op jit(solution)/shard_map/logs_most/pallas_call | solution.py:229
  134.9 2.7 %collective-permute-done.4.refs_4_ = f32[384,1024]{1,0:T(8,128)} collective-permute-done((f32[384,1024]{1,0:T(8,128)}, f32[384,1024]{1,0:T(8,128)}, u32[]{:S(2)}, u32[]{:S(2)}) %collective-permute-start.4) | collective-permute-done | bytes 1572896 | tf_op jit(solution)/shard_map/ppermute | solution.py:401
  137.6 2.2 collective-permute-done.5.refs_5_
  139.9 2.2 collective-permute-done.6.refs_6_
  142.1 2.2 collective-permute-done.7.refs_7_
  144.4 15.8 %raw_most.1 = (f32[512,4096]{1,0:T(8,128)}, f32[512,1,4096]{2,1,0:T(1,128)}, f32[1]{0:T(128)}) custom-call(s32[1]{0:T(128)} %bitcast.2.start_ref, f32[384,1024]{1,0:T(8,128)} %get-tuple-element.36.refs_0_, f32[384,1024]{1,0:T(8,128)} %get-tuple-element.37.refs_1_, f32[384,1024]{1,0:T(8,128)} %get-tuple-element.38.refs_2_, ...), custom_call_target="tpu_custom_call" | custom-call | flops 98304 | bytes 393216 | tf_op jit(solution)/shard_map/raw_most/pallas_call | solution.py:295
  160.2 34.3 %collective-permute-done.2.refs_3_ = f32[128,4096]{1,0:T(8,128)S(1)} collective-permute-done((f32[128,4096]{1,0:T(8,128)}, f32[128,4096]{1,0:T(8,128)S(1)}, u32[]{:S(2)}, u32[]{:S(2)}) %collective-permute-start.2) | collective-permute-done | bytes 2097184 | tf_op jit(solution)/shard_map/ppermute | solution.py:395
  194.5 10.1 %logs_near.1 = (f32[128,1024]{1,0:T(8,128)S(1)}, f32[128,1024]{1,0:T(8,128)S(1)}, f32[128,1024]{1,0:T(8,128)}, f32[128,1024]{1,0:T(8,128)}, f32[128,4096]{1,0:T(8,128)S(1)}) custom-call(s32[1]{0:T(128)} %bitcast.1.side_ref.refs_0_, f32[128,4096]{1,0:T(8,128)} %ratio_near.1.refs_2_.refs_1_, f32[256,4096]{1,0:T(8,128)} %ratio_inner.1.refs_4_.refs_2_, ...), custom_call_target="tpu_custom_call" | custom-call | flops 44040192 | bytes 327680 | tf_op jit(solution)/shard_map/logs_near/pallas_call | solution.py:229
  208.1 1.5 collective-permute-done.11.refs_7_
  210.1 1.6 copy-done.1
  211.7 5.7 %raw_near.1 = (f32[512,4096]{1,0:T(8,128)}, f32[512,1,4096]{2,1,0:T(1,128)}, f32[1]{0:T(128)}) custom-call(s32[1]{0:T(128)} %bitcast.start_ref, f32[128,1024]{1,0:T(8,128)S(1)} %get-tuple-element.45.refs_0_, f32[128,1024]{1,0:T(8,128)S(1)} %get-tuple-element.46.refs_1_, ...), custom_call_target="tpu_custom_call", output_to_operand_aliasing={{0}: (10, {}), {1}: (11, {})} | custom-call | flops 32768 | bytes 131072 | tf_op jit(solution)/shard_map/raw_near/pallas_call | solution.py:295
  217.4 21.3 %psum.7 = f32[1]{0:T(128)} all-reduce(f32[1]{0:T(128)} %get-tuple-element.55), channel_id=1, replica_groups=mesh['parts'=2,'space'=8,'member'=2] {'space'}, use_global_device_ids=true, to_apply=%region_1.2 | all-reduce | flops 1 | bytes 8 | tf_op jit(solution)/shard_map/psum | solution.py:423
  239.4 13.7 %outputs.1 = (f32[512,4096]{1,0:T(8,128)}, f32[512,32,128]{2,1,0:T(8,128)}) custom-call(f32[512,4096]{1,0:T(8,128)} %get-tuple-element.53.raw_ref, f32[512,32,128]{2,1,0:T(8,128)} %bitcast.5, f32[1]{0:T(128)S(6)} %div.24.scale_ref), custom_call_target="tpu_custom_call" | custom-call | tf_op jit(solution)/shard_map/outputs/pallas_call | solution.py:331
  (24 shorter events, 10.1 us)
Async XLA Ops:
  3.1 33.6 %collective-permute-start = (f32[128,1,4096]{2,1,0:T(1,128)}, f32[128,1,4096]{2,1,0:T(1,128)}, u32[]{:S(2)}, u32[]{:S(2)}) collective-permute-start(f32[128,1,4096]{2,1,0:T(1,128)} %cut_cross.1), channel_id=1, source_target_pairs={{2,4},{6,8},{10,12},{4,2},{8,6},{12,10},{3,5},{7,9},{11,13},{5,3},... | collective-permute-start | bytes 6291464 | tf_op jit(solution)/shard_map/ppermute | solution.py:365
  7.5 91.5 %collective-permute-start.1 = (f32[128,1,4096]{2,1,0:T(1,128)}, f32[128,1,4096]{2,1,0:T(1,128)S(1)}, u32[]{:S(2)}, u32[]{:S(2)}) collective-permute-start(f32[128,1,4096]{2,1,0:T(1,128)} %cut_near.1), channel_id=1, source_target_pairs={{0,2},{4,6},{8,10},{12,14},{2,0},{6,4},{10,8},{14,12},{1,3},{5,7},... | collective-permute-start | bytes 6291464 | tf_op jit(solution)/shard_map/ppermute | solution.py:366
  99.0 18.7 %collective-permute-start.3 = (f32[128,4096]{1,0:T(8,128)}, f32[128,4096]{1,0:T(8,128)}, u32[]{:S(2)}, u32[]{:S(2)}) collective-permute-start(f32[128,4096]{1,0:T(8,128)} %ratio_cross.1.refs_1_), channel_id=1, source_target_pairs={{2,4},{6,8},{10,12},{4,2},{8,6},{12,10},{3,5},{7,9},{11,13},{5,3},... | collective-permute-start | bytes 6291464 | tf_op jit(solution)/shard_map/ppermute | solution.py:391
  101.0 13.7 %copy-start.2 = (f32[2]{0:T(128)S(1)}, f32[2]{0:T(128)}, u32[]{:S(2)}) copy-start(f32[2]{0:T(128)} %param.6) | copy-start | bytes 28
  110.6 83.8 %collective-permute-start.2 = (f32[128,4096]{1,0:T(8,128)}, f32[128,4096]{1,0:T(8,128)S(1)}, u32[]{:S(2)}, u32[]{:S(2)}) collective-permute-start(f32[128,4096]{1,0:T(8,128)} %ratio_near.1.refs_2_.refs_1_), channel_id=1, source_target_pairs={{0,2},{4,6},{8,10},{12,14},{2,0},{6,4},{10,8},{14,12},{1,3},{5,7},... | collective-permute-start | bytes 6291464 | tf_op jit(solution)/shard_map/ppermute | solution.py:395
  133.8 3.8 %collective-permute-start.4 = (f32[384,1024]{1,0:T(8,128)}, f32[384,1024]{1,0:T(8,128)}, u32[]{:S(2)}, u32[]{:S(2)}) collective-permute-start(f32[384,1024]{1,0:T(8,128)} %get-tuple-element.36.refs_0_), channel_id=1, source_target_pairs={{0,1},{1,0},{2,3},{3,2},{4,5},{5,4},{6,7},{7,6},{8,9},{9,8},{10,11... | collective-permute-start | bytes 4718600 | tf_op jit(solution)/shard_map/ppermute | solution.py:401
  133.9 6.0 %collective-permute-start.5 = (f32[384,1024]{1,0:T(8,128)}, f32[384,1024]{1,0:T(8,128)}, u32[]{:S(2)}, u32[]{:S(2)}) collective-permute-start(f32[384,1024]{1,0:T(8,128)} %get-tuple-element.37.refs_1_), channel_id=1, source_target_pairs={{0,1},{1,0},{2,3},{3,2},{4,5},{5,4},{6,7},{7,6},{8,9},{9,8},{10,11... | collective-permute-start | bytes 4718600 | tf_op jit(solution)/shard_map/ppermute | solution.py:401
  134.4 7.7 %collective-permute-start.6 = (f32[384,1024]{1,0:T(8,128)}, f32[384,1024]{1,0:T(8,128)}, u32[]{:S(2)}, u32[]{:S(2)}) collective-permute-start(f32[384,1024]{1,0:T(8,128)} %get-tuple-element.38.refs_2_), channel_id=1, source_target_pairs={{0,1},{1,0},{2,3},{3,2},{4,5},{5,4},{6,7},{7,6},{8,9},{9,8},{10,11... | collective-permute-start | bytes 4718600 | tf_op jit(solution)/shard_map/ppermute | solution.py:401
  134.5 9.9 %collective-permute-start.7 = (f32[384,1024]{1,0:T(8,128)}, f32[384,1024]{1,0:T(8,128)}, u32[]{:S(2)}, u32[]{:S(2)}) collective-permute-start(f32[384,1024]{1,0:T(8,128)} %get-tuple-element.39.refs_3_), channel_id=1, source_target_pairs={{0,1},{1,0},{2,3},{3,2},{4,5},{5,4},{6,7},{7,6},{8,9},{9,8},{10,11... | collective-permute-start | bytes 4718600 | tf_op jit(solution)/shard_map/ppermute | solution.py:401
  204.6 1.3 copy-start
  205.9 2.1 collective-permute-start.10
  206.0 3.6 %collective-permute-start.11 = (f32[128,1024]{1,0:T(8,128)}, f32[128,1024]{1,0:T(8,128)S(1)}, u32[]{:S(2)}, u32[]{:S(2)}) collective-permute-start(f32[128,1024]{1,0:T(8,128)} %get-tuple-element.48.refs_3_), channel_id=1, source_target_pairs={{0,1},{1,0},{2,3},{3,2},{4,5},{5,4},{6,7},{7,6},{8,9},{9,8},{10,11... | collective-permute-start | bytes 1572872 | tf_op jit(solution)/shard_map/ppermute | solution.py:401
  206.5 3.1 %collective-permute-start.8 = (f32[128,1024]{1,0:T(8,128)S(1)}, f32[128,1024]{1,0:T(8,128)S(1)}, u32[]{:S(2)}, u32[]{:S(2)}) collective-permute-start(f32[128,1024]{1,0:T(8,128)S(1)} %get-tuple-element.45.refs_0_), channel_id=1, source_target_pairs={{0,1},{1,0},{2,3},{3,2},{4,5},{5,4},{6,7},{7,6},{8,9},{9,8},{10,11... | collective-permute-start | bytes 1572872 | tf_op jit(solution)/shard_map/ppermute | solution.py:401
  206.5 3.6 %collective-permute-start.9 = (f32[128,1024]{1,0:T(8,128)S(1)}, f32[128,1024]{1,0:T(8,128)S(1)}, u32[]{:S(2)}, u32[]{:S(2)}) collective-permute-start(f32[128,1024]{1,0:T(8,128)S(1)} %get-tuple-element.46.refs_1_), channel_id=1, source_target_pairs={{0,1},{1,0},{2,3},{3,2},{4,5},{5,4},{6,7},{7,6},{8,9},{9,8},{10,11... | collective-permute-start | bytes 1572872 | tf_op jit(solution)/shard_map/ppermute | solution.py:401
  210.1 1.6 copy-start.1

commit v5 on v4

--- a/solution.py
+++ b/solution.py
@@ -20,9 +20,11 @@
     return high, (x - high.astype(F32)).astype(BF16)
 
 
-def dot3(a, b, dims):
+def dot3(stack, b, dims):
     one = functools.partial(lax.dot_general, dimension_numbers=(dims, ((), ())), preferred_element_type=F32)
-    return one(a[0], b[0]) + (one(a[0], b[1]) + one(a[1], b[0]))
+    rows = stack.shape[0] // 2
+    both = one(stack, b[0])
+    return both[:rows] + (one(stack[:rows], b[1]) + both[rows:])
 
 
 def params(mebibytes):
@@ -31,6 +33,10 @@
 
 def hbm(*arrays):
     return [pltpu.with_memory_space_constraint(a, pltpu.HBM) for a in arrays]
+
+
+def vmem(*arrays):
+    return [pltpu.with_memory_space_constraint(a, pltpu.VMEM) for a in arrays]
 
 
 def pick(choice, side):
@@ -116,8 +122,8 @@
         share_ref, rest = rest[0], rest[1:]
     nouts = GROUPS + 1 if final else 1
     outs = rest[:nouts]
-    field, ahigh, alow, yhigh, ylow, whigh, wlow, other = rest[nouts : nouts + 8]
-    *results, in_sems, late_sems, out_sems = rest[nouts + 8 :]
+    field, a_both, y_both, whigh, wlow, other = rest[nouts : nouts + 6]
+    *results, in_sems, late_sems, out_sems = rest[nouts + 6 :]
 
     side = side_ref[0]
     nout, _, width, _ = band_ref.shape
@@ -156,17 +162,17 @@
     for copy in late[GROUPS - 1]:
         copy.start()
 
-    ahigh[...] = jnp.zeros_like(ahigh)
-    alow[...] = jnp.zeros_like(alow)
-    for i in range(nout):
-        for j in range(3):
-            k = i % 2 + j
-            place = (slice(i * width, (i + 1) * width), slice(k * width, (k + 1) * width))
-            ahigh[place], alow[place] = split(band_ref[i, j])
     blocks = [(i, min(2, nout - i)) for i in range(0, nout, 2)]
-    for y in (yhigh, ylow):
-        y[:, :width] = jnp.zeros((y.shape[0], width), BF16)
-        y[:, columns + width :] = jnp.zeros((y.shape[0], width), BF16)
+    total = nout * width
+    a_both[...] = jnp.zeros_like(a_both)
+    for first, n in blocks:
+        for i in range(n):
+            for j in range(3):
+                for part, value in enumerate(split(band_ref[first + i, j])):
+                    row = (2 * first + part * n + i) * width
+                    a_both[row : row + width, (i + j) * width : (i + j + 1) * width] = value
+    y_both[:, :width] = jnp.zeros((2 * total, width), BF16)
+    y_both[:, columns + width :] = jnp.zeros((2 * total, width), BF16)
 
     def columns_pass(g):
         for copy in inside[g]:
@@ -175,10 +181,11 @@
             at = slice(i * 2 * width, (i + 1) * 2 * width)
             to = slice((2 * i + 1) * width, (2 * i + 3) * width)
             for first, n in blocks:
-                rows = slice(first * width, (first + n) * width)
-                a = (ahigh[rows, : (n + 2) * width], alow[rows, : (n + 2) * width])
+                a = a_both[2 * first * width : 2 * (first + n) * width, : (n + 2) * width]
                 y = dot3(a, split(field[first * width : (first + n + 2) * width, at]), ((1,), (0,)))
-                yhigh[rows, to], ylow[rows, to] = split(y)
+                for part, value in enumerate(split(y)):
+                    row = part * total + first * width
+                    y_both[row : row + n * width, to] = value
 
     def rows_pass(g):
         for copy in late[g]:
@@ -186,7 +193,7 @@
         for t in range(g * pairs, (g + 1) * pairs):
             source = slice(t * 2 * width, (t + 2) * 2 * width)
             at = slice(t * 2 * width, (t + 1) * 2 * width)
-            value = dot3((yhigh[:, source], ylow[:, source]), (whigh[t], wlow[t]), ((1,), (1,)))
+            value = dot3(y_both[:, source], (whigh[t], wlow[t]), ((1,), (1,)))
             if final:
                 results[0][:, at] = value
                 results[1][:, at] = share_ref[0] * jnp.log(other[:, at] * value)
@@ -221,7 +228,7 @@
     nouts = 2 if final else 1
     kind = pltpu.HBM if pin else jax.ShapeDtypeStruct
     shapes = [kind((rows, columns // GROUPS), F32)] * (GROUPS if final else 0)
-    shapes.append(kind((rows, columns), F32))
+    shapes.append(pltpu.HBM((rows, columns), F32))
     plan = (tuple(pieces), len(arrays), extra, final)
     work = 3 * 2 * rows * columns * (depth + 4 * width)
     moved = 4 * (depth + 3 * rows) * columns + npairs * 2 * 2 * 8 * width * width
@@ -233,10 +240,8 @@
         out_shape=shapes,
         scratch_shapes=[
             pltpu.VMEM((depth, columns), F32),
-            pltpu.VMEM((rows, min(depth, 4 * width)), BF16),
-            pltpu.VMEM((rows, min(depth, 4 * width)), BF16),
-            pltpu.VMEM((rows, columns + 2 * width), BF16),
-            pltpu.VMEM((rows, columns + 2 * width), BF16),
+            pltpu.VMEM((2 * rows, min(depth, 4 * width)), BF16),
+            pltpu.VMEM((2 * rows, columns + 2 * width), BF16),
             pltpu.VMEM((npairs, 2 * width, 4 * width), BF16),
             pltpu.VMEM((npairs, 2 * width, 4 * width), BF16),
             pltpu.VMEM((rows, columns), F32),
@@ -306,15 +311,15 @@
             scratch_shapes=[pltpu.VMEM((2, tile, columns), F32), pltpu.SemaphoreType.DMA((2,))],
         ),
         out_shape=(
-            pltpu.HBM((rows_here, columns), F32),
-            pltpu.HBM((rows_here, 1, columns), F32),
+            pltpu.VMEM((rows_here, columns), F32),
+            pltpu.VMEM((rows_here, 1, columns), F32),
             jax.ShapeDtypeStruct((1,), F32),
         ),
         input_output_aliases={} if fresh else {2 * GROUPS + 2: 0, 2 * GROUPS + 3: 1},
         compiler_params=params(16),
         cost_estimate=pl.CostEstimate(flops=m.size // 16, bytes_accessed=m.size // 4, transcendentals=0),
         name=name,
-    )(choose([r // tile for r in row]).reshape(1), *t, *peers, m, *([] if fresh else hbm(*so_far[:2]) + [so_far[2]]))
+    )(choose([r // tile for r in row]).reshape(1), *t, *peers, m, *([] if fresh else vmem(*so_far[:2]) + [so_far[2]]))
 
 
 def output_kernel(raw_ref, quotient_ref, scale_ref, barycenter_ref, scaling_ref):
@@ -336,7 +341,7 @@
         out_shape=(jax.ShapeDtypeStruct(raw.shape, F32), jax.ShapeDtypeStruct(quotient.shape, F32)),
         compiler_params=params(16),
         name="outputs",
-    )(*hbm(raw, quotient), scale)
+    )(*vmem(raw, quotient), scale)
 
 
 def local(densities, scaling, weights, band):
@@ -398,7 +403,7 @@
         t, m = blur("logs_" + name, side, arrays, pieces, bands, wts, scaling, row, share, pin)
         keep = hbm if pin else lambda *a: list(a)
         return raw_rows(
-            "raw_" + name, row, keep(*t), [swap(part) for part in t], *keep(m), choose, rows_here, state
+            "raw_" + name, row, keep(*t), [swap(part) for part in t], *hbm(m), choose, rows_here, state
         )
 
     if nlocal == 1:

time: 254 us -> 263 us (1.035)
  local copies, waits for them, and re-layouts: 6.69 us -> 30.9 us
  Pallas kernels: 108 us -> 93.1 us
    unnamed x6 -> x18, local copies, waits for them, and re-layouts: 2.91 us -> 27.1 us
    pallas_call x1, Pallas kernels: 13.7 us -> 6.4 us  [outputs(): pl.pallas_call(output_kernel, grid=(rows // tile,), in_specs=[flat, deep,...]
    pallas_call x5, Pallas kernels: 56.5 us -> 51.6 us  [blur(): pl.pallas_call(functools.partial(blur_kernel, plan), in_specs=[INSMEM] +...]
    pallas_call x2, Pallas kernels: 21.4 us -> 18.5 us  [raw_rows(): pl.pallas_call(functools.partial(raw_kernel, fresh), grid_spec=pltpu.Pref...]
  transfers between devices with their start and end apart: 12 -> 12, of which waited for: 9 -> 9; matrix products, arithmetic and copies ran while one was open for 2% -> 2% of each run, Pallas kernels for 30% -> 27%
where the time goes in v5:
time: 263 us; the launch traced here: 262 us
  waiting for transfers between devices  98.6 us (37%)
  Pallas kernels  93.1 us (35%)
  local copies, waits for them, and re-layouts  30.9 us (12%)
  blocking collectives  22.4 us (9%)
  starting transfers between devices  14.7 us (6%)
    ppermute x1, waiting for transfers between devices, local(): near1 = near(cut('cut_near', side, scaling, near_row, width))  54.2 us
    pallas_call x5, Pallas kernels, blur(): pl.pallas_call(functools.partial(blur_kernel, plan), in_specs=[INSMEM] +...  51.6 us
    ppermute x1, waiting for transfers between devices, local(): near2 = near(ratio_near)  31.7 us
    unnamed x18, local copies, waits for them, and re-layouts  27.1 us
    psum x1, blocking collectives, local(): mass = lax.psum(mass, 'space')  22.4 us
    pallas_call x2, Pallas kernels, raw_rows(): pl.pallas_call(functools.partial(raw_kernel, fresh), grid_spec=pltpu.Pref...  18.5 us
    ppermute x8, waiting for transfers between devices, finish(): swap(part)  12.6 us
    pallas_call x1, Pallas kernels, row_weights(): pl.pallas_call(functools.partial(weight_kernel, nblocks), grid=(nblocks /...  11.7 us
  transfers between devices with their start and end apart: 12, of which 9 were waited for; matrix products, arithmetic and copies ran while one was open for 2% of the time, Pallas kernels for 27%

profile of v5, /device:TPU:0, one launch (start us, length us, event | category | flops | bytes accessed | tf_op | source)
XLA Modules:
  0.0 262.3 jit_solution(10759784147610001332)
XLA Ops:
  0.6 2.4 cut_cross.1
  7.5 4.5 %collective-permute-start.1 = (f32[128,1,4096]{2,1,0:T(1,128)}, f32[128,1,4096]{2,1,0:T(1,128)S(1)}, u32[]{:S(2)}, u32[]{:S(2)}) collective-permute-start(f32[128,1,4096]{2,1,0:T(1,128)} %cut_near.1), channel_id=1, source_target_pairs={{0,2},{4,6},{8,10},{12,14},{2,0},{6,4},{10,8},{14,12},{1,3},{5,7},... | collective-permute-start | bytes 6291464 | tf_op jit(solution)/shard_map/ppermute | solution.py:371
  12.0 11.7 %row_weights.1 = (bf16[16,256,512]{2,1,0:T(8,128)(2,1)}, bf16[16,256,512]{2,1,0:T(8,128)(2,1)}) custom-call(f32[32,3,128,128]{3,2,1,0:T(8,128)} %band_ref.1), custom_call_target="tpu_custom_call" | custom-call | tf_op jit(solution)/shard_map/row_weights/pallas_call | solution.py:105
  24.7 10.9 %ratio_inner.1.refs_4_.refs_2_ = f32[256,4096]{1,0:T(8,128)} custom-call(s32[1]{0:T(128)} %bitcast.1.side_ref.refs_0_, f32[512,1,4096]{2,1,0:T(1,128)} %refs_7_.1, f32[2,3,128,128]{3,2,1,0:T(8,128)S(1)} %constant_dynamic-slice_fusion.3.refs_2_, bf16[16,256,512]{2,1,0:T(8,128)(2,1)} %get-tuple-element.30.refs_3_.refs_4_.refs_6_.refs_5_, ...), custom_call_target="tpu_custom_call" | custom-call | flops 100663296 | bytes 458752 | tf_op jit(solution)/shard_map/ratio_inner/pallas_call | solution.py:236
  36.6 8.1 %ratio_cross.1.refs_1_ = f32[128,4096]{1,0:T(8,128)} custom-call(s32[1]{0:T(128)} %bitcast.1.side_ref.refs_0_, f32[512,1,4096]{2,1,0:T(1,128)} %refs_7_.1, f32[128,1,4096]{2,1,0:T(1,128)} %collective-permute-done.refs_2_, f32[1,3,128,128]{3,2,1,0:T(8,128)S(1)} %get-tuple-element.61.refs_3_, ...), custom_call_target="tpu_custom_call" | custom-call | flops 44040192 | bytes 327680 | tf_op jit(solution)/shard_map/ratio_cross/pallas_call | solution.py:236
  44.8 54.2 %collective-permute-done.1.refs_2_ = f32[128,1,4096]{2,1,0:T(1,128)S(1)} collective-permute-done((f32[128,1,4096]{2,1,0:T(1,128)}, f32[128,1,4096]{2,1,0:T(1,128)S(1)}, u32[]{:S(2)}, u32[]{:S(2)}) %collective-permute-start.1) | collective-permute-done | bytes 2097184 | tf_op jit(solution)/shard_map/ppermute | solution.py:371
  101.0 8.0 %ratio_near.1.refs_2_.refs_1_ = f32[128,4096]{1,0:T(8,128)} custom-call(s32[1]{0:T(128)} %bitcast.1.side_ref.refs_0_, f32[512,1,4096]{2,1,0:T(1,128)} %refs_7_.1, f32[128,1,4096]{2,1,0:T(1,128)S(1)} %collective-permute-done.1.refs_2_, f32[1,3,128,128]{3,2,1,0:T(8,128)S(1)} %get-tuple-element.60.refs_3_.refs_4_, ...), custom_call_target="tpu_custom_call" | custom-call | flops 44040192 | bytes 327680 | tf_op jit(solution)/shard_map/ratio_near/pallas_call | solution.py:236
  109.0 4.1 %collective-permute-start.2 = (f32[128,4096]{1,0:T(8,128)}, f32[128,4096]{1,0:T(8,128)S(1)}, u32[]{:S(2)}, u32[]{:S(2)}) collective-permute-start(f32[128,4096]{1,0:T(8,128)} %ratio_near.1.refs_2_.refs_1_), channel_id=1, source_target_pairs={{0,2},{4,6},{8,10},{12,14},{2,0},{6,4},{10,8},{14,12},{1,3},{5,7},... | collective-permute-start | bytes 6291464 | tf_op jit(solution)/shard_map/ppermute | solution.py:400
  116.0 16.0 %logs_most.1 = (f32[384,1024]{1,0:T(8,128)}, f32[384,1024]{1,0:T(8,128)}, f32[384,1024]{1,0:T(8,128)}, f32[384,1024]{1,0:T(8,128)}, f32[384,4096]{1,0:T(8,128)}) custom-call(s32[1]{0:T(128)} %bitcast.1.side_ref.refs_0_, f32[128,4096]{1,0:T(8,128)} %ratio_cross.1.refs_1_, f32[128,4096]{1,0:T(8,128)} %ratio_near.1.refs_2_.refs_1_, ...), custom_call_target="tpu_custom_call" | custom-call | flops 169869312 | bytes 589824 | tf_op jit(solution)/shard_map/logs_most/pallas_call | solution.py:236
  133.1 2.7 %collective-permute-done.4.refs_4_ = f32[384,1024]{1,0:T(8,128)} collective-permute-done((f32[384,1024]{1,0:T(8,128)}, f32[384,1024]{1,0:T(8,128)}, u32[]{:S(2)}, u32[]{:S(2)}) %collective-permute-start.4) | collective-permute-done | bytes 1572896 | tf_op jit(solution)/shard_map/ppermute | solution.py:406
  142.6 13.3 %raw_most.1 = (f32[512,4096]{1,0:T(8,128)S(1)}, f32[512,1,4096]{2,1,0:T(1,128)S(1)}, f32[1]{0:T(128)}) custom-call(s32[1]{0:T(128)} %bitcast.2.start_ref, f32[384,1024]{1,0:T(8,128)} %get-tuple-element.36.refs_0_, f32[384,1024]{1,0:T(8,128)} %get-tuple-element.37.refs_1_, f32[384,1024]{1,0:T(8,128)} %get-tuple-element.38.refs_2_, ...), custom_call_target="tpu_custom_call" | custom-call | flops 98304 | bytes 393216 | tf_op jit(solution)/shard_map/raw_most/pallas_call | solution.py:300
  155.9 3.4 %copy-done = f32[512,4096]{1,0:T(8,128)} copy-done((f32[512,4096]{1,0:T(8,128)}, f32[512,4096]{1,0:T(8,128)S(1)}, u32[]{:S(2)}) %copy-start) | copy-done | bytes 8388632
  159.3 3.4 %copy-done.4 = f32[512,1,4096]{2,1,0:T(1,128)} copy-done((f32[512,1,4096]{2,1,0:T(1,128)}, f32[512,1,4096]{2,1,0:T(1,128)S(1)}, u32[]{:S(2)}) %copy-start.4) | copy-done | bytes 8388632
  162.7 31.7 %collective-permute-done.2.refs_3_ = f32[128,4096]{1,0:T(8,128)S(1)} collective-permute-done((f32[128,4096]{1,0:T(8,128)}, f32[128,4096]{1,0:T(8,128)S(1)}, u32[]{:S(2)}, u32[]{:S(2)}) %collective-permute-start.2) | collective-permute-done | bytes 2097184 | tf_op jit(solution)/shard_map/ppermute | solution.py:400
  194.5 8.6 %logs_near.1 = (f32[128,1024]{1,0:T(8,128)S(1)}, f32[128,1024]{1,0:T(8,128)S(1)}, f32[128,1024]{1,0:T(8,128)}, f32[128,1024]{1,0:T(8,128)}, f32[128,4096]{1,0:T(8,128)}) custom-call(s32[1]{0:T(128)} %bitcast.1.side_ref.refs_0_, f32[128,4096]{1,0:T(8,128)} %ratio_near.1.refs_2_.refs_1_, f32[256,4096]{1,0:T(8,128)} %ratio_inner.1.refs_4_.refs_2_, ...), custom_call_target="tpu_custom_call" | custom-call | flops 44040192 | bytes 327680 | tf_op jit(solution)/shard_map/logs_near/pallas_call | solution.py:236
  207.3 3.4 %copy-done.1 = f32[512,4096]{1,0:T(8,128)S(1)} copy-done((f32[512,4096]{1,0:T(8,128)S(1)}, f32[512,4096]{1,0:T(8,128)}, u32[]{:S(2)}) %copy-start.1) | copy-done | bytes 8388632
  210.7 3.4 %copy-done.5 = f32[512,1,4096]{2,1,0:T(1,128)S(1)} copy-done((f32[512,1,4096]{2,1,0:T(1,128)S(1)}, f32[512,1,4096]{2,1,0:T(1,128)}, u32[]{:S(2)}) %copy-start.5) | copy-done | bytes 8388632
  214.1 5.2 %raw_near.1 = (f32[512,4096]{1,0:T(8,128)S(1)}, f32[512,1,4096]{2,1,0:T(1,128)S(1)}, f32[1]{0:T(128)}) custom-call(s32[1]{0:T(128)} %bitcast.start_ref, f32[128,1024]{1,0:T(8,128)S(1)} %get-tuple-element.45.refs_0_, f32[128,1024]{1,0:T(8,128)S(1)} %get-tuple-element.46.refs_1_, ...), custom_call_target="tpu_custom_call", output_to_operand_aliasing={{0}: (10, {}), {1}: (11, {})} | custom-call | flops 32768 | bytes 131072 | tf_op jit(solution)/shard_map/raw_near/pallas_call | solution.py:300
  219.3 3.4 %copy-done.2 = f32[512,4096]{1,0:T(8,128)} copy-done((f32[512,4096]{1,0:T(8,128)}, f32[512,4096]{1,0:T(8,128)S(1)}, u32[]{:S(2)}) %copy-start.2) | copy-done | bytes 8388632
  222.7 3.4 %copy-done.6 = f32[512,1,4096]{2,1,0:T(1,128)} copy-done((f32[512,1,4096]{2,1,0:T(1,128)}, f32[512,1,4096]{2,1,0:T(1,128)S(1)}, u32[]{:S(2)}) %copy-start.6) | copy-done | bytes 8388632
  226.1 22.4 %psum.7 = f32[1]{0:T(128)} all-reduce(f32[1]{0:T(128)} %get-tuple-element.55), channel_id=1, replica_groups=mesh['parts'=2,'space'=8,'member'=2] {'space'}, use_global_device_ids=true, to_apply=%region_1.2 | all-reduce | flops 1 | bytes 8 | tf_op jit(solution)/shard_map/psum | solution.py:428
  249.2 3.4 %copy-done.3 = f32[512,4096]{1,0:T(8,128)S(1)} copy-done((f32[512,4096]{1,0:T(8,128)S(1)}, f32[512,4096]{1,0:T(8,128)}, u32[]{:S(2)}) %copy-start.3) | copy-done | bytes 8388632
  252.5 3.4 %copy-done.7 = f32[512,1,4096]{2,1,0:T(1,128)S(1)} copy-done((f32[512,1,4096]{2,1,0:T(1,128)S(1)}, f32[512,1,4096]{2,1,0:T(1,128)}, u32[]{:S(2)}) %copy-start.7) | copy-done | bytes 8388632
  255.9 6.4 %outputs.1 = (f32[512,4096]{1,0:T(8,128)}, f32[512,32,128]{2,1,0:T(8,128)}) custom-call(f32[512,4096]{1,0:T(8,128)S(1)} %copy-done.3, f32[512,32,128]{2,1,0:T(8,128)S(1)} %bitcast.5, f32[1]{0:T(128)S(6)} %div.24.scale_ref), custom_call_target="tpu_custom_call" | custom-call | tf_op jit(solution)/shard_map/outputs/pallas_call | solution.py:336
  (36 shorter events, 23.5 us)
Async XLA Ops:
  3.1 33.6 %collective-permute-start = (f32[128,1,4096]{2,1,0:T(1,128)}, f32[128,1,4096]{2,1,0:T(1,128)}, u32[]{:S(2)}, u32[]{:S(2)}) collective-permute-start(f32[128,1,4096]{2,1,0:T(1,128)} %cut_cross.1), channel_id=1, source_target_pairs={{2,4},{6,8},{10,12},{4,2},{8,6},{12,10},{3,5},{7,9},{11,13},{5,3},... | collective-permute-start | bytes 6291464 | tf_op jit(solution)/shard_map/ppermute | solution.py:370
  7.5 91.5 %collective-permute-start.1 = (f32[128,1,4096]{2,1,0:T(1,128)}, f32[128,1,4096]{2,1,0:T(1,128)S(1)}, u32[]{:S(2)}, u32[]{:S(2)}) collective-permute-start(f32[128,1,4096]{2,1,0:T(1,128)} %cut_near.1), channel_id=1, source_target_pairs={{0,2},{4,6},{8,10},{12,14},{2,0},{6,4},{10,8},{14,12},{1,3},{5,7},... | collective-permute-start | bytes 6291464 | tf_op jit(solution)/shard_map/ppermute | solution.py:371
  99.0 17.0 %collective-permute-start.3 = (f32[128,4096]{1,0:T(8,128)}, f32[128,4096]{1,0:T(8,128)}, u32[]{:S(2)}, u32[]{:S(2)}) collective-permute-start(f32[128,4096]{1,0:T(8,128)} %ratio_cross.1.refs_1_), channel_id=1, source_target_pairs={{2,4},{6,8},{10,12},{4,2},{8,6},{12,10},{3,5},{7,9},{11,13},{5,3},... | collective-permute-start | bytes 6291464 | tf_op jit(solution)/shard_map/ppermute | solution.py:396
  101.0 12.0 %copy-start.8 = (f32[2]{0:T(128)S(1)}, f32[2]{0:T(128)}, u32[]{:S(2)}) copy-start(f32[2]{0:T(128)} %param.6) | copy-start | bytes 28
  109.0 85.5 %collective-permute-start.2 = (f32[128,4096]{1,0:T(8,128)}, f32[128,4096]{1,0:T(8,128)S(1)}, u32[]{:S(2)}, u32[]{:S(2)}) collective-permute-start(f32[128,4096]{1,0:T(8,128)} %ratio_near.1.refs_2_.refs_1_), channel_id=1, source_target_pairs={{0,2},{4,6},{8,10},{12,14},{2,0},{6,4},{10,8},{14,12},{1,3},{5,7},... | collective-permute-start | bytes 6291464 | tf_op jit(solution)/shard_map/ppermute | solution.py:400
  132.0 3.8 %collective-permute-start.4 = (f32[384,1024]{1,0:T(8,128)}, f32[384,1024]{1,0:T(8,128)}, u32[]{:S(2)}, u32[]{:S(2)}) collective-permute-start(f32[384,1024]{1,0:T(8,128)} %get-tuple-element.36.refs_0_), channel_id=1, source_target_pairs={{0,1},{1,0},{2,3},{3,2},{4,5},{5,4},{6,7},{7,6},{8,9},{9,8},{10,11... | collective-permute-start | bytes 4718600 | tf_op jit(solution)/shard_map/ppermute | solution.py:406
  132.1 6.0 %collective-permute-start.5 = (f32[384,1024]{1,0:T(8,128)}, f32[384,1024]{1,0:T(8,128)}, u32[]{:S(2)}, u32[]{:S(2)}) collective-permute-start(f32[384,1024]{1,0:T(8,128)} %get-tuple-element.37.refs_1_), channel_id=1, source_target_pairs={{0,1},{1,0},{2,3},{3,2},{4,5},{5,4},{6,7},{7,6},{8,9},{9,8},{10,11... | collective-permute-start | bytes 4718600 | tf_op jit(solution)/shard_map/ppermute | solution.py:406
  132.6 7.7 %collective-permute-start.6 = (f32[384,1024]{1,0:T(8,128)}, f32[384,1024]{1,0:T(8,128)}, u32[]{:S(2)}, u32[]{:S(2)}) collective-permute-start(f32[384,1024]{1,0:T(8,128)} %get-tuple-element.38.refs_2_), channel_id=1, source_target_pairs={{0,1},{1,0},{2,3},{3,2},{4,5},{5,4},{6,7},{7,6},{8,9},{9,8},{10,11... | collective-permute-start | bytes 4718600 | tf_op jit(solution)/shard_map/ppermute | solution.py:406
  132.7 9.9 %collective-permute-start.7 = (f32[384,1024]{1,0:T(8,128)}, f32[384,1024]{1,0:T(8,128)}, u32[]{:S(2)}, u32[]{:S(2)}) collective-permute-start(f32[384,1024]{1,0:T(8,128)} %get-tuple-element.39.refs_3_), channel_id=1, source_target_pairs={{0,1},{1,0},{2,3},{3,2},{4,5},{5,4},{6,7},{7,6},{8,9},{9,8},{10,11... | collective-permute-start | bytes 4718600 | tf_op jit(solution)/shard_map/ppermute | solution.py:406
  155.9 3.4 %copy-start = (f32[512,4096]{1,0:T(8,128)}, f32[512,4096]{1,0:T(8,128)S(1)}, u32[]{:S(2)}) copy-start(f32[512,4096]{1,0:T(8,128)S(1)} %get-tuple-element.50.refs_9_) | copy-start | bytes 25165828
  159.3 3.4 %copy-start.4 = (f32[512,1,4096]{2,1,0:T(1,128)}, f32[512,1,4096]{2,1,0:T(1,128)S(1)}, u32[]{:S(2)}) copy-start(f32[512,1,4096]{2,1,0:T(1,128)S(1)} %get-tuple-element.51.refs_10_) | copy-start | bytes 25165828
  203.1 2.2 collective-permute-start.10
  203.1 3.6 %collective-permute-start.11 = (f32[128,1024]{1,0:T(8,128)}, f32[128,1024]{1,0:T(8,128)S(1)}, u32[]{:S(2)}, u32[]{:S(2)}) collective-permute-start(f32[128,1024]{1,0:T(8,128)} %get-tuple-element.48.refs_3_), channel_id=1, source_target_pairs={{0,1},{1,0},{2,3},{3,2},{4,5},{5,4},{6,7},{7,6},{8,9},{9,8},{10,11... | collective-permute-start | bytes 1572872 | tf_op jit(solution)/shard_map/ppermute | solution.py:406
  203.6 3.1 %collective-permute-start.8 = (f32[128,1024]{1,0:T(8,128)S(1)}, f32[128,1024]{1,0:T(8,128)S(1)}, u32[]{:S(2)}, u32[]{:S(2)}) collective-permute-start(f32[128,1024]{1,0:T(8,128)S(1)} %get-tuple-element.45.refs_0_), channel_id=1, source_target_pairs={{0,1},{1,0},{2,3},{3,2},{4,5},{5,4},{6,7},{7,6},{8,9},{9,8},{10,11... | collective-permute-start | bytes 1572872 | tf_op jit(solution)/shard_map/ppermute | solution.py:406
  203.7 3.6 %collective-permute-start.9 = (f32[128,1024]{1,0:T(8,128)S(1)}, f32[128,1024]{1,0:T(8,128)S(1)}, u32[]{:S(2)}, u32[]{:S(2)}) collective-permute-start(f32[128,1024]{1,0:T(8,128)S(1)} %get-tuple-element.46.refs_1_), channel_id=1, source_target_pairs={{0,1},{1,0},{2,3},{3,2},{4,5},{5,4},{6,7},{7,6},{8,9},{9,8},{10,11... | collective-permute-start | bytes 1572872 | tf_op jit(solution)/shard_map/ppermute | solution.py:406
  207.3 3.4 %copy-start.1 = (f32[512,4096]{1,0:T(8,128)S(1)}, f32[512,4096]{1,0:T(8,128)}, u32[]{:S(2)}) copy-start(f32[512,4096]{1,0:T(8,128)} %copy-done) | copy-start | bytes 25165828
  210.7 3.4 %copy-start.5 = (f32[512,1,4096]{2,1,0:T(1,128)S(1)}, f32[512,1,4096]{2,1,0:T(1,128)}, u32[]{:S(2)}) copy-start(f32[512,1,4096]{2,1,0:T(1,128)} %copy-done.4) | copy-start | bytes 25165828
  219.3 3.4 %copy-start.2 = (f32[512,4096]{1,0:T(8,128)}, f32[512,4096]{1,0:T(8,128)S(1)}, u32[]{:S(2)}) copy-start(f32[512,4096]{1,0:T(8,128)S(1)} %get-tuple-element.53.raw_ref) | copy-start | bytes 25165828
  222.7 3.4 %copy-start.6 = (f32[512,1,4096]{2,1,0:T(1,128)}, f32[512,1,4096]{2,1,0:T(1,128)S(1)}, u32[]{:S(2)}) copy-start(f32[512,1,4096]{2,1,0:T(1,128)S(1)} %get-tuple-element.54) | copy-start | bytes 25165828
  249.1 3.4 %copy-start.3 = (f32[512,4096]{1,0:T(8,128)S(1)}, f32[512,4096]{1,0:T(8,128)}, u32[]{:S(2)}) copy-start(f32[512,4096]{1,0:T(8,128)} %copy-done.2) | copy-start | bytes 25165828
  252.5 3.4 %copy-start.7 = (f32[512,1,4096]{2,1,0:T(1,128)S(1)}, f32[512,1,4096]{2,1,0:T(1,128)}, u32[]{:S(2)}) copy-start(f32[512,1,4096]{2,1,0:T(1,128)} %copy-done.6) | copy-start | bytes 25165828

commit v6 on v5

--- a/solution.py
+++ b/solution.py
@@ -259,7 +259,7 @@
     return (result[:-1], result[-1]) if final else result[0]
 
 
-def raw_kernel(fresh, start_ref, *refs):
+def raw_kernel(fresh, first, side_ref, *refs):
     own, peer, m_ref = refs[:GROUPS], refs[GROUPS : 2 * GROUPS], refs[2 * GROUPS]
     raw_ref, quotient_ref, mass_ref, quotient, sems = refs[-5:]
     tile = raw_ref.shape[0]
@@ -267,7 +267,7 @@
     slot = lax.rem(at, 2)
 
     def copy(step, slot):
-        row = pl.multiple_of((start_ref[0] + step) * tile, tile)
+        row = pl.multiple_of(pick(first, side_ref[0]) + step * tile, tile)
         return pltpu.make_async_copy(quotient.at[slot], area(quotient_ref, row, tile, slice(None)), sems.at[slot])
 
     @pl.when(at >= 2)
@@ -291,20 +291,21 @@
         copy(at, slot).wait()
 
 
-def raw_rows(name, row, t, peers, m, choose, rows_here, so_far):
+def raw_rows(name, side, row, t, peers, m, rows_here, so_far):
     fresh = so_far is None
     rows, columns = m.shape
     tile = 32
+    starts = [r // tile for r in row]
     part = pl.BlockSpec((tile, columns), lambda i, at: (i, 0))
     group = pl.BlockSpec((tile, columns // GROUPS), lambda i, at: (i, 0))
     return pl.pallas_call(
-        functools.partial(raw_kernel, fresh),
+        functools.partial(raw_kernel, fresh, row),
         grid_spec=pltpu.PrefetchScalarGridSpec(
             num_scalar_prefetch=1,
             grid=(rows // tile,),
             in_specs=[group] * (2 * GROUPS) + [part] + ([] if fresh else [ANY, ANY, INSMEM]),
             out_specs=(
-                pl.BlockSpec((tile, columns), lambda i, at: (at[0] + i, 0)),
+                pl.BlockSpec((tile, columns), lambda i, at: (jnp.where(at[0] == 0, *starts) + i, 0)),
                 ANY,
                 INSMEM,
             ),
@@ -319,29 +320,58 @@
         compiler_params=params(16),
         cost_estimate=pl.CostEstimate(flops=m.size // 16, bytes_accessed=m.size // 4, transcendentals=0),
         name=name,
-    )(choose([r // tile for r in row]).reshape(1), *t, *peers, m, *([] if fresh else vmem(*so_far[:2]) + [so_far[2]]))
-
-
-def output_kernel(raw_ref, quotient_ref, scale_ref, barycenter_ref, scaling_ref):
-    scale = scale_ref[0]
+    )(side, *t, *peers, m, *([] if fresh else vmem(*so_far[:2]) + [so_far[2]]))
+
+
+def sum_kernel(a_ref, b_ref, out_ref):
+    out_ref[0] = a_ref[0] + b_ref[0]
+
+
+def mass_parts(mass):
+    count = lax.axis_size("space")
+    if count & (count - 1):
+        return [lax.psum(mass, "space")]
+    parts = [mass]
+    for bit in range(count.bit_length() - 1):
+        if len(parts) == 2:
+            parts = [
+                pl.pallas_call(
+                    sum_kernel,
+                    in_specs=[INSMEM, INSMEM],
+                    out_specs=INSMEM,
+                    out_shape=jax.ShapeDtypeStruct((1,), F32),
+                    compiler_params=params(1),
+                    name="mass",
+                )(*parts)
+            ]
+        parts.append(lax.ppermute(parts[0], "space", [(i, i ^ (1 << bit)) for i in range(count)]))
+    return parts
+
+
+def output_kernel(total, raw_ref, quotient_ref, *refs):
+    *masses, barycenter_ref, scaling_ref = refs
+    mass = masses[0][0]
+    for part in masses[1:]:
+        mass += part[0]
+    scale = jnp.full((1, raw_ref.shape[1]), total, F32) / jnp.full((1, raw_ref.shape[1]), mass, F32)
     barycenter_ref[...] = raw_ref[...] * scale
-    scaling_ref[...] = quotient_ref[...] * scale
-
-
-def outputs(raw, quotient, scale):
+    scaling_ref[...] = quotient_ref[...] * scale[:, : quotient_ref.shape[2]].reshape(1, 1, quotient_ref.shape[2])
+
+
+def outputs(raw, quotient, masses):
     rows, columns = raw.shape
     tile = 64
     flat = pl.BlockSpec((tile, columns), lambda i: (i, 0))
     deep = pl.BlockSpec((tile,) + quotient.shape[1:], lambda i: (i, 0, 0))
     return pl.pallas_call(
-        output_kernel,
+        functools.partial(output_kernel, float(columns * columns)),
         grid=(rows // tile,),
-        in_specs=[flat, deep, INSMEM],
+        in_specs=[flat, deep] + [INSMEM] * len(masses),
         out_specs=(flat, deep),
         out_shape=(jax.ShapeDtypeStruct(raw.shape, F32), jax.ShapeDtypeStruct(quotient.shape, F32)),
         compiler_params=params(16),
         name="outputs",
-    )(*vmem(raw, quotient), scale)
+    )(*vmem(raw, quotient), *masses)
 
 
 def local(densities, scaling, weights, band):
@@ -365,7 +395,7 @@
     swap = functools.partial(lax.ppermute, axis_name="member", perm=[(0, 1), (1, 0)])
 
     def choose(choice):
-        return jnp.where(odd == 0, choice[0], choice[1]).astype(jnp.int32)
+        return jnp.where(odd == 0, *[c // width for c in choice]).astype(jnp.int32)
 
     cross1 = cross(cut("cut_cross", side, scaling, cross_row, width))
     near1 = near(cut("cut_near", side, scaling, near_row, width))
@@ -374,10 +404,10 @@
     share = lax.dynamic_slice_in_dim(shares, lax.axis_index("member"), 1)
     wts = row_weights(band)
     mine = place * nlocal
-    band_at = lambda row, blocks: lax.dynamic_slice_in_dim(band, mine + row // width, blocks, 0)
+    band_at = lambda block, blocks: lax.dynamic_slice_in_dim(band, mine + block, blocks, 0)
 
     if inner > 0:
-        inner_bands = band_at(width, inner)
+        inner_bands = band_at(1, inner)
         ratio_inner = blur(
             "ratio_inner", side, hbm(scaling), [(0, 0, rows_here, 0)], inner_bands, wts, densities, width
         )
@@ -403,7 +433,7 @@
         t, m = blur("logs_" + name, side, arrays, pieces, bands, wts, scaling, row, share, pin)
         keep = hbm if pin else lambda *a: list(a)
         return raw_rows(
-            "raw_" + name, row, keep(*t), [swap(part) for part in t], *hbm(m), choose, rows_here, state
+            "raw_" + name, side, row, keep(*t), [swap(part) for part in t], *hbm(m), rows_here, state
         )
 
     if nlocal == 1:
@@ -425,8 +455,7 @@
         state = finish("near", hbm(ratio_near, beside) + [near2], pieces, bands, near_row, share, state, False)
 
     raw, quotient, mass = state
-    mass = lax.psum(mass, "space")
-    barycenter, new_scaling = outputs(raw, quotient.reshape(rows_here, cols_all // width, width), float(cols_all * cols_all) / mass)
+    barycenter, new_scaling = outputs(raw, quotient.reshape(rows_here, cols_all // width, width), mass_parts(mass))
     return barycenter, new_scaling.reshape(rows_here, 1, cols_all)
 
 

time: 263 us -> 237 us (0.901)
  local copies, waits for them, and re-layouts: 30.9 us -> 3.74 us
  blocking collectives: 22.4 us -> 0 us
  waiting for transfers between devices: 98.6 us -> 112 us
  starting transfers between devices: 14.7 us -> 22.4 us
  Pallas kernels: 93.1 us -> 96.1 us
    unnamed x18 -> x2, local copies, waits for them, and re-layouts: 27.1 us -> 0.01 us
    psum x1 -> x0, blocking collectives: 22.4 us -> none  [local(): mass = lax.psum(mass, 'space')]
    ppermute x1, waiting for transfers between devices: 31.7 us -> 39.9 us  [local(): near2 = near(ratio_near)]
    ppermute x0 -> x3, starting transfers between devices: none -> 7.69 us  [mass_parts(): lax.ppermute(parts[0], 'space', [(i, i ^ 1 << bit) for i in range(count)])]
    ppermute x0 -> x3, waiting for transfers between devices: none -> 5.36 us  [mass_parts(): lax.ppermute(parts[0], 'space', [(i, i ^ 1 << bit) for i in range(count)])]
    pallas_call x3 -> x5, Pallas kernels: 24.9 us -> 28.3 us  [the longest x2 17.1 us: raw_rows(): pl.pallas_call(functools.partial(raw_kernel, fresh, row), grid_spec=pltpu...]
  transfers between devices with their start and end apart: 12 -> 15, of which waited for: 9 -> 13; matrix products, arithmetic and copies ran while one was open for 2% -> 2% of each run, Pallas kernels for 27% -> 29%
where the time goes in v6:
time: 237 us; the launch traced here: 236 us
  waiting for transfers between devices  112 us (47%)
  Pallas kernels  96.1 us (41%)
  starting transfers between devices  22.4 us (9%)
  local copies, waits for them, and re-layouts  3.74 us (2%)
    ppermute x1, waiting for transfers between devices, local(): near1 = near(cut('cut_near', side, scaling, near_row, width))  54.2 us
    pallas_call x5, Pallas kernels, blur(): pl.pallas_call(functools.partial(blur_kernel, plan), in_specs=[INSMEM] +...  51.3 us
    ppermute x1, waiting for transfers between devices, local(): near2 = near(ratio_near)  39.9 us
    pallas_call x2, Pallas kernels, raw_rows(): pl.pallas_call(functools.partial(raw_kernel, fresh, row), grid_spec=pltpu...  17.1 us
    ppermute x8, waiting for transfers between devices, finish(): swap(part)  12.5 us
    pallas_call x1, Pallas kernels, row_weights(): pl.pallas_call(functools.partial(weight_kernel, nblocks), grid=(nblocks /...  11.6 us
    ppermute x3, starting transfers between devices, mass_parts(): lax.ppermute(parts[0], 'space', [(i, i ^ 1 << bit) for i in range(count)])  7.69 us
    pallas_call x1, Pallas kernels, outputs(): pl.pallas_call(functools.partial(output_kernel, float(columns * columns))...  7.64 us
  transfers between devices with their start and end apart: 15, of which 13 were waited for; matrix products, arithmetic and copies ran while one was open for 2% of the time, Pallas kernels for 29%

profile of v6, /device:TPU:0, one launch (start us, length us, event | category | flops | bytes accessed | tf_op | source)
XLA Modules:
  0.0 236.3 jit_solution(81901558187515030)
XLA Ops:
  0.6 2.5 %cut_cross.1 = f32[128,1,4096]{2,1,0:T(1,128)} custom-call(s32[1]{0:T(128)} %bitcast.side_ref.refs_0_, f32[512,1,4096]{2,1,0:T(1,128)} %refs_7_.1), custom_call_target="tpu_custom_call" | custom-call | tf_op jit(solution)/shard_map/cut_cross/pallas_call | solution.py:68
  3.1 2.1 collective-permute-start
  5.2 2.4 %cut_near.1 = f32[128,1,4096]{2,1,0:T(1,128)} custom-call(s32[1]{0:T(128)} %bitcast.side_ref.refs_0_, f32[512,1,4096]{2,1,0:T(1,128)} %refs_7_.1), custom_call_target="tpu_custom_call" | custom-call | tf_op jit(solution)/shard_map/cut_near/pallas_call | solution.py:68
  7.6 4.4 %collective-permute-start.1 = (f32[128,1,4096]{2,1,0:T(1,128)}, f32[128,1,4096]{2,1,0:T(1,128)S(1)}, u32[]{:S(2)}, u32[]{:S(2)}) collective-permute-start(f32[128,1,4096]{2,1,0:T(1,128)} %cut_near.1), channel_id=1, source_target_pairs={{0,2},{4,6},{8,10},{12,14},{2,0},{6,4},{10,8},{14,12},{1,3},{5,7},... | collective-permute-start | bytes 6291464 | tf_op jit(solution)/shard_map/ppermute | solution.py:401
  12.0 11.6 %row_weights.1 = (bf16[16,256,512]{2,1,0:T(8,128)(2,1)}, bf16[16,256,512]{2,1,0:T(8,128)(2,1)}) custom-call(f32[32,3,128,128]{3,2,1,0:T(8,128)} %band_ref.1), custom_call_target="tpu_custom_call" | custom-call | tf_op jit(solution)/shard_map/row_weights/pallas_call | solution.py:105
  24.6 10.9 %ratio_inner.1.refs_4_.refs_2_ = f32[256,4096]{1,0:T(8,128)} custom-call(s32[1]{0:T(128)} %bitcast.side_ref.refs_0_, f32[512,1,4096]{2,1,0:T(1,128)} %refs_7_.1, f32[2,3,128,128]{3,2,1,0:T(8,128)S(1)} %constant_dynamic-slice_fusion.3.refs_2_, bf16[16,256,512]{2,1,0:T(8,128)(2,1)} %get-tuple-element.30.refs_3_.refs_4_.refs_6_.refs_5_, ...), custom_call_target="tpu_custom_call" | custom-call | flops 100663296 | bytes 458752 | tf_op jit(solution)/shard_map/ratio_inner/pallas_call | solution.py:236
  36.6 8.2 %ratio_cross.1.refs_1_ = f32[128,4096]{1,0:T(8,128)} custom-call(s32[1]{0:T(128)} %bitcast.side_ref.refs_0_, f32[512,1,4096]{2,1,0:T(1,128)} %refs_7_.1, f32[128,1,4096]{2,1,0:T(1,128)} %collective-permute-done.refs_2_, f32[1,3,128,128]{3,2,1,0:T(8,128)S(1)} %get-tuple-element.61.refs_3_, ...), custom_call_target="tpu_custom_call" | custom-call | flops 44040192 | bytes 327680 | tf_op jit(solution)/shard_map/ratio_cross/pallas_call | solution.py:236
  44.8 54.2 %collective-permute-done.1.refs_2_ = f32[128,1,4096]{2,1,0:T(1,128)S(1)} collective-permute-done((f32[128,1,4096]{2,1,0:T(1,128)}, f32[128,1,4096]{2,1,0:T(1,128)S(1)}, u32[]{:S(2)}, u32[]{:S(2)}) %collective-permute-start.1) | collective-permute-done | bytes 2097184 | tf_op jit(solution)/shard_map/ppermute | solution.py:401
  99.0 2.0 collective-permute-start.3
  101.0 8.0 %ratio_near.1.refs_2_.refs_1_ = f32[128,4096]{1,0:T(8,128)} custom-call(s32[1]{0:T(128)} %bitcast.side_ref.refs_0_, f32[512,1,4096]{2,1,0:T(1,128)} %refs_7_.1, f32[128,1,4096]{2,1,0:T(1,128)S(1)} %collective-permute-done.1.refs_2_, f32[1,3,128,128]{3,2,1,0:T(8,128)S(1)} %get-tuple-element.60.refs_3_.refs_4_, ...), custom_call_target="tpu_custom_call" | custom-call | flops 44040192 | bytes 327680 | tf_op jit(solution)/shard_map/ratio_near/pallas_call | solution.py:236
  109.0 4.1 %collective-permute-start.2 = (f32[128,4096]{1,0:T(8,128)}, f32[128,4096]{1,0:T(8,128)S(1)}, u32[]{:S(2)}, u32[]{:S(2)}) collective-permute-start(f32[128,4096]{1,0:T(8,128)} %ratio_near.1.refs_2_.refs_1_), channel_id=1, source_target_pairs={{0,2},{4,6},{8,10},{12,14},{2,0},{6,4},{10,8},{14,12},{1,3},{5,7},... | collective-permute-start | bytes 6291464 | tf_op jit(solution)/shard_map/ppermute | solution.py:430
  116.0 16.0 %logs_most.1 = (f32[384,1024]{1,0:T(8,128)}, f32[384,1024]{1,0:T(8,128)}, f32[384,1024]{1,0:T(8,128)}, f32[384,1024]{1,0:T(8,128)}, f32[384,4096]{1,0:T(8,128)}) custom-call(s32[1]{0:T(128)} %bitcast.side_ref.refs_0_, f32[128,4096]{1,0:T(8,128)} %ratio_cross.1.refs_1_, f32[128,4096]{1,0:T(8,128)} %ratio_near.1.refs_2_.refs_1_, ...), custom_call_target="tpu_custom_call" | custom-call | flops 169869312 | bytes 589824 | tf_op jit(solution)/shard_map/logs_most/pallas_call | solution.py:236
  133.1 2.6 %collective-permute-done.4.refs_4_ = f32[384,1024]{1,0:T(8,128)S(1)} collective-permute-done((f32[384,1024]{1,0:T(8,128)}, f32[384,1024]{1,0:T(8,128)S(1)}, u32[]{:S(2)}, u32[]{:S(2)}) %collective-permute-start.4) | collective-permute-done | bytes 1572896 | tf_op jit(solution)/shard_map/ppermute | solution.py:436
  135.7 2.2 collective-permute-done.5.refs_5_
  137.9 2.2 collective-permute-done.6.refs_6_
  140.2 2.2 collective-permute-done.7.refs_7_
  142.4 12.2 %raw_most.1 = (f32[512,4096]{1,0:T(8,128)S(1)}, f32[512,1,4096]{2,1,0:T(1,128)S(1)}, f32[1]{0:T(128)}) custom-call(s32[1]{0:T(128)} %bitcast.side_ref.refs_0_, f32[384,1024]{1,0:T(8,128)} %get-tuple-element.36.refs_0_, f32[384,1024]{1,0:T(8,128)} %get-tuple-element.37.refs_1_, f32[384,1024]{1,0:T(8,128)} %get-tuple-element.38.refs_2_, ...), custom_call_target="tpu_custom_call" | custom-call | flops 98304 | bytes 393216 | tf_op jit(solution)/shard_map/raw_most/pallas_call | solution.py:301
  154.6 39.9 %collective-permute-done.2.refs_3_ = f32[128,4096]{1,0:T(8,128)S(1)} collective-permute-done((f32[128,4096]{1,0:T(8,128)}, f32[128,4096]{1,0:T(8,128)S(1)}, u32[]{:S(2)}, u32[]{:S(2)}) %collective-permute-start.2) | collective-permute-done | bytes 2097184 | tf_op jit(solution)/shard_map/ppermute | solution.py:430
  194.5 8.3 %logs_near.1 = (f32[128,1024]{1,0:T(8,128)S(1)}, f32[128,1024]{1,0:T(8,128)S(1)}, f32[128,1024]{1,0:T(8,128)S(1)}, f32[128,1024]{1,0:T(8,128)S(1)}, f32[128,4096]{1,0:T(8,128)}) custom-call(s32[1]{0:T(128)} %bitcast.side_ref.refs_0_, f32[128,4096]{1,0:T(8,128)} %ratio_near.1.refs_2_.refs_1_, f32[256,4096]{1,0:T(8,128)} %ratio_inner.1.refs_4_.refs_2_, ...), custom_call_target="tpu_custom_call" | custom-call | flops 44040192 | bytes 327680 | tf_op jit(solution)/shard_map/logs_near/pallas_call | solution.py:236
  207.1 5.0 %raw_near.1 = (f32[512,4096]{1,0:T(8,128)S(1)}, f32[512,1,4096]{2,1,0:T(1,128)S(1)}, f32[1]{0:T(128)}) custom-call(s32[1]{0:T(128)} %bitcast.side_ref.refs_0_, f32[128,1024]{1,0:T(8,128)S(1)} %get-tuple-element.45.refs_0_, f32[128,1024]{1,0:T(8,128)S(1)} %get-tuple-element.46.refs_1_, ...), custom_call_target="tpu_custom_call", output_to_operand_aliasing={{0}: (10, {}), {1}: (11, {})} | custom-call | flops 32768 | bytes 131072 | tf_op jit(solution)/shard_map/raw_near/pallas_call | solution.py:301
  212.0 2.5 %collective-permute-start.12 = (f32[1]{0:T(128)}, f32[1]{0:T(128)}, u32[]{:S(2)}, u32[]{:S(2)}) collective-permute-start(f32[1]{0:T(128)} %get-tuple-element.55.a_ref), channel_id=1, source_target_pairs={{0,2},{2,0},{4,6},{6,4},{8,10},{10,8},{12,14},{14,12},{1,3},{3,1},... | collective-permute-start | bytes 20 | tf_op jit(solution)/shard_map/ppermute | solution.py:347
  218.0 2.1 collective-permute-start.13
  223.7 3.1 %collective-permute-start.14 = (f32[1]{0:T(128)}, f32[1]{0:T(128)}, u32[]{:S(2)}, u32[]{:S(2)}) collective-permute-start(f32[1]{0:T(128)} %mass.3.refs_0_), channel_id=1, source_target_pairs={{0,8},{2,10},{4,12},{6,14},{8,0},{10,2},{12,4},{14,6},{1,9},{3,11}... | collective-permute-start | bytes 20 | tf_op jit(solution)/shard_map/ppermute | solution.py:347
  228.6 7.6 %outputs.1 = (f32[512,4096]{1,0:T(8,128)}, f32[512,32,128]{2,1,0:T(8,128)}) custom-call(f32[512,4096]{1,0:T(8,128)S(1)} %get-tuple-element.53.raw_ref, f32[512,32,128]{2,1,0:T(8,128)S(1)} %bitcast.3, f32[1]{0:T(128)} %mass.3.refs_0_, f32[1]{0:T(128)} %collective-permute-done.14.refs_1_), custom_call_target="tpu_custom_call" | custom-call | tf_op jit(solution)/shard_map/outputs/pallas_call | solution.py:366
  (27 shorter events, 19.2 us)
Async XLA Ops:
  3.1 33.5 %collective-permute-start = (f32[128,1,4096]{2,1,0:T(1,128)}, f32[128,1,4096]{2,1,0:T(1,128)}, u32[]{:S(2)}, u32[]{:S(2)}) collective-permute-start(f32[128,1,4096]{2,1,0:T(1,128)} %cut_cross.1), channel_id=1, source_target_pairs={{2,4},{6,8},{10,12},{4,2},{8,6},{12,10},{3,5},{7,9},{11,13},{5,3},... | collective-permute-start | bytes 6291464 | tf_op jit(solution)/shard_map/ppermute | solution.py:400
  7.6 91.4 %collective-permute-start.1 = (f32[128,1,4096]{2,1,0:T(1,128)}, f32[128,1,4096]{2,1,0:T(1,128)S(1)}, u32[]{:S(2)}, u32[]{:S(2)}) collective-permute-start(f32[128,1,4096]{2,1,0:T(1,128)} %cut_near.1), channel_id=1, source_target_pairs={{0,2},{4,6},{8,10},{12,14},{2,0},{6,4},{10,8},{14,12},{1,3},{5,7},... | collective-permute-start | bytes 6291464 | tf_op jit(solution)/shard_map/ppermute | solution.py:401
  99.0 17.0 %collective-permute-start.3 = (f32[128,4096]{1,0:T(8,128)}, f32[128,4096]{1,0:T(8,128)}, u32[]{:S(2)}, u32[]{:S(2)}) collective-permute-start(f32[128,4096]{1,0:T(8,128)} %ratio_cross.1.refs_1_), channel_id=1, source_target_pairs={{2,4},{6,8},{10,12},{4,2},{8,6},{12,10},{3,5},{7,9},{11,13},{5,3},... | collective-permute-start | bytes 6291464 | tf_op jit(solution)/shard_map/ppermute | solution.py:426
  101.0 12.1 %copy-start = (f32[2]{0:T(128)S(1)}, f32[2]{0:T(128)}, u32[]{:S(2)}) copy-start(f32[2]{0:T(128)} %param.6) | copy-start | bytes 28
  109.0 85.5 %collective-permute-start.2 = (f32[128,4096]{1,0:T(8,128)}, f32[128,4096]{1,0:T(8,128)S(1)}, u32[]{:S(2)}, u32[]{:S(2)}) collective-permute-start(f32[128,4096]{1,0:T(8,128)} %ratio_near.1.refs_2_.refs_1_), channel_id=1, source_target_pairs={{0,2},{4,6},{8,10},{12,14},{2,0},{6,4},{10,8},{14,12},{1,3},{5,7},... | collective-permute-start | bytes 6291464 | tf_op jit(solution)/shard_map/ppermute | solution.py:430
  132.0 3.7 %collective-permute-start.4 = (f32[384,1024]{1,0:T(8,128)}, f32[384,1024]{1,0:T(8,128)S(1)}, u32[]{:S(2)}, u32[]{:S(2)}) collective-permute-start(f32[384,1024]{1,0:T(8,128)} %get-tuple-element.36.refs_0_), channel_id=1, source_target_pairs={{0,1},{1,0},{2,3},{3,2},{4,5},{5,4},{6,7},{7,6},{8,9},{9,8},{10,11... | collective-permute-start | bytes 4718600 | tf_op jit(solution)/shard_map/ppermute | solution.py:436
  132.0 5.9 %collective-permute-start.5 = (f32[384,1024]{1,0:T(8,128)}, f32[384,1024]{1,0:T(8,128)S(1)}, u32[]{:S(2)}, u32[]{:S(2)}) collective-permute-start(f32[384,1024]{1,0:T(8,128)} %get-tuple-element.37.refs_1_), channel_id=1, source_target_pairs={{0,1},{1,0},{2,3},{3,2},{4,5},{5,4},{6,7},{7,6},{8,9},{9,8},{10,11... | collective-permute-start | bytes 4718600 | tf_op jit(solution)/shard_map/ppermute | solution.py:436
  132.5 7.6 %collective-permute-start.6 = (f32[384,1024]{1,0:T(8,128)}, f32[384,1024]{1,0:T(8,128)S(1)}, u32[]{:S(2)}, u32[]{:S(2)}) collective-permute-start(f32[384,1024]{1,0:T(8,128)} %get-tuple-element.38.refs_2_), channel_id=1, source_target_pairs={{0,1},{1,0},{2,3},{3,2},{4,5},{5,4},{6,7},{7,6},{8,9},{9,8},{10,11... | collective-permute-start | bytes 4718600 | tf_op jit(solution)/shard_map/ppermute | solution.py:436
  132.6 9.8 %collective-permute-start.7 = (f32[384,1024]{1,0:T(8,128)}, f32[384,1024]{1,0:T(8,128)S(1)}, u32[]{:S(2)}, u32[]{:S(2)}) collective-permute-start(f32[384,1024]{1,0:T(8,128)} %get-tuple-element.39.refs_3_), channel_id=1, source_target_pairs={{0,1},{1,0},{2,3},{3,2},{4,5},{5,4},{6,7},{7,6},{8,9},{9,8},{10,11... | collective-permute-start | bytes 4718600 | tf_op jit(solution)/shard_map/ppermute | solution.py:436
  202.8 2.0 collective-permute-start.10
  202.9 2.6 %collective-permute-start.11 = (f32[128,1024]{1,0:T(8,128)S(1)}, f32[128,1024]{1,0:T(8,128)S(1)}, u32[]{:S(2)}, u32[]{:S(2)}) collective-permute-start(f32[128,1024]{1,0:T(8,128)S(1)} %get-tuple-element.48.refs_3_), channel_id=1, source_target_pairs={{0,1},{1,0},{2,3},{3,2},{4,5},{5,4},{6,7},{7,6},{8,9},{9,8},{10,11... | collective-permute-start | bytes 1572872 | tf_op jit(solution)/shard_map/ppermute | solution.py:436
  203.4 2.9 %collective-permute-start.8 = (f32[128,1024]{1,0:T(8,128)S(1)}, f32[128,1024]{1,0:T(8,128)S(1)}, u32[]{:S(2)}, u32[]{:S(2)}) collective-permute-start(f32[128,1024]{1,0:T(8,128)S(1)} %get-tuple-element.45.refs_0_), channel_id=1, source_target_pairs={{0,1},{1,0},{2,3},{3,2},{4,5},{5,4},{6,7},{7,6},{8,9},{9,8},{10,11... | collective-permute-start | bytes 1572872 | tf_op jit(solution)/shard_map/ppermute | solution.py:436
  203.5 3.6 %collective-permute-start.9 = (f32[128,1024]{1,0:T(8,128)S(1)}, f32[128,1024]{1,0:T(8,128)S(1)}, u32[]{:S(2)}, u32[]{:S(2)}) collective-permute-start(f32[128,1024]{1,0:T(8,128)S(1)} %get-tuple-element.46.refs_1_), channel_id=1, source_target_pairs={{0,1},{1,0},{2,3},{3,2},{4,5},{5,4},{6,7},{7,6},{8,9},{9,8},{10,11... | collective-permute-start | bytes 1572872 | tf_op jit(solution)/shard_map/ppermute | solution.py:436
  212.0 4.2 %collective-permute-start.12 = (f32[1]{0:T(128)}, f32[1]{0:T(128)}, u32[]{:S(2)}, u32[]{:S(2)}) collective-permute-start(f32[1]{0:T(128)} %get-tuple-element.55.a_ref), channel_id=1, source_target_pairs={{0,2},{2,0},{4,6},{6,4},{8,10},{10,8},{12,14},{14,12},{1,3},{3,1},... | collective-permute-start | bytes 20 | tf_op jit(solution)/shard_map/ppermute | solution.py:347
  218.0 3.9 %collective-permute-start.13 = (f32[1]{0:T(128)}, f32[1]{0:T(128)}, u32[]{:S(2)}, u32[]{:S(2)}) collective-permute-start(f32[1]{0:T(128)} %mass.2.a_ref), channel_id=1, source_target_pairs={{0,4},{2,6},{4,0},{6,2},{8,12},{10,14},{12,8},{14,10},{1,5},{3,7},... | collective-permute-start | bytes 20 | tf_op jit(solution)/shard_map/ppermute | solution.py:347
  223.7 4.9 %collective-permute-start.14 = (f32[1]{0:T(128)}, f32[1]{0:T(128)}, u32[]{:S(2)}, u32[]{:S(2)}) collective-permute-start(f32[1]{0:T(128)} %mass.3.refs_0_), channel_id=1, source_target_pairs={{0,8},{2,10},{4,12},{6,14},{8,0},{10,2},{12,4},{14,6},{1,9},{3,11}... | collective-permute-start | bytes 20 | tf_op jit(solution)/shard_map/ppermute | solution.py:347

commit v7 on v6

--- a/solution.py
+++ b/solution.py
@@ -10,6 +10,7 @@
 F32 = jnp.float32
 BF16 = jnp.bfloat16
 GROUPS = 4
+SPREAD_BOTH = False
 ANY = pl.BlockSpec(memory_space=pl.ANY)
 INVMEM = pl.BlockSpec(memory_space=pltpu.VMEM)
 INSMEM = pl.BlockSpec(memory_space=pltpu.SMEM)
@@ -45,35 +46,83 @@
     return choice
 
 
-def cut_kernel(first, side_ref, src, dst, stage, sems):
+def cut_kernel(first, columns, side_ref, src, *refs):
+    *outs, stage, sems = refs
     rows = stage.shape[0] // GROUPS
     start = pick(first, side_ref[0])
-    parts = [pl.ds(g * rows, rows) for g in range(GROUPS)]
+    outward = []
     inward = [
-        pltpu.make_async_copy(src.at[pl.ds(start + g * rows, rows)], stage.at[part], sems.at[0, g])
-        for g, part in enumerate(parts)
+        pltpu.make_async_copy(src.at[pl.ds(start + g * rows, rows)], stage.at[pl.ds(g * rows, rows)], sems.at[0, g])
+        for g in range(GROUPS)
     ]
-    outward = [pltpu.make_async_copy(stage.at[part], dst.at[part], sems.at[1, g]) for g, part in enumerate(parts)]
     for copy in inward:
         copy.start()
     for g in range(GROUPS):
         inward[g].wait()
-        outward[g].start()
+        part = pl.ds(g * rows, rows)
+        for k, (out, column) in enumerate(zip(outs, columns)):
+            at = pl.ds(column_of(column, side_ref), out.shape[2])
+            outward.append(pltpu.make_async_copy(stage.at[part, :, at], out.at[part], sems.at[1 + k, g]))
+            outward[-1].start()
     for copy in outward:
         copy.wait()
 
 
-def cut(name, side, array, first, rows):
-    shape = (rows,) + array.shape[1:]
+def cut(name, side, array, first, rows, parts):
+    columns = array.shape[2]
     return pl.pallas_call(
-        functools.partial(cut_kernel, first),
+        functools.partial(cut_kernel, first, [column for column, _ in parts]),
         in_specs=[INSMEM, ANY],
-        out_specs=ANY,
-        out_shape=pltpu.HBM(shape, F32),
-        scratch_shapes=[pltpu.VMEM(shape, F32), pltpu.SemaphoreType.DMA((2, GROUPS))],
+        out_specs=[ANY] * len(parts),
+        out_shape=[pltpu.HBM((rows, 1, n), F32) for _, n in parts],
+        scratch_shapes=[
+            pltpu.VMEM((rows, 1, columns), F32),
+            pltpu.SemaphoreType.DMA((1 + len(parts), GROUPS)),
+        ],
         compiler_params=params(8),
         name=name,
     )(side, *hbm(array))
+
+
+def column_of(column, side_ref):
+    if isinstance(column, tuple):
+        return pl.multiple_of(jnp.where(side_ref[1] == 1, column[0], column[1]), 128)
+    return column
+
+
+def cross_parts(columns):
+    half, quarter = columns // 2, columns // 4
+    return [(0, half), (half, quarter), ((half, 0), half), (3 * quarter, quarter)]
+
+
+def cross_send(parts, behind=()):
+    def send(part, numbers, ends):
+        pairs = []
+        for k in range(3):
+            for direction, number in ((0, k), (1, 2 - k)):
+                if number in numbers:
+                    pairs.append(ends(k)[direction])
+        return lax.ppermute(part, "space", pairs)
+
+    to_partner = lambda k: ((2 * k + 1, 2 * k), (2 * k + 2, 2 * k + 3))
+    onward = lambda k: ((2 * k, 2 * k + 2), (2 * k + 3, 2 * k + 1))
+    direct = lambda k: ((2 * k + 1, 2 * k + 2), (2 * k + 2, 2 * k + 1))
+    relayed = [send(part, numbers, to_partner) for part, numbers in zip(parts[:2], ((0, 1), (0, 2)))]
+    straight = [send(part, numbers, direct) for part, numbers in zip(parts[2:], ((1, 2), (0, 2)))]
+    a, b, c, d, *behind = lax.optimization_barrier((*relayed, *straight, *behind))
+    relayed, straight = [a, b], [c, d]
+    passed = [send(part, numbers, onward) for part, numbers in zip(relayed, ((0, 1), (0, 2)))]
+    return passed + straight, behind
+
+
+def cross_received(base, columns):
+    a, b, c, d = range(base, base + 4)
+    q = columns // 4
+    return ((2, (c, 0), (a, 0)), (2, (c, q), (a, q)), (1, (c, 0), (b, 0)), (1, (c, q), (d, 0)))
+
+
+def cross_own(base, columns):
+    return ((base, 0), (base, columns // 4), (base + 1, 0), (base + 3, 0))
 
 
 def area(ref, row, rows, columns):
@@ -113,14 +162,14 @@
 
 
 def blur_kernel(plan, *refs):
-    pieces, narrays, extra, final = plan
+    pieces, narrays, extra, final, split_out = plan
     side_ref, refs = refs[0], refs[1:]
     arrays = refs[:narrays]
     band_ref, high_ref, low_ref, extra_ref = refs[narrays : narrays + 4]
     rest = refs[narrays + 4 :]
     if final:
         share_ref, rest = rest[0], rest[1:]
-    nouts = GROUPS + 1 if final else 1
+    nouts = GROUPS + 1 if final else 4 if split_out else 1
     outs = rest[:nouts]
     field, a_both, y_both, whigh, wlow, other = rest[nouts : nouts + 6]
     *results, in_sems, late_sems, out_sems = rest[nouts + 6 :]
@@ -131,18 +180,32 @@
     step = columns // GROUPS
     pairs = step // (2 * width)
     inside, late = [], []
+
+    def copy_in(g, k, place):
+        _, row, rows, to = pieces[k]
+        which, column = place
+        return pltpu.make_async_copy(
+            area(arrays[which], pick(row, side), rows, pl.ds(column, step)),
+            field.at[pl.ds(pick(to, side), rows), pl.ds(g * step, step)],
+            in_sems.at[g, k],
+        )
+
+    def start_in(g, k):
+        source = pieces[k][0]
+        if isinstance(source, int):
+            copy = copy_in(g, k, (source, g * step))
+        elif len(source[g]) == 2:
+            copy = copy_in(g, k, source[g])
+        else:
+            number, this, other_one = source[g]
+            pl.when(side_ref[2] == number)(copy_in(g, k, this).start)
+            pl.when(side_ref[2] != number)(copy_in(g, k, other_one).start)
+            return copy_in(g, k, other_one)
+        copy.start()
+        return copy
+
     for g in range(GROUPS):
         at = pl.ds(g * step, step)
-        inside.append(
-            [
-                pltpu.make_async_copy(
-                    area(arrays[which], pick(row, side), rows, at),
-                    field.at[pl.ds(pick(to, side), rows), at],
-                    in_sems.at[g, k],
-                )
-                for k, (which, row, rows, to) in enumerate(pieces)
-            ]
-        )
         some = pl.ds(g * pairs, pairs)
         late.append(
             [
@@ -154,8 +217,7 @@
             ]
         )
     for g in range(GROUPS):
-        for copy in inside[g]:
-            copy.start()
+        inside.append([start_in(g, k) for k in range(len(pieces))])
         if g > 0:
             for copy in late[g - 1]:
                 copy.start()
@@ -200,7 +262,11 @@
             else:
                 results[0][:, at] = other[:, at] / value
         at = pl.ds(g * step, step)
-        targets = [outs[-1].at[:, at]] + ([outs[g]] if final else [])
+        if split_out:
+            which, column = cross_own(0, columns)[g]
+            targets = [outs[which].at[:, pl.ds(column, step)]]
+        else:
+            targets = [outs[-1].at[:, at]] + ([outs[g]] if final else [])
         copies = [
             pltpu.make_async_copy(src.at[:, at], dst, out_sems.at[g, k])
             for k, (src, dst) in enumerate(zip(results, targets))
@@ -215,11 +281,16 @@
         if g > 0:
             going += rows_pass(g - 1)
     going += rows_pass(GROUPS - 1)
+    if split_out:
+        column, n = cross_parts(columns)[2]
+        at = pl.ds(column_of(column, side_ref), n)
+        going.append(pltpu.make_async_copy(results[0].at[:, at], outs[2], out_sems.at[GROUPS, 0]))
+        going[-1].start()
     for copy in going:
         copy.wait()
 
 
-def blur(name, side, arrays, pieces, bands, weights, other, extra, share=None, pin=True):
+def blur(name, side, arrays, pieces, bands, weights, other, extra, share=None, pin=True, split_out=False):
     nout, _, width, _ = bands.shape
     npairs = weights[0].shape[0]
     columns = npairs * 2 * width
@@ -228,8 +299,11 @@
     nouts = 2 if final else 1
     kind = pltpu.HBM if pin else jax.ShapeDtypeStruct
     shapes = [kind((rows, columns // GROUPS), F32)] * (GROUPS if final else 0)
-    shapes.append(pltpu.HBM((rows, columns), F32))
-    plan = (tuple(pieces), len(arrays), extra, final)
+    if split_out:
+        shapes = [pltpu.HBM((rows, n), F32) for _, n in cross_parts(columns)]
+    else:
+        shapes.append(pltpu.HBM((rows, columns), F32))
+    plan = (tuple(pieces), len(arrays), extra, final, split_out)
     work = 3 * 2 * rows * columns * (depth + 4 * width)
     moved = 4 * (depth + 3 * rows) * columns + npairs * 2 * 2 * 8 * width * width
     size = 4 * columns * (depth + (1 + nouts) * rows) + 4 * rows * columns + npairs * 2 * 2 * 8 * width * width
@@ -250,13 +324,13 @@
         + [
             pltpu.SemaphoreType.DMA((GROUPS, len(pieces))),
             pltpu.SemaphoreType.DMA((GROUPS, 3)),
-            pltpu.SemaphoreType.DMA((GROUPS, nouts)),
+            pltpu.SemaphoreType.DMA((GROUPS + 1, nouts)),
         ],
         compiler_params=params(size // 2**20 + 6),
         cost_estimate=pl.CostEstimate(flops=work // 64, bytes_accessed=moved // 64, transcendentals=0),
         name=name,
     )(side, *arrays, bands, *hbm(*weights, other), *([share] if final else []))
-    return (result[:-1], result[-1]) if final else result[0]
+    return (result[:-1], result[-1]) if final else list(result) if split_out else result[0]
 
 
 def raw_kernel(fresh, first, side_ref, *refs):
@@ -384,7 +458,9 @@
     assert maps_here == 1 and lax.axis_size("member") == 2 and count % 2 == 0
 
     odd = place & 1
-    side = odd.reshape(1)
+    middle = place >> 1
+    side = jnp.stack([odd, jnp.where(odd == 1, middle, 3 - middle), jnp.where(odd == 1, 2 - middle, middle - 1)])
+    spread = count == 8 and nlocal > 1
     last = rows_here - width
     cross_row, near_row = (0, last), (last, 0)
     both = lambda pairs: pairs + [(b, a) for a, b in pairs]
@@ -397,8 +473,14 @@
     def choose(choice):
         return jnp.where(odd == 0, *[c // width for c in choice]).astype(jnp.int32)
 
-    cross1 = cross(cut("cut_cross", side, scaling, cross_row, width))
-    near1 = near(cut("cut_near", side, scaling, near_row, width))
+    whole_rows = [(0, cols_all)]
+    near_edge = cut("cut_near", side, scaling, near_row, width, whole_rows)
+    if spread:
+        edge = cut("cut_cross", side, scaling, cross_row, width, cross_parts(cols_all))
+        cross1, near_edge = cross_send(edge, near_edge)
+    else:
+        cross1 = [cross(cut("cut_cross", side, scaling, cross_row, width, whole_rows)[0])]
+    near1 = near(near_edge[0])
 
     shares = weights / jnp.sum(weights)
     share = lax.dynamic_slice_in_dim(shares, lax.axis_index("member"), 1)
@@ -411,22 +493,29 @@
         ratio_inner = blur(
             "ratio_inner", side, hbm(scaling), [(0, 0, rows_here, 0)], inner_bands, wts, densities, width
         )
-        cross1, ratio_inner = lax.optimization_barrier((cross1, ratio_inner))
+        *cross1, ratio_inner = lax.optimization_barrier((*cross1, ratio_inner))
     if nlocal == 1:
         pieces = [(0, 0, width, width), (1, 0, width, (0, 2 * width)), (2, 0, width, (2 * width, 0))]
         bands = band_at(0, 1)
-        ratio = blur("ratio_only", side, [scaling, cross1, near1], pieces, bands, wts, densities, 0)
+        ratio = blur("ratio_only", side, [scaling, *cross1, near1], pieces, bands, wts, densities, 0)
         cross2, near2 = cross(ratio), near(ratio)
     else:
         two = rows_here - 2 * width
-        pieces = [(0, (0, two), 2 * width, (width, 0)), (1, 0, width, (0, 2 * width))]
+        halo = cross_received(1, cols_all) if spread else 1
+        pieces = [(0, (0, two), 2 * width, (width, 0)), (halo, 0, width, (0, 2 * width))]
         bands = band_at(choose(cross_row), 1)
-        ratio_cross = blur("ratio_cross", side, hbm(scaling) + [cross1], pieces, bands, wts, densities, cross_row)
+        ratio_cross = blur(
+            "ratio_cross", side, hbm(scaling) + cross1, pieces, bands, wts, densities, cross_row,
+            split_out=spread and SPREAD_BOTH,
+        )
         ratio_cross, near1 = lax.optimization_barrier((ratio_cross, near1))
-        cross2 = cross(ratio_cross)
+        if spread and SPREAD_BOTH:
+            cross2, _ = cross_send(ratio_cross)
+        else:
+            cross2, ratio_cross = [cross(ratio_cross)], [ratio_cross]
         pieces = [(0, (two, 0), 2 * width, (0, width)), (1, 0, width, (2 * width, 0))]
-        bands = band_at(choose(near_row), 1)
-        ratio_near = blur("ratio_near", side, hbm(scaling) + [near1], pieces, bands, wts, densities, near_row)
+        near_bands = band_at(choose(near_row), 1)
+        ratio_near = blur("ratio_near", side, hbm(scaling) + [near1], pieces, near_bands, wts, densities, near_row)
         near2 = near(ratio_near)
 
     def finish(name, arrays, pieces, bands, row, share, state, pin=True):
@@ -441,18 +530,22 @@
         state = finish("only", [ratio, cross2, near2], pieces, bands, (0, 0), share, None)
     else:
         most, end = rows_here - width, rows_here
-        pieces = [(0, 0, width, (width, most)), (1, 0, width, (end, 0)), (2, 0, width, (0, end))]
-        arrays = [ratio_cross, ratio_near, cross2]
-        beside, beside_row = ratio_cross, 0
+        n = len(ratio_cross)
+        own = cross_own(1, cols_all) if n == 4 else 1
+        halo = cross_received(1 + n, cols_all) if n == 4 else 1 + n
+        arrays = hbm(ratio_near, *ratio_cross) + cross2
+        pieces = [(own, 0, width, (width, most)), (0, 0, width, (end, 0)), (halo, 0, width, (0, end))]
+        beside, beside_row = ratio_cross[0], 0
         if inner > 0:
-            pieces.append((3, 0, inner * width, (2 * width, width)))
-            arrays.append(ratio_inner)
+            pieces.append((len(arrays), 0, inner * width, (2 * width, width)))
+            arrays += hbm(ratio_inner)
             beside, beside_row = ratio_inner, ((inner - 1) * width, 0)
         row = (0, width)
-        state = finish("most", hbm(*arrays[:2]) + arrays[2:3] + hbm(*arrays[3:]), pieces, band_at(choose(row), nlocal - 1), row, share, None)
+        bands = band_at(choose(row), nlocal - 1)
+        state = finish("most", arrays, pieces, bands, row, share, None)
         share, state = lax.optimization_barrier((share, state))
         pieces = [(0, 0, width, width), (1, beside_row, width, (0, 2 * width)), (2, 0, width, (2 * width, 0))]
-        state = finish("near", hbm(ratio_near, beside) + [near2], pieces, bands, near_row, share, state, False)
+        state = finish("near", hbm(ratio_near, beside) + [near2], pieces, near_bands, near_row, share, state, False)
 
     raw, quotient, mass = state
     barycenter, new_scaling = outputs(raw, quotient.reshape(rows_here, cols_all // width, width), mass_parts(mass))

time: 237 us -> 235 us (level)
  waiting for transfers between devices: 112 us -> 90 us
  starting transfers between devices: 22.4 us -> 35.4 us
  Pallas kernels: 96.1 us -> 102 us
    ppermute x3 -> x8, waiting for transfers between devices: 54.2 us -> 36.8 us  [the longest x6 36.8 us: send(): return lax.ppermute(part, 'space', pairs)]
    ppermute x3 -> x8, starting transfers between devices: 8.48 us -> 19.8 us  [the longest x6 12.3 us: send(): return lax.ppermute(part, 'space', pairs)]
    ppermute x1, waiting for transfers between devices: 39.9 us -> 35.7 us  [local(): near2 = near(ratio_near)]
    pallas_call x5, Pallas kernels: 51.3 us -> 54.5 us  [blur(): pl.pallas_call(functools.partial(blur_kernel, plan), in_specs=[INSMEM] +...]
  transfers between devices with their start and end apart: 15 -> 20, of which waited for: 13 -> 14; matrix products, arithmetic and copies ran while one was open for 2% -> 2% of each run, Pallas kernels for 29% -> 31%
where the time goes in v7:
time: 235 us; the launch traced here: 234 us
  Pallas kernels  102 us (43%)
  waiting for transfers between devices  90 us (38%)
  starting transfers between devices  35.4 us (15%)
  local copies, waits for them, and re-layouts  4.63 us (2%)
    pallas_call x5, Pallas kernels, blur(): pl.pallas_call(functools.partial(blur_kernel, plan), in_specs=[INSMEM] +...  54.5 us
    ppermute x6, waiting for transfers between devices, send(): return lax.ppermute(part, 'space', pairs)  36.8 us
    ppermute x1, waiting for transfers between devices, local(): near2 = near(ratio_near)  35.7 us
    pallas_call x2, Pallas kernels, raw_rows(): pl.pallas_call(functools.partial(raw_kernel, fresh, row), grid_spec=pltpu...  18.1 us
    ppermute x8, waiting for transfers between devices, finish(): swap(part)  12.5 us
    ppermute x6, starting transfers between devices, send(): return lax.ppermute(part, 'space', pairs)  12.3 us
    pallas_call x1, Pallas kernels, row_weights(): pl.pallas_call(functools.partial(weight_kernel, nblocks), grid=(nblocks /...  11.6 us
    ppermute x3, starting transfers between devices, mass_parts(): lax.ppermute(parts[0], 'space', [(i, i ^ 1 << bit) for i in range(count)])  9.45 us
  transfers between devices with their start and end apart: 20, of which 14 were waited for; matrix products, arithmetic and copies ran while one was open for 2% of the time, Pallas kernels for 31%

profile of v7, /device:TPU:0, one launch (start us, length us, event | category | flops | bytes accessed | tf_op | source)
XLA Modules:
  0.0 234.2 jit_solution(13785579423794116429)
XLA Ops:
  0.7 3.4 %cut_cross.1 = (f32[128,1,2048]{2,1,0:T(1,128)}, f32[128,1,1024]{2,1,0:T(1,128)}, f32[128,1,2048]{2,1,0:T(1,128)}, f32[128,1,1024]{2,1,0:T(1,128)}) custom-call(s32[3]{0:T(128)S(1)} %pad_add_fusion.side_ref.refs_0_, f32[512,1,4096]{2,1,0:T(1,128)} %refs_7_.1), custom_call_target="tpu_custom_call" | custom-call | tf_op jit(solution)/shard_map/cut_cross/pallas_call | solution.py:73
  8.2 3.0 %cut_near.1 = f32[128,1,4096]{2,1,0:T(1,128)} custom-call(s32[3]{0:T(128)S(1)} %pad_add_fusion.side_ref.refs_0_, f32[512,1,4096]{2,1,0:T(1,128)} %refs_7_.1), custom_call_target="tpu_custom_call" | custom-call | tf_op jit(solution)/shard_map/cut_near/pallas_call | solution.py:73
  11.1 32.0 %collective-permute-done.1 = f32[128,1,1024]{2,1,0:T(1,128)} collective-permute-done((f32[128,1,1024]{2,1,0:T(1,128)}, f32[128,1,1024]{2,1,0:T(1,128)}, u32[]{:S(2)}, u32[]{:S(2)}) %collective-permute-start.1) | collective-permute-done | bytes 524320 | tf_op jit(solution)/shard_map/ppermute | solution.py:105
  43.9 5.5 %collective-permute-start.6 = (f32[128,1,4096]{2,1,0:T(1,128)}, f32[128,1,4096]{2,1,0:T(1,128)S(1)}, u32[]{:S(2)}, u32[]{:S(2)}) collective-permute-start(f32[128,1,4096]{2,1,0:T(1,128)} %cut_near.1), channel_id=1, source_target_pairs={{0,2},{4,6},{8,10},{12,14},{2,0},{6,4},{10,8},{14,12},{1,3},{5,7},... | collective-permute-start | bytes 6291464 | tf_op jit(solution)/shard_map/ppermute | solution.py:483
  49.4 5.4 %collective-permute-start.4 = (f32[128,1,2048]{2,1,0:T(1,128)}, f32[128,1,2048]{2,1,0:T(1,128)}, u32[]{:S(2)}, u32[]{:S(2)}) collective-permute-start(f32[128,1,2048]{2,1,0:T(1,128)} %collective-permute-done), channel_id=1, source_target_pairs={{0,4},{4,8},{10,6},{14,10},{1,5},{5,9},{11,7},{15,11},{16,20},{20,... | collective-permute-start | bytes 3145736 | tf_op jit(solution)/shard_map/ppermute | solution.py:105
  54.8 2.9 %collective-permute-start.5 = (f32[128,1,1024]{2,1,0:T(1,128)}, f32[128,1,1024]{2,1,0:T(1,128)}, u32[]{:S(2)}, u32[]{:S(2)}) collective-permute-start(f32[128,1,1024]{2,1,0:T(1,128)} %collective-permute-done.1), channel_id=1, source_target_pairs={{0,4},{6,2},{8,12},{14,10},{1,5},{7,3},{9,13},{15,11},{16,20},{22,... | collective-permute-start | bytes 1572872 | tf_op jit(solution)/shard_map/ppermute | solution.py:105
  57.7 11.6 %row_weights.1 = (bf16[16,256,512]{2,1,0:T(8,128)(2,1)}, bf16[16,256,512]{2,1,0:T(8,128)(2,1)}) custom-call(f32[32,3,128,128]{3,2,1,0:T(8,128)} %band_ref.1), custom_call_target="tpu_custom_call" | custom-call | tf_op jit(solution)/shard_map/row_weights/pallas_call | solution.py:154
  70.4 11.4 %ratio_inner.1.refs_4_.refs_2_ = f32[256,4096]{1,0:T(8,128)} custom-call(s32[3]{0:T(128)S(1)} %pad_add_fusion.side_ref.refs_0_, f32[512,1,4096]{2,1,0:T(1,128)} %refs_7_.1, f32[2,3,128,128]{3,2,1,0:T(8,128)S(1)} %constant_dynamic-slice_fusion.3.refs_2_, bf16[16,256,512]{2,1,0:T(8,128)(2,1)} %get-tuple-element.50.refs_3_.refs_7_.refs_4_.refs_6_.refs_5_, ...), custom_call_target="tpu_custom_call" | custom-call | flops 100663296 | bytes 458752 | tf_op jit(solution)/shard_map/ratio_inner/pallas_call | solution.py:310
  82.8 4.8 %collective-permute-done.5.refs_3_ = f32[128,1,1024]{2,1,0:T(1,128)} collective-permute-done((f32[128,1,1024]{2,1,0:T(1,128)}, f32[128,1,1024]{2,1,0:T(1,128)}, u32[]{:S(2)}, u32[]{:S(2)}) %collective-permute-start.5) | collective-permute-done | bytes 524320 | tf_op jit(solution)/shard_map/ppermute | solution.py:105
  87.7 8.7 %ratio_cross.1.refs_2_ = f32[128,4096]{1,0:T(8,128)} custom-call(s32[3]{0:T(128)S(1)} %pad_add_fusion.side_ref.refs_0_, f32[512,1,4096]{2,1,0:T(1,128)} %refs_7_.1, f32[128,1,2048]{2,1,0:T(1,128)} %collective-permute-done.4.refs_2_, f32[128,1,1024]{2,1,0:T(1,128)} %collective-permute-done.5.refs_3_, f32[128,1,2048]{2,1,0:T(1,128)S(1)} %collective-permute-done.2.refs_4_, ...), custom_call_target="tpu_custom_call" | custom-call | flops 44040192 | bytes 327680 | tf_op jit(solution)/shard_map/ratio_cross/pallas_call | solution.py:310
  98.3 8.5 %ratio_near.1.refs_1_ = f32[128,4096]{1,0:T(8,128)} custom-call(s32[3]{0:T(128)S(1)} %pad_add_fusion.side_ref.refs_0_, f32[512,1,4096]{2,1,0:T(1,128)} %refs_7_.1, f32[128,1,4096]{2,1,0:T(1,128)S(1)} %collective-permute-done.6.refs_2_, f32[1,3,128,128]{3,2,1,0:T(8,128)S(1)} %get-tuple-element.84.refs_3_.refs_4_, ...), custom_call_target="tpu_custom_call" | custom-call | flops 44040192 | bytes 327680 | tf_op jit(solution)/shard_map/ratio_near/pallas_call | solution.py:310
  106.9 4.0 %collective-permute-start.7 = (f32[128,4096]{1,0:T(8,128)}, f32[128,4096]{1,0:T(8,128)S(1)}, u32[]{:S(2)}, u32[]{:S(2)}) collective-permute-start(f32[128,4096]{1,0:T(8,128)} %ratio_near.1.refs_1_), channel_id=1, source_target_pairs={{0,2},{4,6},{8,10},{12,14},{2,0},{6,4},{10,8},{14,12},{1,3},{5,7},... | collective-permute-start | bytes 6291464 | tf_op jit(solution)/shard_map/ppermute | solution.py:519
  113.9 16.9 %logs_most.1 = (f32[384,1024]{1,0:T(8,128)}, f32[384,1024]{1,0:T(8,128)}, f32[384,1024]{1,0:T(8,128)}, f32[384,1024]{1,0:T(8,128)}, f32[384,4096]{1,0:T(8,128)}) custom-call(s32[3]{0:T(128)S(1)} %pad_add_fusion.side_ref.refs_0_, f32[128,4096]{1,0:T(8,128)} %ratio_near.1.refs_1_, f32[128,4096]{1,0:T(8,128)} %ratio_cross.1.refs_2_, ...), custom_call_target="tpu_custom_call" | custom-call | flops 169869312 | bytes 589824 | tf_op jit(solution)/shard_map/logs_most/pallas_call | solution.py:310
  131.9 2.6 %collective-permute-done.10.refs_5_ = f32[384,1024]{1,0:T(8,128)S(1)} collective-permute-done((f32[384,1024]{1,0:T(8,128)}, f32[384,1024]{1,0:T(8,128)S(1)}, u32[]{:S(2)}, u32[]{:S(2)}) %collective-permute-start.10) | collective-permute-done | bytes 1572896 | tf_op jit(solution)/shard_map/ppermute | solution.py:525
  134.5 2.2 collective-permute-done.11.refs_6_
  139.0 2.2 collective-permute-done.9.refs_4_
  141.2 12.7 %raw_most.1 = (f32[512,4096]{1,0:T(8,128)S(1)}, f32[512,1,4096]{2,1,0:T(1,128)S(1)}, f32[1]{0:T(128)}) custom-call(s32[3]{0:T(128)S(1)} %pad_add_fusion.side_ref.refs_0_, f32[384,1024]{1,0:T(8,128)} %get-tuple-element.60.refs_0_, f32[384,1024]{1,0:T(8,128)} %get-tuple-element.61.refs_1_, f32[384,1024]{1,0:T(8,128)} %get-tuple-element.62.refs_2_, ...), custom_call_target="tpu_custom_call" | custom-call | flops 98304 | bytes 393216 | tf_op jit(solution)/shard_map/raw_most/pallas_call | solution.py:375
  153.9 35.7 %collective-permute-done.7.refs_3_ = f32[128,4096]{1,0:T(8,128)S(1)} collective-permute-done((f32[128,4096]{1,0:T(8,128)}, f32[128,4096]{1,0:T(8,128)S(1)}, u32[]{:S(2)}, u32[]{:S(2)}) %collective-permute-start.7) | collective-permute-done | bytes 2097184 | tf_op jit(solution)/shard_map/ppermute | solution.py:519
  189.6 9.0 %logs_near.1 = (f32[128,1024]{1,0:T(8,128)S(1)}, f32[128,1024]{1,0:T(8,128)S(1)}, f32[128,1024]{1,0:T(8,128)S(1)}, f32[128,1024]{1,0:T(8,128)S(1)}, f32[128,4096]{1,0:T(8,128)}) custom-call(s32[3]{0:T(128)S(1)} %pad_add_fusion.side_ref.refs_0_, f32[128,4096]{1,0:T(8,128)} %ratio_near.1.refs_1_, f32[256,4096]{1,0:T(8,128)} %ratio_inner.1.refs_4_.refs_2_, ...), custom_call_target="tpu_custom_call" | custom-call | flops 44040192 | bytes 327680 | tf_op jit(solution)/shard_map/logs_near/pallas_call | solution.py:310
  202.8 5.4 %raw_near.1 = (f32[512,4096]{1,0:T(8,128)S(1)}, f32[512,1,4096]{2,1,0:T(1,128)S(1)}, f32[1]{0:T(128)}) custom-call(s32[3]{0:T(128)S(1)} %pad_add_fusion.side_ref.refs_0_, f32[128,1024]{1,0:T(8,128)S(1)} %get-tuple-element.69.refs_0_, f32[128,1024]{1,0:T(8,128)S(1)} %get-tuple-element.70.refs_1_, ...), custom_call_target="tpu_custom_call", output_to_operand_aliasing={{0}: (10, {}), {1}: (11, {})} | custom-call | flops 32768 | bytes 131072 | tf_op jit(solution)/shard_map/raw_near/pallas_call | solution.py:375
  208.3 2.5 %collective-permute-start.17 = (f32[1]{0:T(128)}, f32[1]{0:T(128)}, u32[]{:S(2)}, u32[]{:S(2)}) collective-permute-start(f32[1]{0:T(128)} %get-tuple-element.79.a_ref), channel_id=1, source_target_pairs={{0,2},{2,0},{4,6},{6,4},{8,10},{10,8},{12,14},{14,12},{1,3},{3,1},... | collective-permute-start | bytes 20 | tf_op jit(solution)/shard_map/ppermute | solution.py:421
  214.2 3.3 %collective-permute-start.18 = (f32[1]{0:T(128)}, f32[1]{0:T(128)}, u32[]{:S(2)}, u32[]{:S(2)}) collective-permute-start(f32[1]{0:T(128)} %mass.2.a_ref), channel_id=1, source_target_pairs={{0,4},{2,6},{4,0},{6,2},{8,12},{10,14},{12,8},{14,10},{1,5},{3,7},... | collective-permute-start | bytes 20 | tf_op jit(solution)/shard_map/ppermute | solution.py:421
  221.0 3.7 %collective-permute-start.19 = (f32[1]{0:T(128)}, f32[1]{0:T(128)}, u32[]{:S(2)}, u32[]{:S(2)}) collective-permute-start(f32[1]{0:T(128)} %mass.3.refs_0_), channel_id=1, source_target_pairs={{0,8},{2,10},{4,12},{6,14},{8,0},{10,2},{12,4},{14,6},{1,9},{3,11}... | collective-permute-start | bytes 20 | tf_op jit(solution)/shard_map/ppermute | solution.py:421
  226.4 7.8 %outputs.1 = (f32[512,4096]{1,0:T(8,128)}, f32[512,32,128]{2,1,0:T(8,128)}) custom-call(f32[512,4096]{1,0:T(8,128)S(1)} %get-tuple-element.77.raw_ref, f32[512,32,128]{2,1,0:T(8,128)S(1)} %bitcast.5, f32[1]{0:T(128)} %mass.3.refs_0_, f32[1]{0:T(128)} %collective-permute-done.19.refs_1_), custom_call_target="tpu_custom_call" | custom-call | tf_op jit(solution)/shard_map/outputs/pallas_call | solution.py:440
  (42 shorter events, 28.2 us)
Async XLA Ops:
  4.1 39.8 %collective-permute-start = (f32[128,1,2048]{2,1,0:T(1,128)}, f32[128,1,2048]{2,1,0:T(1,128)}, u32[]{:S(2)}, u32[]{:S(2)}) collective-permute-start(f32[128,1,2048]{2,1,0:T(1,128)} %get-tuple-element.42), channel_id=1, source_target_pairs={{2,0},{6,4},{8,10},{12,14},{3,1},{7,5},{9,11},{13,15},{18,16},{22,... | collective-permute-start | bytes 3145736 | tf_op jit(solution)/shard_map/ppermute | solution.py:105
  5.4 38.5 %collective-permute-start.2 = (f32[128,1,2048]{2,1,0:T(1,128)}, f32[128,1,2048]{2,1,0:T(1,128)S(1)}, u32[]{:S(2)}, u32[]{:S(2)}) collective-permute-start(f32[128,1,2048]{2,1,0:T(1,128)} %get-tuple-element.44), channel_id=1, source_target_pairs={{4,2},{6,8},{8,6},{10,12},{5,3},{7,9},{9,7},{11,13},{20,18},{22,24... | collective-permute-start | bytes 3145736 | tf_op jit(solution)/shard_map/ppermute | solution.py:105
  6.2 36.9 %collective-permute-start.1 = (f32[128,1,1024]{2,1,0:T(1,128)}, f32[128,1,1024]{2,1,0:T(1,128)}, u32[]{:S(2)}, u32[]{:S(2)}) collective-permute-start(f32[128,1,1024]{2,1,0:T(1,128)} %get-tuple-element.43), channel_id=1, source_target_pairs={{2,0},{4,6},{10,8},{12,14},{3,1},{5,7},{11,9},{13,15},{18,16},{20,... | collective-permute-start | bytes 1572872 | tf_op jit(solution)/shard_map/ppermute | solution.py:105
  7.5 35.6 %collective-permute-start.3 = (f32[128,1,1024]{2,1,0:T(1,128)}, f32[128,1,1024]{2,1,0:T(1,128)S(1)}, u32[]{:S(2)}, u32[]{:S(2)}) collective-permute-start(f32[128,1,1024]{2,1,0:T(1,128)} %get-tuple-element.45), channel_id=1, source_target_pairs={{2,4},{4,2},{10,12},{12,10},{3,5},{5,3},{11,13},{13,11},{18,20},{2... | collective-permute-start | bytes 1572872 | tf_op jit(solution)/shard_map/ppermute | solution.py:105
  43.1 0.8 copy-start
  43.9 52.4 %collective-permute-start.6 = (f32[128,1,4096]{2,1,0:T(1,128)}, f32[128,1,4096]{2,1,0:T(1,128)S(1)}, u32[]{:S(2)}, u32[]{:S(2)}) collective-permute-start(f32[128,1,4096]{2,1,0:T(1,128)} %cut_near.1), channel_id=1, source_target_pairs={{0,2},{4,6},{8,10},{12,14},{2,0},{6,4},{10,8},{14,12},{1,3},{5,7},... | collective-permute-start | bytes 6291464 | tf_op jit(solution)/shard_map/ppermute | solution.py:483
  49.4 38.3 %collective-permute-start.4 = (f32[128,1,2048]{2,1,0:T(1,128)}, f32[128,1,2048]{2,1,0:T(1,128)}, u32[]{:S(2)}, u32[]{:S(2)}) collective-permute-start(f32[128,1,2048]{2,1,0:T(1,128)} %collective-permute-done), channel_id=1, source_target_pairs={{0,4},{4,8},{10,6},{14,10},{1,5},{5,9},{11,7},{15,11},{16,20},{20,... | collective-permute-start | bytes 3145736 | tf_op jit(solution)/shard_map/ppermute | solution.py:105
  54.8 32.8 %collective-permute-start.5 = (f32[128,1,1024]{2,1,0:T(1,128)}, f32[128,1,1024]{2,1,0:T(1,128)}, u32[]{:S(2)}, u32[]{:S(2)}) collective-permute-start(f32[128,1,1024]{2,1,0:T(1,128)} %collective-permute-done.1), channel_id=1, source_target_pairs={{0,4},{6,2},{8,12},{14,10},{1,5},{7,3},{9,13},{15,11},{16,20},{22,... | collective-permute-start | bytes 1572872 | tf_op jit(solution)/shard_map/ppermute | solution.py:105
  70.3 17.3 %copy-start.1 = (f32[128,1,1024]{2,1,0:T(1,128)S(1)}, f32[128,1,1024]{2,1,0:T(1,128)}, u32[]{:S(2)}) copy-start(f32[128,1,1024]{2,1,0:T(1,128)} %copy-done) | copy-start | bytes 1572868
  96.4 17.5 %collective-permute-start.8 = (f32[128,4096]{1,0:T(8,128)}, f32[128,4096]{1,0:T(8,128)}, u32[]{:S(2)}, u32[]{:S(2)}) collective-permute-start(f32[128,4096]{1,0:T(8,128)} %ratio_cross.1.refs_2_), channel_id=1, source_target_pairs={{2,4},{6,8},{10,12},{4,2},{8,6},{12,10},{3,5},{7,9},{11,13},{5,3},... | collective-permute-start | bytes 6291464 | tf_op jit(solution)/shard_map/ppermute | solution.py:515
  98.3 12.5 %copy-start.2 = (f32[2]{0:T(128)S(1)}, f32[2]{0:T(128)}, u32[]{:S(2)}) copy-start(f32[2]{0:T(128)} %param.6) | copy-start | bytes 28
  106.9 82.8 %collective-permute-start.7 = (f32[128,4096]{1,0:T(8,128)}, f32[128,4096]{1,0:T(8,128)S(1)}, u32[]{:S(2)}, u32[]{:S(2)}) collective-permute-start(f32[128,4096]{1,0:T(8,128)} %ratio_near.1.refs_1_), channel_id=1, source_target_pairs={{0,2},{4,6},{8,10},{12,14},{2,0},{6,4},{10,8},{14,12},{1,3},{5,7},... | collective-permute-start | bytes 6291464 | tf_op jit(solution)/shard_map/ppermute | solution.py:519
  130.8 3.7 %collective-permute-start.10 = (f32[384,1024]{1,0:T(8,128)}, f32[384,1024]{1,0:T(8,128)S(1)}, u32[]{:S(2)}, u32[]{:S(2)}) collective-permute-start(f32[384,1024]{1,0:T(8,128)} %get-tuple-element.61.refs_1_), channel_id=1, source_target_pairs={{0,1},{1,0},{2,3},{3,2},{4,5},{5,4},{6,7},{7,6},{8,9},{9,8},{10,11... | collective-permute-start | bytes 4718600 | tf_op jit(solution)/shard_map/ppermute | solution.py:525
  130.9 5.9 %collective-permute-start.11 = (f32[384,1024]{1,0:T(8,128)}, f32[384,1024]{1,0:T(8,128)S(1)}, u32[]{:S(2)}, u32[]{:S(2)}) collective-permute-start(f32[384,1024]{1,0:T(8,128)} %get-tuple-element.62.refs_2_), channel_id=1, source_target_pairs={{0,1},{1,0},{2,3},{3,2},{4,5},{5,4},{6,7},{7,6},{8,9},{9,8},{10,11... | collective-permute-start | bytes 4718600 | tf_op jit(solution)/shard_map/ppermute | solution.py:525
  131.3 7.6 %collective-permute-start.12 = (f32[384,1024]{1,0:T(8,128)}, f32[384,1024]{1,0:T(8,128)S(1)}, u32[]{:S(2)}, u32[]{:S(2)}) collective-permute-start(f32[384,1024]{1,0:T(8,128)} %get-tuple-element.63.refs_3_), channel_id=1, source_target_pairs={{0,1},{1,0},{2,3},{3,2},{4,5},{5,4},{6,7},{7,6},{8,9},{9,8},{10,11... | collective-permute-start | bytes 4718600 | tf_op jit(solution)/shard_map/ppermute | solution.py:525
  131.4 9.8 %collective-permute-start.9 = (f32[384,1024]{1,0:T(8,128)}, f32[384,1024]{1,0:T(8,128)S(1)}, u32[]{:S(2)}, u32[]{:S(2)}) collective-permute-start(f32[384,1024]{1,0:T(8,128)} %get-tuple-element.60.refs_0_), channel_id=1, source_target_pairs={{0,1},{1,0},{2,3},{3,2},{4,5},{5,4},{6,7},{7,6},{8,9},{9,8},{10,11... | collective-permute-start | bytes 4718600 | tf_op jit(solution)/shard_map/ppermute | solution.py:525
  198.6 2.0 collective-permute-start.13
  198.7 2.6 %collective-permute-start.14 = (f32[128,1024]{1,0:T(8,128)S(1)}, f32[128,1024]{1,0:T(8,128)S(1)}, u32[]{:S(2)}, u32[]{:S(2)}) collective-permute-start(f32[128,1024]{1,0:T(8,128)S(1)} %get-tuple-element.70.refs_1_), channel_id=1, source_target_pairs={{0,1},{1,0},{2,3},{3,2},{4,5},{5,4},{6,7},{7,6},{8,9},{9,8},{10,11... | collective-permute-start | bytes 1572872 | tf_op jit(solution)/shard_map/ppermute | solution.py:525
  199.2 2.9 %collective-permute-start.15 = (f32[128,1024]{1,0:T(8,128)S(1)}, f32[128,1024]{1,0:T(8,128)S(1)}, u32[]{:S(2)}, u32[]{:S(2)}) collective-permute-start(f32[128,1024]{1,0:T(8,128)S(1)} %get-tuple-element.71.refs_2_), channel_id=1, source_target_pairs={{0,1},{1,0},{2,3},{3,2},{4,5},{5,4},{6,7},{7,6},{8,9},{9,8},{10,11... | collective-permute-start | bytes 1572872 | tf_op jit(solution)/shard_map/ppermute | solution.py:525
  199.3 3.6 %collective-permute-start.16 = (f32[128,1024]{1,0:T(8,128)S(1)}, f32[128,1024]{1,0:T(8,128)S(1)}, u32[]{:S(2)}, u32[]{:S(2)}) collective-permute-start(f32[128,1024]{1,0:T(8,128)S(1)} %get-tuple-element.72.refs_3_), channel_id=1, source_target_pairs={{0,1},{1,0},{2,3},{3,2},{4,5},{5,4},{6,7},{7,6},{8,9},{9,8},{10,11... | collective-permute-start | bytes 1572872 | tf_op jit(solution)/shard_map/ppermute | solution.py:525
  208.3 4.1 %collective-permute-start.17 = (f32[1]{0:T(128)}, f32[1]{0:T(128)}, u32[]{:S(2)}, u32[]{:S(2)}) collective-permute-start(f32[1]{0:T(128)} %get-tuple-element.79.a_ref), channel_id=1, source_target_pairs={{0,2},{2,0},{4,6},{6,4},{8,10},{10,8},{12,14},{14,12},{1,3},{3,1},... | collective-permute-start | bytes 20 | tf_op jit(solution)/shard_map/ppermute | solution.py:421
  214.2 5.0 %collective-permute-start.18 = (f32[1]{0:T(128)}, f32[1]{0:T(128)}, u32[]{:S(2)}, u32[]{:S(2)}) collective-permute-start(f32[1]{0:T(128)} %mass.2.a_ref), channel_id=1, source_target_pairs={{0,4},{2,6},{4,0},{6,2},{8,12},{10,14},{12,8},{14,10},{1,5},{3,7},... | collective-permute-start | bytes 20 | tf_op jit(solution)/shard_map/ppermute | solution.py:421
  221.0 5.4 %collective-permute-start.19 = (f32[1]{0:T(128)}, f32[1]{0:T(128)}, u32[]{:S(2)}, u32[]{:S(2)}) collective-permute-start(f32[1]{0:T(128)} %mass.3.refs_0_), channel_id=1, source_target_pairs={{0,8},{2,10},{4,12},{6,14},{8,0},{10,2},{12,4},{14,6},{1,9},{3,11}... | collective-permute-start | bytes 20 | tf_op jit(solution)/shard_map/ppermute | solution.py:421

commit v8 on v7

--- a/solution.py
+++ b/solution.py
@@ -397,6 +397,84 @@
     )(side, *t, *peers, m, *([] if fresh else vmem(*so_far[:2]) + [so_far[2]]))
 
 
+def raw_only_kernel(side_ref, *refs):
+    own, peer, before_ref, raw_ref, mass_ref = refs[:GROUPS], refs[GROUPS : 2 * GROUPS], *refs[-3:]
+    mass = 0.0
+    for g in range(GROUPS):
+        raw = jnp.exp(own[g][...] + peer[g][...])
+        step = raw.shape[1]
+        raw_ref[:, g * step : (g + 1) * step] = raw
+        mass += jnp.sum(raw)
+    mass_ref[0] = mass + jnp.where(pl.program_id(0) == 0, before_ref[0], mass_ref[0])
+
+
+def raw_only(name, side, row, t, peers, raw_all, mass):
+    rows, columns = t[0].shape[0], raw_all.shape[1]
+    tile = 64
+    starts = [r // tile for r in row]
+    group = pl.BlockSpec((tile, columns // GROUPS), lambda i, at: (i, 0))
+    return pl.pallas_call(
+        raw_only_kernel,
+        grid_spec=pltpu.PrefetchScalarGridSpec(
+            num_scalar_prefetch=1,
+            grid=(rows // tile,),
+            in_specs=[group] * (2 * GROUPS) + [ANY, INSMEM],
+            out_specs=(pl.BlockSpec((tile, columns), lambda i, at: (jnp.where(at[0] == 0, *starts) + i, 0)), INSMEM),
+        ),
+        out_shape=(pltpu.VMEM(raw_all.shape, F32), jax.ShapeDtypeStruct((1,), F32)),
+        input_output_aliases={2 * GROUPS + 1: 0},
+        compiler_params=params(16),
+        cost_estimate=pl.CostEstimate(flops=rows * columns // 16, bytes_accessed=rows * columns // 4, transcendentals=0),
+        name=name,
+    )(side, *t, *peers, *vmem(raw_all), mass)
+
+
+def quotient_kernel(first, side_ref, raw_ref, m_ref, _, quotient_ref, quotient, sems):
+    tile = raw_ref.shape[0]
+    at = pl.program_id(0)
+    row = pl.multiple_of(pick(first, side_ref[0]) + at * tile, tile)
+    quotient[at] = raw_ref[...] / m_ref[...]
+    copies = [
+        pltpu.make_async_copy(quotient.at[k], area(quotient_ref, row + (k - at) * tile, tile, slice(None)), sems.at[k])
+        for k in range(quotient.shape[0])
+    ]
+    for k, copy in enumerate(copies):
+        pl.when(at == k)(copy.start)
+
+    @pl.when(at == len(copies) - 1)
+    def _():
+        for copy in copies:
+            copy.wait()
+
+
+def quotient_rows(name, side, row, raw_all, m, quotient_all):
+    rows, columns = m.shape
+    tile = 64
+    starts = [r // tile for r in row]
+    return pl.pallas_call(
+        functools.partial(quotient_kernel, row),
+        grid_spec=pltpu.PrefetchScalarGridSpec(
+            num_scalar_prefetch=1,
+            grid=(rows // tile,),
+            in_specs=[
+                pl.BlockSpec((tile, columns), lambda i, at: (jnp.where(at[0] == 0, *starts) + i, 0)),
+                pl.BlockSpec((tile, columns), lambda i, at: (i, 0)),
+                ANY,
+            ],
+            out_specs=ANY,
+            scratch_shapes=[
+                pltpu.VMEM((rows // tile, tile, columns), F32),
+                pltpu.SemaphoreType.DMA((rows // tile,)),
+            ],
+        ),
+        out_shape=pltpu.VMEM(quotient_all.shape, F32),
+        input_output_aliases={3: 0},
+        compiler_params=params(16),
+        cost_estimate=pl.CostEstimate(flops=rows * columns // 16, bytes_accessed=rows * columns // 4, transcendentals=0),
+        name=name,
+    )(side, *vmem(raw_all), *hbm(m), *vmem(quotient_all))
+
+
 def sum_kernel(a_ref, b_ref, out_ref):
     out_ref[0] = a_ref[0] + b_ref[0]
 
@@ -405,21 +483,19 @@
     count = lax.axis_size("space")
     if count & (count - 1):
         return [lax.psum(mass, "space")]
-    parts = [mass]
-    for bit in range(count.bit_length() - 1):
-        if len(parts) == 2:
-            parts = [
-                pl.pallas_call(
-                    sum_kernel,
-                    in_specs=[INSMEM, INSMEM],
-                    out_specs=INSMEM,
-                    out_shape=jax.ShapeDtypeStruct((1,), F32),
-                    compiler_params=params(1),
-                    name="mass",
-                )(*parts)
-            ]
-        parts.append(lax.ppermute(parts[0], "space", [(i, i ^ (1 << bit)) for i in range(count)]))
-    return parts
+    across = lambda part, distance: lax.ppermute(part, "space", [(i, i ^ distance) for i in range(count)])
+    far = count
+    while far > 8:
+        far //= 2
+        mass = pl.pallas_call(
+            sum_kernel,
+            in_specs=[INSMEM, INSMEM],
+            out_specs=INSMEM,
+            out_shape=jax.ShapeDtypeStruct((1,), F32),
+            compiler_params=params(1),
+            name="mass",
+        )(mass, across(mass, far))
+    return [mass] + [across(mass, distance) for distance in range(1, far)]
 
 
 def output_kernel(total, raw_ref, quotient_ref, *refs):
@@ -521,6 +597,10 @@
     def finish(name, arrays, pieces, bands, row, share, state, pin=True):
         t, m = blur("logs_" + name, side, arrays, pieces, bands, wts, scaling, row, share, pin)
         keep = hbm if pin else lambda *a: list(a)
+        if state is not None:
+            raw, quotient, mass = state
+            raw, mass = raw_only("raw_" + name, side, row, t, [swap(part) for part in t], raw, mass)
+            return raw, quotient_rows("quotient_" + name, side, row, raw, m, quotient), mass
         return raw_rows(
             "raw_" + name, side, row, keep(*t), [swap(part) for part in t], *hbm(m), rows_here, state
         )

time: 235 us -> 239 us (1.017)
  starting transfers between devices: 35.4 us -> 39.3 us
    pallas_call x2 -> x1, Pallas kernels: 18.1 us -> 12.9 us  [raw_rows(): pl.pallas_call(functools.partial(raw_kernel, fresh, row), grid_spec=pltpu...]
    ppermute x3 -> x7, starting transfers between devices: 9.45 us -> 13.5 us  [mass_parts(): lax.ppermute(part, 'space', [(i, i ^ distance) for i in range(count)])]
    pallas_call x1, Pallas kernels: 7.77 us -> 11.4 us  [outputs(): pl.pallas_call(functools.partial(output_kernel, float(columns * columns))...]
    ppermute x3 -> x7, waiting for transfers between devices: 5.05 us -> 4.54 us  [mass_parts(): lax.ppermute(part, 'space', [(i, i ^ distance) for i in range(count)])]
  transfers between devices with their start and end apart: 20 -> 24, of which waited for: 14 -> 13; matrix products, arithmetic and copies ran while one was open for 2% -> 2% of each run, Pallas kernels for 31% -> 32%
where the time goes in v8:
time: 239 us; the launch traced here: 238 us
  Pallas kernels  103 us (43%)
  waiting for transfers between devices  89.5 us (37%)
  starting transfers between devices  39.3 us (16%)
  local copies, waits for them, and re-layouts  4.54 us (2%)
    pallas_call x5, Pallas kernels, blur(): pl.pallas_call(functools.partial(blur_kernel, plan), in_specs=[INSMEM] +...  54.4 us
    ppermute x6, waiting for transfers between devices, send(): return lax.ppermute(part, 'space', pairs)  36.8 us
    ppermute x1, waiting for transfers between devices, local(): near2 = near(ratio_near)  35.7 us
    ppermute x7, starting transfers between devices, mass_parts(): lax.ppermute(part, 'space', [(i, i ^ distance) for i in range(count)])  13.5 us
    pallas_call x1, Pallas kernels, raw_rows(): pl.pallas_call(functools.partial(raw_kernel, fresh, row), grid_spec=pltpu...  12.9 us
    ppermute x8, waiting for transfers between devices, finish(): swap(part)  12.5 us
    ppermute x6, starting transfers between devices, send(): return lax.ppermute(part, 'space', pairs)  12.3 us
    pallas_call x1, Pallas kernels, row_weights(): pl.pallas_call(functools.partial(weight_kernel, nblocks), grid=(nblocks /...  11.6 us
  transfers between devices with their start and end apart: 24, of which 13 were waited for; matrix products, arithmetic and copies ran while one was open for 2% of the time, Pallas kernels for 32%

profile of v8, /device:TPU:0, one launch (start us, length us, event | category | flops | bytes accessed | tf_op | source)
XLA Modules:
  0.0 238.3 jit_solution(16401726494252430893)
XLA Ops:
  0.7 3.4 %cut_cross.1 = (f32[128,1,2048]{2,1,0:T(1,128)}, f32[128,1,1024]{2,1,0:T(1,128)}, f32[128,1,2048]{2,1,0:T(1,128)}, f32[128,1,1024]{2,1,0:T(1,128)}) custom-call(s32[3]{0:T(128)S(1)} %pad_add_fusion.side_ref.refs_0_, f32[512,1,4096]{2,1,0:T(1,128)} %refs_7_.1), custom_call_target="tpu_custom_call" | custom-call | tf_op jit(solution)/shard_map/cut_cross/pallas_call | solution.py:73
  8.2 3.0 %cut_near.1 = f32[128,1,4096]{2,1,0:T(1,128)} custom-call(s32[3]{0:T(128)S(1)} %pad_add_fusion.side_ref.refs_0_, f32[512,1,4096]{2,1,0:T(1,128)} %refs_7_.1), custom_call_target="tpu_custom_call" | custom-call | tf_op jit(solution)/shard_map/cut_near/pallas_call | solution.py:73
  11.2 32.0 %collective-permute-done.1 = f32[128,1,1024]{2,1,0:T(1,128)} collective-permute-done((f32[128,1,1024]{2,1,0:T(1,128)}, f32[128,1,1024]{2,1,0:T(1,128)}, u32[]{:S(2)}, u32[]{:S(2)}) %collective-permute-start.1) | collective-permute-done | bytes 524320 | tf_op jit(solution)/shard_map/ppermute | solution.py:105
  43.9 5.5 %collective-permute-start.6 = (f32[128,1,4096]{2,1,0:T(1,128)}, f32[128,1,4096]{2,1,0:T(1,128)S(1)}, u32[]{:S(2)}, u32[]{:S(2)}) collective-permute-start(f32[128,1,4096]{2,1,0:T(1,128)} %cut_near.1), channel_id=1, source_target_pairs={{0,2},{4,6},{8,10},{12,14},{2,0},{6,4},{10,8},{14,12},{1,3},{5,7},... | collective-permute-start | bytes 6291464 | tf_op jit(solution)/shard_map/ppermute | solution.py:559
  49.4 5.4 %collective-permute-start.4 = (f32[128,1,2048]{2,1,0:T(1,128)}, f32[128,1,2048]{2,1,0:T(1,128)}, u32[]{:S(2)}, u32[]{:S(2)}) collective-permute-start(f32[128,1,2048]{2,1,0:T(1,128)} %collective-permute-done), channel_id=1, source_target_pairs={{0,4},{4,8},{10,6},{14,10},{1,5},{5,9},{11,7},{15,11},{16,20},{20,... | collective-permute-start | bytes 3145736 | tf_op jit(solution)/shard_map/ppermute | solution.py:105
  54.8 2.8 %collective-permute-start.5 = (f32[128,1,1024]{2,1,0:T(1,128)}, f32[128,1,1024]{2,1,0:T(1,128)}, u32[]{:S(2)}, u32[]{:S(2)}) collective-permute-start(f32[128,1,1024]{2,1,0:T(1,128)} %collective-permute-done.1), channel_id=1, source_target_pairs={{0,4},{6,2},{8,12},{14,10},{1,5},{7,3},{9,13},{15,11},{16,20},{22,... | collective-permute-start | bytes 1572872 | tf_op jit(solution)/shard_map/ppermute | solution.py:105
  57.6 11.6 %row_weights.1 = (bf16[16,256,512]{2,1,0:T(8,128)(2,1)}, bf16[16,256,512]{2,1,0:T(8,128)(2,1)}) custom-call(f32[32,3,128,128]{3,2,1,0:T(8,128)} %band_ref.1), custom_call_target="tpu_custom_call" | custom-call | tf_op jit(solution)/shard_map/row_weights/pallas_call | solution.py:154
  70.3 11.5 %ratio_inner.1.refs_4_.refs_2_ = f32[256,4096]{1,0:T(8,128)} custom-call(s32[3]{0:T(128)S(1)} %pad_add_fusion.side_ref.refs_0_, f32[512,1,4096]{2,1,0:T(1,128)} %refs_7_.1, f32[2,3,128,128]{3,2,1,0:T(8,128)S(1)} %constant_dynamic-slice_fusion.3.refs_2_, bf16[16,256,512]{2,1,0:T(8,128)(2,1)} %get-tuple-element.49.refs_3_.refs_7_.refs_4_.refs_6_.refs_5_, ...), custom_call_target="tpu_custom_call" | custom-call | flops 100663296 | bytes 458752 | tf_op jit(solution)/shard_map/ratio_inner/pallas_call | solution.py:310
  82.8 4.8 %collective-permute-done.5.refs_3_ = f32[128,1,1024]{2,1,0:T(1,128)} collective-permute-done((f32[128,1,1024]{2,1,0:T(1,128)}, f32[128,1,1024]{2,1,0:T(1,128)}, u32[]{:S(2)}, u32[]{:S(2)}) %collective-permute-start.5) | collective-permute-done | bytes 524320 | tf_op jit(solution)/shard_map/ppermute | solution.py:105
  87.7 8.7 %ratio_cross.1.refs_2_ = f32[128,4096]{1,0:T(8,128)} custom-call(s32[3]{0:T(128)S(1)} %pad_add_fusion.side_ref.refs_0_, f32[512,1,4096]{2,1,0:T(1,128)} %refs_7_.1, f32[128,1,2048]{2,1,0:T(1,128)} %collective-permute-done.4.refs_2_, f32[128,1,1024]{2,1,0:T(1,128)} %collective-permute-done.5.refs_3_, f32[128,1,2048]{2,1,0:T(1,128)S(1)} %collective-permute-done.2.refs_4_, ...), custom_call_target="tpu_custom_call" | custom-call | flops 44040192 | bytes 327680 | tf_op jit(solution)/shard_map/ratio_cross/pallas_call | solution.py:310
  98.3 8.5 %ratio_near.1.refs_1_ = f32[128,4096]{1,0:T(8,128)} custom-call(s32[3]{0:T(128)S(1)} %pad_add_fusion.side_ref.refs_0_, f32[512,1,4096]{2,1,0:T(1,128)} %refs_7_.1, f32[128,1,4096]{2,1,0:T(1,128)S(1)} %collective-permute-done.6.refs_2_, f32[1,3,128,128]{3,2,1,0:T(8,128)S(1)} %get-tuple-element.82.refs_3_.refs_4_, ...), custom_call_target="tpu_custom_call" | custom-call | flops 44040192 | bytes 327680 | tf_op jit(solution)/shard_map/ratio_near/pallas_call | solution.py:310
  106.9 4.0 %collective-permute-start.7 = (f32[128,4096]{1,0:T(8,128)}, f32[128,4096]{1,0:T(8,128)S(1)}, u32[]{:S(2)}, u32[]{:S(2)}) collective-permute-start(f32[128,4096]{1,0:T(8,128)} %ratio_near.1.refs_1_), channel_id=1, source_target_pairs={{0,2},{4,6},{8,10},{12,14},{2,0},{6,4},{10,8},{14,12},{1,3},{5,7},... | collective-permute-start | bytes 6291464 | tf_op jit(solution)/shard_map/ppermute | solution.py:595
  113.8 16.8 %logs_most.1 = (f32[384,1024]{1,0:T(8,128)}, f32[384,1024]{1,0:T(8,128)}, f32[384,1024]{1,0:T(8,128)}, f32[384,1024]{1,0:T(8,128)}, f32[384,4096]{1,0:T(8,128)}) custom-call(s32[3]{0:T(128)S(1)} %pad_add_fusion.side_ref.refs_0_, f32[128,4096]{1,0:T(8,128)} %ratio_near.1.refs_1_, f32[128,4096]{1,0:T(8,128)} %ratio_cross.1.refs_2_, ...), custom_call_target="tpu_custom_call" | custom-call | flops 169869312 | bytes 589824 | tf_op jit(solution)/shard_map/logs_most/pallas_call | solution.py:310
  131.7 2.6 %collective-permute-done.10.refs_5_ = f32[384,1024]{1,0:T(8,128)S(1)} collective-permute-done((f32[384,1024]{1,0:T(8,128)}, f32[384,1024]{1,0:T(8,128)S(1)}, u32[]{:S(2)}, u32[]{:S(2)}) %collective-permute-start.10) | collective-permute-done | bytes 1572896 | tf_op jit(solution)/shard_map/ppermute | solution.py:605
  141.1 12.9 %raw_most.1 = (f32[512,4096]{1,0:T(8,128)S(1)}, f32[512,1,4096]{2,1,0:T(1,128)S(1)}, f32[1]{0:T(128)}) custom-call(s32[3]{0:T(128)S(1)} %pad_add_fusion.side_ref.refs_0_, f32[384,1024]{1,0:T(8,128)} %get-tuple-element.59.refs_0_, f32[384,1024]{1,0:T(8,128)} %get-tuple-element.60.refs_1_, f32[384,1024]{1,0:T(8,128)} %get-tuple-element.61.refs_2_, ...), custom_call_target="tpu_custom_call" | custom-call | flops 98304 | bytes 393216 | tf_op jit(solution)/shard_map/raw_most/pallas_call | solution.py:375
  153.9 35.7 %collective-permute-done.7.refs_3_ = f32[128,4096]{1,0:T(8,128)S(1)} collective-permute-done((f32[128,4096]{1,0:T(8,128)}, f32[128,4096]{1,0:T(8,128)S(1)}, u32[]{:S(2)}, u32[]{:S(2)}) %collective-permute-start.7) | collective-permute-done | bytes 2097184 | tf_op jit(solution)/shard_map/ppermute | solution.py:595
  189.6 8.9 %logs_near.1 = (f32[128,1024]{1,0:T(8,128)S(1)}, f32[128,1024]{1,0:T(8,128)S(1)}, f32[128,1024]{1,0:T(8,128)S(1)}, f32[128,1024]{1,0:T(8,128)S(1)}, f32[128,4096]{1,0:T(8,128)}) custom-call(s32[3]{0:T(128)S(1)} %pad_add_fusion.side_ref.refs_0_, f32[128,4096]{1,0:T(8,128)} %ratio_near.1.refs_1_, f32[256,4096]{1,0:T(8,128)} %ratio_inner.1.refs_4_.refs_2_, ...), custom_call_target="tpu_custom_call" | custom-call | flops 44040192 | bytes 327680 | tf_op jit(solution)/shard_map/logs_near/pallas_call | solution.py:310
  202.8 2.4 %raw_near.1 = (f32[512,4096]{1,0:T(8,128)S(1)}, f32[1]{0:T(128)}) custom-call(s32[3]{0:T(128)S(1)} %pad_add_fusion.side_ref.refs_0_, f32[128,1024]{1,0:T(8,128)S(1)} %get-tuple-element.68.refs_0_, f32[128,1024]{1,0:T(8,128)S(1)} %get-tuple-element.69.refs_1_, f32[128,1024]{1,0:T(8,128)S(1)} %get-tuple-element.70.refs_2_, ...), custom_call_target="tpu_custom_call", output_to_operand_aliasing={{0}: (9, {})} | custom-call | flops 32768 | bytes 131072 | tf_op jit(solution)/shard_map/raw_near/pallas_call | solution.py:416
  205.2 2.4 %collective-permute-start.17 = (f32[1]{0:T(128)}, f32[1]{0:T(128)}, u32[]{:S(2)}, u32[]{:S(2)}) collective-permute-start(f32[1]{0:T(128)} %get-tuple-element.77.refs_0_), channel_id=1, source_target_pairs={{0,2},{2,0},{4,6},{6,4},{8,10},{10,8},{12,14},{14,12},{1,3},{3,1},... | collective-permute-start | bytes 20 | tf_op jit(solution)/shard_map/ppermute | solution.py:486
  210.3 3.6 %collective-permute-start.20 = (f32[1]{0:T(128)}, f32[1]{0:T(128)}, u32[]{:S(2)}, u32[]{:S(2)}) collective-permute-start(f32[1]{0:T(128)} %get-tuple-element.77.refs_0_), channel_id=1, source_target_pairs={{0,8},{2,10},{4,12},{6,14},{8,0},{10,2},{12,4},{14,6},{1,9},{3,11}... | collective-permute-start | bytes 20 | tf_op jit(solution)/shard_map/ppermute | solution.py:486
  214.3 3.6 %quotient_near.1 = f32[512,1,4096]{2,1,0:T(1,128)S(1)} custom-call(s32[3]{0:T(128)S(1)} %pad_add_fusion.side_ref.refs_0_, f32[512,4096]{1,0:T(8,128)S(1)} %get-tuple-element.74.raw_ref, f32[128,4096]{1,0:T(8,128)} %get-tuple-element.75.m_ref, f32[512,1,4096]{2,1,0:T(1,128)S(1)} %get-tuple-element.76._), custom_call_target="tpu_custom_call", output_to_operand_aliasing={{}: (3, {})} | custom-call | flops 32768 | bytes 131072 | tf_op jit(solution)/shard_map/quotient_near/pallas_call | solution.py:454
  217.9 2.4 %collective-permute-start.22 = (f32[1]{0:T(128)}, f32[1]{0:T(128)}, u32[]{:S(2)}, u32[]{:S(2)}) collective-permute-start(f32[1]{0:T(128)} %get-tuple-element.77.refs_0_), channel_id=1, source_target_pairs={{0,12},{2,14},{4,8},{6,10},{8,4},{10,6},{12,0},{14,2},{1,13},{3,15... | collective-permute-start | bytes 20 | tf_op jit(solution)/shard_map/ppermute | solution.py:486
  223.6 3.3 %collective-permute-done.23.refs_7_ = f32[1]{0:T(128)} collective-permute-done((f32[1]{0:T(128)}, f32[1]{0:T(128)}, u32[]{:S(2)}, u32[]{:S(2)}) %collective-permute-start.23) | collective-permute-done | bytes 36 | tf_op jit(solution)/shard_map/ppermute | solution.py:486
  226.9 11.4 %outputs.1 = (f32[512,4096]{1,0:T(8,128)}, f32[512,32,128]{2,1,0:T(8,128)}) custom-call(f32[512,4096]{1,0:T(8,128)S(1)} %get-tuple-element.74.raw_ref, f32[512,32,128]{2,1,0:T(8,128)S(1)} %bitcast.5, f32[1]{0:T(128)} %get-tuple-element.77.refs_0_, f32[1]{0:T(128)} %collective-permute-done.17.refs_1_, f32[1]{0:T(128)} %collective-permute-done.18.refs_2_, ...), custom_call_target="tpu_custom_call" | custom-call | tf_op jit(solution)/shard_map/outputs/pallas_call | solution.py:516
  (49 shorter events, 30.2 us)
Async XLA Ops:
  4.1 39.8 %collective-permute-start = (f32[128,1,2048]{2,1,0:T(1,128)}, f32[128,1,2048]{2,1,0:T(1,128)}, u32[]{:S(2)}, u32[]{:S(2)}) collective-permute-start(f32[128,1,2048]{2,1,0:T(1,128)} %get-tuple-element.41), channel_id=1, source_target_pairs={{2,0},{6,4},{8,10},{12,14},{3,1},{7,5},{9,11},{13,15},{18,16},{22,... | collective-permute-start | bytes 3145736 | tf_op jit(solution)/shard_map/ppermute | solution.py:105
  5.4 38.5 %collective-permute-start.2 = (f32[128,1,2048]{2,1,0:T(1,128)}, f32[128,1,2048]{2,1,0:T(1,128)S(1)}, u32[]{:S(2)}, u32[]{:S(2)}) collective-permute-start(f32[128,1,2048]{2,1,0:T(1,128)} %get-tuple-element.43), channel_id=1, source_target_pairs={{4,2},{6,8},{8,6},{10,12},{5,3},{7,9},{9,7},{11,13},{20,18},{22,24... | collective-permute-start | bytes 3145736 | tf_op jit(solution)/shard_map/ppermute | solution.py:105
  6.2 36.9 %collective-permute-start.1 = (f32[128,1,1024]{2,1,0:T(1,128)}, f32[128,1,1024]{2,1,0:T(1,128)}, u32[]{:S(2)}, u32[]{:S(2)}) collective-permute-start(f32[128,1,1024]{2,1,0:T(1,128)} %get-tuple-element.42), channel_id=1, source_target_pairs={{2,0},{4,6},{10,8},{12,14},{3,1},{5,7},{11,9},{13,15},{18,16},{20,... | collective-permute-start | bytes 1572872 | tf_op jit(solution)/shard_map/ppermute | solution.py:105
  7.5 35.6 %collective-permute-start.3 = (f32[128,1,1024]{2,1,0:T(1,128)}, f32[128,1,1024]{2,1,0:T(1,128)S(1)}, u32[]{:S(2)}, u32[]{:S(2)}) collective-permute-start(f32[128,1,1024]{2,1,0:T(1,128)} %get-tuple-element.44), channel_id=1, source_target_pairs={{2,4},{4,2},{10,12},{12,10},{3,5},{5,3},{11,13},{13,11},{18,20},{2... | collective-permute-start | bytes 1572872 | tf_op jit(solution)/shard_map/ppermute | solution.py:105
  43.9 52.4 %collective-permute-start.6 = (f32[128,1,4096]{2,1,0:T(1,128)}, f32[128,1,4096]{2,1,0:T(1,128)S(1)}, u32[]{:S(2)}, u32[]{:S(2)}) collective-permute-start(f32[128,1,4096]{2,1,0:T(1,128)} %cut_near.1), channel_id=1, source_target_pairs={{0,2},{4,6},{8,10},{12,14},{2,0},{6,4},{10,8},{14,12},{1,3},{5,7},... | collective-permute-start | bytes 6291464 | tf_op jit(solution)/shard_map/ppermute | solution.py:559
  49.4 38.3 %collective-permute-start.4 = (f32[128,1,2048]{2,1,0:T(1,128)}, f32[128,1,2048]{2,1,0:T(1,128)}, u32[]{:S(2)}, u32[]{:S(2)}) collective-permute-start(f32[128,1,2048]{2,1,0:T(1,128)} %collective-permute-done), channel_id=1, source_target_pairs={{0,4},{4,8},{10,6},{14,10},{1,5},{5,9},{11,7},{15,11},{16,20},{20,... | collective-permute-start | bytes 3145736 | tf_op jit(solution)/shard_map/ppermute | solution.py:105
  54.8 32.9 %collective-permute-start.5 = (f32[128,1,1024]{2,1,0:T(1,128)}, f32[128,1,1024]{2,1,0:T(1,128)}, u32[]{:S(2)}, u32[]{:S(2)}) collective-permute-start(f32[128,1,1024]{2,1,0:T(1,128)} %collective-permute-done.1), channel_id=1, source_target_pairs={{0,4},{6,2},{8,12},{14,10},{1,5},{7,3},{9,13},{15,11},{16,20},{22,... | collective-permute-start | bytes 1572872 | tf_op jit(solution)/shard_map/ppermute | solution.py:105
  96.4 17.4 %collective-permute-start.8 = (f32[128,4096]{1,0:T(8,128)}, f32[128,4096]{1,0:T(8,128)}, u32[]{:S(2)}, u32[]{:S(2)}) collective-permute-start(f32[128,4096]{1,0:T(8,128)} %ratio_cross.1.refs_2_), channel_id=1, source_target_pairs={{2,4},{6,8},{10,12},{4,2},{8,6},{12,10},{3,5},{7,9},{11,13},{5,3},... | collective-permute-start | bytes 6291464 | tf_op jit(solution)/shard_map/ppermute | solution.py:591
  106.9 82.7 %collective-permute-start.7 = (f32[128,4096]{1,0:T(8,128)}, f32[128,4096]{1,0:T(8,128)S(1)}, u32[]{:S(2)}, u32[]{:S(2)}) collective-permute-start(f32[128,4096]{1,0:T(8,128)} %ratio_near.1.refs_1_), channel_id=1, source_target_pairs={{0,2},{4,6},{8,10},{12,14},{2,0},{6,4},{10,8},{14,12},{1,3},{5,7},... | collective-permute-start | bytes 6291464 | tf_op jit(solution)/shard_map/ppermute | solution.py:595
  130.6 3.7 %collective-permute-start.10 = (f32[384,1024]{1,0:T(8,128)}, f32[384,1024]{1,0:T(8,128)S(1)}, u32[]{:S(2)}, u32[]{:S(2)}) collective-permute-start(f32[384,1024]{1,0:T(8,128)} %get-tuple-element.60.refs_1_), channel_id=1, source_target_pairs={{0,1},{1,0},{2,3},{3,2},{4,5},{5,4},{6,7},{7,6},{8,9},{9,8},{10,11... | collective-permute-start | bytes 4718600 | tf_op jit(solution)/shard_map/ppermute | solution.py:605
  130.7 5.9 %collective-permute-start.11 = (f32[384,1024]{1,0:T(8,128)}, f32[384,1024]{1,0:T(8,128)S(1)}, u32[]{:S(2)}, u32[]{:S(2)}) collective-permute-start(f32[384,1024]{1,0:T(8,128)} %get-tuple-element.61.refs_2_), channel_id=1, source_target_pairs={{0,1},{1,0},{2,3},{3,2},{4,5},{5,4},{6,7},{7,6},{8,9},{9,8},{10,11... | collective-permute-start | bytes 4718600 | tf_op jit(solution)/shard_map/ppermute | solution.py:605
  131.2 7.6 %collective-permute-start.12 = (f32[384,1024]{1,0:T(8,128)}, f32[384,1024]{1,0:T(8,128)S(1)}, u32[]{:S(2)}, u32[]{:S(2)}) collective-permute-start(f32[384,1024]{1,0:T(8,128)} %get-tuple-element.62.refs_3_), channel_id=1, source_target_pairs={{0,1},{1,0},{2,3},{3,2},{4,5},{5,4},{6,7},{7,6},{8,9},{9,8},{10,11... | collective-permute-start | bytes 4718600 | tf_op jit(solution)/shard_map/ppermute | solution.py:605
  131.3 9.8 %collective-permute-start.9 = (f32[384,1024]{1,0:T(8,128)}, f32[384,1024]{1,0:T(8,128)S(1)}, u32[]{:S(2)}, u32[]{:S(2)}) collective-permute-start(f32[384,1024]{1,0:T(8,128)} %get-tuple-element.59.refs_0_), channel_id=1, source_target_pairs={{0,1},{1,0},{2,3},{3,2},{4,5},{5,4},{6,7},{7,6},{8,9},{9,8},{10,11... | collective-permute-start | bytes 4718600 | tf_op jit(solution)/shard_map/ppermute | solution.py:605
  198.6 2.0 collective-permute-start.13
  198.6 2.6 %collective-permute-start.14 = (f32[128,1024]{1,0:T(8,128)S(1)}, f32[128,1024]{1,0:T(8,128)S(1)}, u32[]{:S(2)}, u32[]{:S(2)}) collective-permute-start(f32[128,1024]{1,0:T(8,128)S(1)} %get-tuple-element.69.refs_1_), channel_id=1, source_target_pairs={{0,1},{1,0},{2,3},{3,2},{4,5},{5,4},{6,7},{7,6},{8,9},{9,8},{10,11... | collective-permute-start | bytes 1572872 | tf_op jit(solution)/shard_map/ppermute | solution.py:602
  199.1 2.9 %collective-permute-start.15 = (f32[128,1024]{1,0:T(8,128)S(1)}, f32[128,1024]{1,0:T(8,128)S(1)}, u32[]{:S(2)}, u32[]{:S(2)}) collective-permute-start(f32[128,1024]{1,0:T(8,128)S(1)} %get-tuple-element.70.refs_2_), channel_id=1, source_target_pairs={{0,1},{1,0},{2,3},{3,2},{4,5},{5,4},{6,7},{7,6},{8,9},{9,8},{10,11... | collective-permute-start | bytes 1572872 | tf_op jit(solution)/shard_map/ppermute | solution.py:602
  199.2 3.6 %collective-permute-start.16 = (f32[128,1024]{1,0:T(8,128)S(1)}, f32[128,1024]{1,0:T(8,128)S(1)}, u32[]{:S(2)}, u32[]{:S(2)}) collective-permute-start(f32[128,1024]{1,0:T(8,128)S(1)} %get-tuple-element.71.refs_3_), channel_id=1, source_target_pairs={{0,1},{1,0},{2,3},{3,2},{4,5},{5,4},{6,7},{7,6},{8,9},{9,8},{10,11... | collective-permute-start | bytes 1572872 | tf_op jit(solution)/shard_map/ppermute | solution.py:602
  205.2 12.7 %collective-permute-start.17 = (f32[1]{0:T(128)}, f32[1]{0:T(128)}, u32[]{:S(2)}, u32[]{:S(2)}) collective-permute-start(f32[1]{0:T(128)} %get-tuple-element.77.refs_0_), channel_id=1, source_target_pairs={{0,2},{2,0},{4,6},{6,4},{8,10},{10,8},{12,14},{14,12},{1,3},{3,1},... | collective-permute-start | bytes 20 | tf_op jit(solution)/shard_map/ppermute | solution.py:486
  207.6 12.7 %collective-permute-start.18 = (f32[1]{0:T(128)}, f32[1]{0:T(128)}, u32[]{:S(2)}, u32[]{:S(2)}) collective-permute-start(f32[1]{0:T(128)} %get-tuple-element.77.refs_0_), channel_id=1, source_target_pairs={{0,4},{2,6},{4,0},{6,2},{8,12},{10,14},{12,8},{14,10},{1,5},{3,7},... | collective-permute-start | bytes 20 | tf_op jit(solution)/shard_map/ppermute | solution.py:486
  209.9 12.4 %collective-permute-start.19 = (f32[1]{0:T(128)}, f32[1]{0:T(128)}, u32[]{:S(2)}, u32[]{:S(2)}) collective-permute-start(f32[1]{0:T(128)} %get-tuple-element.77.refs_0_), channel_id=1, source_target_pairs={{0,6},{2,4},{4,2},{6,0},{8,14},{10,12},{12,10},{14,8},{1,7},{3,5},... | collective-permute-start | bytes 20 | tf_op jit(solution)/shard_map/ppermute | solution.py:486
  210.3 12.1 %collective-permute-start.20 = (f32[1]{0:T(128)}, f32[1]{0:T(128)}, u32[]{:S(2)}, u32[]{:S(2)}) collective-permute-start(f32[1]{0:T(128)} %get-tuple-element.77.refs_0_), channel_id=1, source_target_pairs={{0,8},{2,10},{4,12},{6,14},{8,0},{10,2},{12,4},{14,6},{1,9},{3,11}... | collective-permute-start | bytes 20 | tf_op jit(solution)/shard_map/ppermute | solution.py:486
  213.9 8.4 %collective-permute-start.21 = (f32[1]{0:T(128)}, f32[1]{0:T(128)}, u32[]{:S(2)}, u32[]{:S(2)}) collective-permute-start(f32[1]{0:T(128)} %get-tuple-element.77.refs_0_), channel_id=1, source_target_pairs={{0,10},{2,8},{4,14},{6,12},{8,2},{10,0},{12,6},{14,4},{1,11},{3,9}... | collective-permute-start | bytes 20 | tf_op jit(solution)/shard_map/ppermute | solution.py:486
  217.9 5.7 %collective-permute-start.22 = (f32[1]{0:T(128)}, f32[1]{0:T(128)}, u32[]{:S(2)}, u32[]{:S(2)}) collective-permute-start(f32[1]{0:T(128)} %get-tuple-element.77.refs_0_), channel_id=1, source_target_pairs={{0,12},{2,14},{4,8},{6,10},{8,4},{10,6},{12,0},{14,2},{1,13},{3,15... | collective-permute-start | bytes 20 | tf_op jit(solution)/shard_map/ppermute | solution.py:486
  220.3 6.6 %collective-permute-start.23 = (f32[1]{0:T(128)}, f32[1]{0:T(128)}, u32[]{:S(2)}, u32[]{:S(2)}) collective-permute-start(f32[1]{0:T(128)} %get-tuple-element.77.refs_0_), channel_id=1, source_target_pairs={{0,14},{2,12},{4,10},{6,8},{8,6},{10,4},{12,2},{14,0},{1,15},{3,13... | collective-permute-start | bytes 20 | tf_op jit(solution)/shard_map/ppermute | solution.py:486
  (3 other events, 30.7 us)
